TPU v7x, 128 devices: a whole 4x4x4 slice. The times are simulated.
128 devices in a mesh: ctx: 32 (over z, x, y_lo), dp: 4 (over y_hi, core).
Axes of the slice: x: 4, y: 4 (y_hi: 2, y_lo: 2; y = y_hi * 2 + y_lo), z: 4, core: 2. Of those that a mesh axis runs over, the one named last changes fastest.
Arguments:
- q_latent: bfloat16 [8192, 1536], P(('ctx', 'dp')), may hold values from -600 to 600
- kv_latent: bfloat16 [8192, 512], P(('ctx', 'dp')), may hold values from -6 to 6
- key_rope: bfloat16 [8192, 64], P(('ctx', 'dp')), may hold values from -6 to 6
- block_order: int32 [64], replicated, may hold values from 0 to 63, as said below
- w_query: bfloat16 [1536, 6144], P(None, 'dp'), may hold values from -16 to 16
- w_key: bfloat16 [512, 4096], P(None, 'dp'), may hold values from -6 to 6
- w_value: bfloat16 [512, 4096], P(None, 'dp'), may hold values from -6 to 6
- grad_query: bfloat16 [8192, 6144], P('ctx', 'dp'), may hold values from -6 to 6
- grad_key: bfloat16 [8192, 4096], P('ctx', 'dp'), may hold values from -6 to 6
- mom_query: float32 [1536, 6144], P('ctx', 'dp'), may hold values from -7240.7734 to 7240.7734
- mom_key: float32 [512, 4096], P('ctx', 'dp'), may hold values from -7240.7734 to 7240.7734
- clip_flags: int32 [32], P('dp'), may hold values 0 or 1
Outputs:
- attn_out: bfloat16 [8192, 4096], P('ctx', 'dp')
- max_logits: float32 [32], P('dp')
- step_query: float32 [1536, 6144], P('ctx', 'dp')
- step_key: float32 [512, 4096], P('ctx', 'dp')
- new_query: float32 [1536, 6144], P('ctx', 'dp')
- new_key: float32 [512, 4096], P('ctx', 'dp')
Inputs may be any that keep to these rules, and one draw needn't show every extreme that they name: `block_order`: a permutation of 0 to 63 in which entries 2c and 2c + 1 sum to 63.
All inputs are finite; a program needn't handle non-finite values. No bound on the sum of `clip_flags` on one device may be relied on, other than what follows from the above.
Results may differ from a plain program's by a relative error of at most 0.013.
The roundings to bfloat16 on the way count: a program that leaves them out, or rounds other values in their place, can miss the bound.
Values may be sent and summed in bfloat16 or wider, within the bound.
No kernel may reach another device: no remote copies, remote signals or barrier semaphores. Data moves between devices by JAX's collectives and lax.ppermute only.
A program may use at most 128 MiB of HBM per device.

v0:
```python
import math

import jax
import jax.numpy as jnp
from jax import lax
from jax.sharding import PartitionSpec as P

QR = 1536
KVR = 512
NOPE = 128
ROPE = 64
VDIM = 128
NS_STEPS = 3


NS_A = 3.4445
NS_B = -4.775
NS_C = 2.0315
MOMENTUM = 0.95
LEARN_RATE = 0.05
DECAY = 0.1
CLIP_TAU = 6.0
ROPE_THETA = 50000.0
FULL_PRECISION = lax.Precision.HIGHEST


def rotate_rope(rope_part, positions):
    pair_count = ROPE // 2
    frequency = ROPE_THETA ** (-2.0 * jnp.arange(pair_count, dtype=jnp.float32) / ROPE)
    angles = positions.astype(jnp.float32)[:, None] * frequency[None, :]
    cosine = jnp.cos(angles)
    sine_part = jnp.sin(angles)
    first_half = rope_part[..., :pair_count]
    second_half = rope_part[..., pair_count:]
    return jnp.concatenate(
        [
            first_half * cosine - second_half * sine_part,
            second_half * cosine + first_half * sine_part,
        ],
        axis=-1,
    )


def gram_of(matrices):
    return jnp.einsum("hrc,hrd->hcd", matrices, matrices, precision=FULL_PRECISION)


def polish(matrices, gram_matrix):
    polynomial = NS_B * gram_matrix + NS_C * jnp.einsum(
        "hcd,hde->hce", gram_matrix, gram_matrix, precision=FULL_PRECISION
    )
    return NS_A * matrices + jnp.einsum(
        "hrc,hcd->hrd", matrices, polynomial, precision=FULL_PRECISION
    )


def heads_first(matrix, column_count):
    return matrix.reshape(matrix.shape[0], -1, column_count).transpose(1, 0, 2)


def heads_last(stacked):
    return stacked.transpose(1, 0, 2).reshape(stacked.shape[1], -1)


def contract_rows(left_side, right_side):
    return lax.dot_general(
        left_side, right_side, (((0,), (0,)), ((), ())), preferred_element_type=jnp.float32
    )


def shards(
    q_latent,
    kv_latent,
    key_rope,
    block_order,
    w_query,
    w_key,
    w_value,
    grad_query,
    grad_key,
    mom_query,
    mom_key,
    clip_flags,
):
    head_width = NOPE + ROPE
    head_count = w_key.shape[1] // NOPE
    score_scale = head_width ** (-0.5)
    ctx_index = lax.axis_index("ctx")
    q_block, kv_block, rope_block = (
        lax.all_gather(q_latent, "dp", axis=0, tiled=True),
        lax.all_gather(kv_latent, "dp", axis=0, tiled=True),
        lax.all_gather(key_rope, "dp", axis=0, tiled=True),
    )
    token_count = q_block.shape[0]
    half_rows = token_count // 2
    local_rows = jnp.arange(token_count, dtype=jnp.int32)
    query_pos = (
        block_order[2 * ctx_index + local_rows // half_rows] * half_rows + local_rows % half_rows
    )
    queries = jnp.dot(q_block, w_query, preferred_element_type=jnp.float32) * QR ** (-0.5)
    queries = queries.reshape(token_count, head_count, head_width)
    query_nope = jnp.transpose(queries[:, :, :NOPE], (1, 0, 2)).astype(jnp.bfloat16)
    query_rope = rotate_rope(jnp.transpose(queries[:, :, NOPE:], (1, 0, 2)), query_pos).astype(
        jnp.bfloat16
    )
    key_heads = w_key.reshape(KVR, head_count, NOPE)
    absorbed = (
        jnp.einsum("htn,khn->htk", query_nope, key_heads, preferred_element_type=jnp.float32)
        * KVR ** (-0.5)
    ).astype(jnp.bfloat16)

    def empty_state():
        return (
            jnp.full((head_count, half_rows), -1e30, jnp.float32),
            jnp.zeros((head_count, half_rows), jnp.float32),
            jnp.zeros((head_count, half_rows, KVR), jnp.float32),
        )

    start_states = (empty_state(), empty_state())
    kv_piece = lax.all_gather(kv_block, "ctx", axis=0, tiled=True)
    rope_piece = lax.all_gather(rope_block, "ctx", axis=0, tiled=True)
    piece_rows = kv_piece.shape[0]
    block_rows = math.gcd(piece_rows, half_rows)

    def one_block(block_index, states):
        offset = block_index * block_rows
        kv_part = lax.dynamic_slice_in_dim(kv_piece, offset, block_rows, 0)
        rope_keys = lax.dynamic_slice_in_dim(rope_piece, offset, block_rows, 0)
        layout_row = offset + jnp.arange(block_rows, dtype=jnp.int32)
        key_pos = block_order[layout_row // half_rows] * half_rows + layout_row % half_rows
        updated = []
        for half_index in range(2):
            first_row = half_index * half_rows
            q_abs = absorbed[:, first_row : first_row + half_rows]
            q_rot = query_rope[:, first_row : first_row + half_rows]
            q_pos = query_pos[first_row : first_row + half_rows]

            def compute(state, q_abs=q_abs, q_rot=q_rot, q_pos=q_pos):
                running, totals, accumulated = state
                scores = jnp.einsum(
                    "htk,sk->hts", q_abs, kv_part, preferred_element_type=jnp.float32
                )
                scores = (
                    scores
                    + jnp.einsum(
                        "htr,sr->hts", q_rot, rope_keys, preferred_element_type=jnp.float32
                    )
                ) * score_scale
                allowed = key_pos[None, None, :] <= q_pos[None, :, None]
                block_peak = jnp.max(jnp.where(allowed, scores, -1e30), axis=2)
                new_peak = jnp.maximum(running, block_peak)
                weights = jnp.where(allowed, jnp.exp(scores - new_peak[:, :, None]), 0.0)
                factor = jnp.exp(running - new_peak)
                totals = totals * factor + jnp.sum(weights, axis=2)
                accumulated = accumulated * factor[:, :, None] + jnp.einsum(
                    "hts,sk->htk",
                    weights.astype(jnp.bfloat16),
                    kv_part,
                    preferred_element_type=jnp.float32,
                )
                return (new_peak, totals, accumulated)

            def unchanged(state):
                return state

            updated.append(
                lax.cond(jnp.min(key_pos) <= jnp.max(q_pos), compute, unchanged, states[half_index])
            )
        return tuple(updated)

    states = lax.fori_loop(0, piece_rows // block_rows, one_block, start_states)
    latent_out = jnp.concatenate(
        [
            (states[half_index][2] / states[half_index][1][:, :, None]).astype(jnp.bfloat16)
            for half_index in range(2)
        ],
        axis=1,
    )
    value_heads = w_value.reshape(KVR, head_count, VDIM)
    attn_out = (
        jnp.einsum("htk,khv->thv", latent_out, value_heads, preferred_element_type=jnp.float32)
        * KVR ** (-0.5)
    ).astype(jnp.bfloat16)
    attn_out = attn_out.reshape(token_count, head_count * VDIM)
    local_peak = jnp.maximum(jnp.max(states[0][0], axis=1), jnp.max(states[1][0], axis=1))
    head_peaks = lax.pmax(local_peak, "ctx")
    ctx_count = lax.axis_size("ctx")
    owned_rows_q = QR // ctx_count
    owned_rows_k = KVR // ctx_count
    row_offset_q = ctx_index * owned_rows_q
    row_offset_k = ctx_index * owned_rows_k
    grad_q_rows = lax.psum_scatter(
        contract_rows(q_block, grad_query), "ctx", scatter_dimension=0, tiled=True
    )
    grad_k_rows = lax.psum_scatter(
        contract_rows(kv_block, grad_key), "ctx", scatter_dimension=0, tiled=True
    )
    matrices_q = heads_first(MOMENTUM * mom_query + grad_q_rows, head_width)
    matrices_k = heads_first(MOMENTUM * mom_key + grad_k_rows, NOPE)
    norms_q, norms_k = lax.psum(
        (
            jnp.sum(matrices_q * matrices_q, axis=(1, 2)),
            jnp.sum(matrices_k * matrices_k, axis=(1, 2)),
        ),
        "ctx",
    )
    matrices_q = matrices_q / (jnp.sqrt(norms_q)[:, None, None] + 1e-07)
    matrices_k = matrices_k / (jnp.sqrt(norms_k)[:, None, None] + 1e-07)
    for iteration in range(NS_STEPS):
        gram_q, gram_k = lax.psum((gram_of(matrices_q), gram_of(matrices_k)), "ctx")
        matrices_q = polish(matrices_q, gram_q)
        matrices_k = polish(matrices_k, gram_k)
    step_query = heads_last(matrices_q) * (0.2 * math.sqrt(QR))
    step_key = heads_last(matrices_k) * (0.2 * math.sqrt(KVR))
    clip_gamma = jnp.where(clip_flags > 0, CLIP_TAU / jnp.maximum(head_peaks, CLIP_TAU), 1.0)
    root_gamma = jnp.sqrt(clip_gamma)
    query_factor = jnp.concatenate(
        [
            jnp.broadcast_to(root_gamma[:, None], (head_count, NOPE)),
            jnp.broadcast_to(clip_gamma[:, None], (head_count, ROPE)),
        ],
        axis=1,
    ).reshape(-1)
    key_factor = jnp.repeat(root_gamma, NOPE)
    owned_query = lax.dynamic_slice_in_dim(w_query, row_offset_q, owned_rows_q, 0).astype(
        jnp.float32
    )
    owned_key = lax.dynamic_slice_in_dim(w_key, row_offset_k, owned_rows_k, 0).astype(jnp.float32)
    new_query = (owned_query * (1.0 - LEARN_RATE * DECAY) - LEARN_RATE * step_query) * query_factor[
        None, :
    ]
    new_key = (owned_key * (1.0 - LEARN_RATE * DECAY) - LEARN_RATE * step_key) * key_factor[None, :]
    return (attn_out, head_peaks, step_query, step_key, new_query, new_key)


def solution(mesh):
    in_specs = (
        P(("ctx", "dp"), None),
        P(("ctx", "dp"), None),
        P(("ctx", "dp"), None),
        P(),
        P(None, "dp"),
        P(None, "dp"),
        P(None, "dp"),
        P("ctx", "dp"),
        P("ctx", "dp"),
        P("ctx", "dp"),
        P("ctx", "dp"),
        P("dp"),
    )
    out_specs = (
        P("ctx", "dp"),
        P("dp"),
        P("ctx", "dp"),
        P("ctx", "dp"),
        P("ctx", "dp"),
        P("ctx", "dp"),
    )
    return jax.shard_map(shards, mesh=mesh, in_specs=in_specs, out_specs=out_specs, check_vma=False)
```

profile of v0, /device:TPU:24, one launch (start us, length us, event | category | flops | bytes accessed | tf_op | source)
XLA Modules:
  0.0 2309.1 jit_solution(16533561966988783652)
XLA Ops:
  7.2 7.6 all_gather.15
  18.7 10.2 all_gather.19
  34.1 144.9 %reduce-scatter.5.cloned.1.call-done = f32[16,1024]{1,0:T(8,128)} async-done(((f32[512,1024]{1,0:T(8,128)}), f32[16,1024]{1,0:T(8,128)}) %reduce-scatter.5.cloned.1.call-update) | async-done | bytes 65552 | tf_op jit(solution)/shard_map/reduce_scatter | solution.py:195
  180.0 211.4 %reduce-scatter.3.cloned.1.call-done = f32[48,1536]{1,0:T(8,128)} async-done(((f32[1536,1536]{1,0:T(8,128)}), f32[48,1536]{1,0:T(8,128)}) %reduce-scatter.3.cloned.1.call-update) | async-done | bytes 294928 | tf_op jit(solution)/shard_map/reduce_scatter | solution.py:192
  392.7 79.8 %all-reduce = (f32[8]{0:T(128)S(1)}, f32[8]{0:T(128)S(1)}) all-reduce(f32[8]{0:T(128)S(1)} %multiply_reduce_fusion, f32[8]{0:T(128)S(1)} %fusion.82), channel_id=1, replica_groups=mesh['ctx'=32,'dp'=4] {'ctx'}, use_global_device_ids=true, to_apply=%region_18.19 | all-reduce | flops 16 | bytes 128 | tf_op jit(solution)/shard_map/psum | solution.py:200
  477.3 7.2 all_gather.17
  484.7 304.8 %all-reduce.12.cloned.1.call-done = (f32[8,192,192]{2,1,0:T(8,128)}, f32[8,128,128]{2,1,0:T(8,128)}) async-done(((f32[8,192,192]{2,1,0:T(8,128)}, f32[8,128,128]{2,1,0:T(8,128)}), (f32[8,192,192]{2,1,0:T(8,128)}, f32[8,128,128]{2,1,0:T(8,128)})) %all-reduce.12.cloned.1.call-update) | async-done | bytes 1703952 | tf_op jit(solution)/shard_map/psum | solution.py:210
  814.7 129.5 %all-gather.5.cloned.1.call-done = bf16[8192,64]{1,0:T(8,128)(2,1)} async-done(((bf16[256,64]{1,0:T(8,128)(2,1)}), bf16[8192,64]{1,0:T(8,128)(2,1)}) %all-gather.5.cloned.1.call-update) | async-done | bytes 1048592 | tf_op jit(solution)/shard_map/all_gather | solution.py:121
  946.9 313.8 %all-reduce.10.cloned.1.call-done = (f32[8,192,192]{2,1,0:T(8,128)}, f32[8,128,128]{2,1,0:T(8,128)}) async-done(((f32[8,192,192]{2,1,0:T(8,128)}, f32[8,128,128]{2,1,0:T(8,128)}), (f32[8,192,192]{2,1,0:T(8,128)}, f32[8,128,128]{2,1,0:T(8,128)})) %all-reduce.10.cloned.1.call-update) | async-done | bytes 1703952 | tf_op jit(solution)/shard_map/psum | solution.py:210
  1272.2 178.4 %all-gather.3.cloned.1.call-done = bf16[8192,512]{1,0:T(8,128)(2,1)} async-done(((bf16[256,512]{1,0:T(8,128)(2,1)}), bf16[8192,512]{1,0:T(8,128)(2,1)}) %all-gather.3.cloned.1.call-update) | async-done | bytes 8388624 | tf_op jit(solution)/shard_map/all_gather | solution.py:120
  1452.4 747.3 %while.25 = (s32[]{:T(128)}, f32[8,128]{1,0:T(8,128)S(1)}, f32[8,128]{1,0:T(8,128)S(1)}, f32[8,128,512]{2,1,0:T(8,128)}, f32[8,128]{1,0:T(8,128)S(1)}, /*index=5...) while((s32[]{:T(128)}, f32[8,128]{1,0:T(8,128)S(1)}, ...), condition=%wide.region_12.13_spmd, body=%wide.region_2.12_spmd.sunk | while | flops 575186176 | bytes 17117196 | solution.py:171
  1470.4 5.7 conditional.4
  1482.2 5.7 conditional.4
  1494.1 5.7 conditional.4
  1509.0 5.7 conditional.4
  1532.7 5.7 conditional.4
  1568.2 5.7 conditional.4
  1580.0 5.7 conditional.4
  1646.0 5.7 conditional.4
  1681.5 5.7 conditional.4
  1693.3 5.7 conditional.4
  1705.2 5.7 conditional.4
  1752.4 5.7 conditional.4
  2200.0 86.7 %pmax.7 = f32[8]{0:T(128)S(1)} all-reduce(f32[8]{0:T(128)S(1)} %max.14), channel_id=1, replica_groups=mesh['ctx'=32,'dp'=4] {'ctx'}, use_global_device_ids=true, to_apply=%region_15.16 | all-reduce | flops 8 | bytes 64 | tf_op jit(solution)/shard_map/pmax | solution.py:186
  (1203 shorter events, 933.1 us)
Async XLA Ops:
  7.2 21.7 copy-start
  7.2 171.8 %reduce-scatter.5.cloned.1.call-start = ((), (), s32[]{:S(2)}) async-start(), calls=%async_computation.5 | async-start | bytes 2162688 | tf_op jit(solution)/shard_map/reduce_scatter | solution.py:195
  14.9 2.9 copy-start.6
  17.8 0.9 copy-start.13
  17.8 373.6 %reduce-scatter.3.cloned.1.call-start = ((), (), s32[]{:S(2)}) async-start(), calls=%async_computation.4 | async-start | bytes 9732096 | tf_op jit(solution)/shard_map/reduce_scatter | solution.py:192
  34.0 145.0 %copy-start.14 = (f32[16,1024]{1,0:T(8,128)S(1)}, f32[16,1024]{1,0:T(8,128)}, u32[]{:S(2)}) copy-start(f32[16,1024]{1,0:T(8,128)} %param.28) | copy-start | bytes 196612
  34.0 357.4 %copy-start.12 = (f32[48,1536]{1,0:T(8,128)S(1)}, f32[48,1536]{1,0:T(8,128)}, u32[]{:S(2)}) copy-start(f32[48,1536]{1,0:T(8,128)} %param.27) | copy-start | bytes 884740
  34.0 755.5 %all-reduce.12.cloned.1.call-start = ((), (), s32[]{:S(2)}) async-start(), calls=%async_computation.8 | async-start | bytes 4194304 | tf_op jit(solution)/shard_map/psum | solution.py:210
  475.3 1.9 copy-start.15
  477.2 467.0 %all-gather.5.cloned.1.call-start = ((), (), s32[]{:S(2)}) async-start(), calls=%async_computation.3 | async-start | bytes 2162688 | tf_op jit(solution)/shard_map/all_gather | solution.py:121
  484.5 776.2 %all-reduce.10.cloned.1.call-start = ((), (), s32[]{:S(2)}) async-start(), calls=%async_computation.7 | async-start | bytes 4194304 | tf_op jit(solution)/shard_map/psum | solution.py:210
  789.5 4.6 copy-start.4
  800.0 1.2 copy-start.10
  800.1 650.5 %all-gather.3.cloned.1.call-start = ((), (), s32[]{:S(2)}) async-start(), calls=%async_computation.2 | async-start | bytes 8650752 | tf_op jit(solution)/shard_map/all_gather | solution.py:120
  800.6 1490.3 %all-reduce.8.cloned.1.call-start = ((), (), s32[]{:S(2)}) async-start(), calls=%async_computation.6 | async-start | bytes 4194304 | tf_op jit(solution)/shard_map/psum | solution.py:210
  807.5 1.9 copy-start.2
  811.4 1.2 copy-start.9
  1260.7 4.8 copy-start.3
  2286.6 4.0 copy-start.17
  2286.6 2.1 copy-start.11
  2288.8 1.8 copy-start.16
  2290.9 3.5 copy-start.5
  2294.4 1.7 copy-start.8
  2297.7 4.6 copy-start.1
  (1 other events, 0.7 us)
Sparse Core Ops, SparseCore 0:
  17.9 160.9 reduce-scatter.4
  181.5 209.8 reduce-scatter.2
  477.3 312.1 all-reduce.11
  791.0 153.1 all-gather.4
  947.2 313.4 all-reduce.9
  1262.9 187.6 all-gather.2
  1453.3 314.5 all-reduce.7
where the time goes:
time: 2320 us; the launch traced here: 2310 us
  waiting for transfers between devices  1280 us (55%)
  matrix products  383 us (17%)
  local copies, waits for them, and re-layouts  199 us (9%)
  blocking collectives  192 us (8%)
  loops' own time  173 us (7%)
  other arithmetic  64.2 us (3%)
    psum x3, waiting for transfers between devices, shards(): gram_q, gram_k = lax.psum((gram_of(matrices_q), gram_of(matrices_k)), 'ctx')  619 us
    reduce_scatter x1, waiting for transfers between devices, shards(): lax.psum_scatter(contract_rows(q_block, grad_query), 'ctx', scatter_dimen...  211 us
    dot_general x65, matrix products, compute(): jnp.einsum('hts,sk->htk', weights.astype(jnp.bfloat16), kv_part, preferre...  206 us
    all_gather x1, waiting for transfers between devices, shards(): kv_piece = lax.all_gather(kv_block, 'ctx', axis=0, tiled=True)  178 us
    another operation x1, loops' own time, shards(): states = lax.fori_loop(0, piece_rows // block_rows, one_block, start_states)  168 us
    reduce_scatter x1, waiting for transfers between devices, shards(): lax.psum_scatter(contract_rows(kv_block, grad_key), 'ctx', scatter_dimens...  145 us
    all_gather x1, waiting for transfers between devices, shards(): rope_piece = lax.all_gather(rope_block, 'ctx', axis=0, tiled=True)  129 us
    dot_general x65, matrix products, compute(): jnp.einsum('htk,sk->hts', q_abs, kv_part, preferred_element_type=jnp.floa...  112 us
  transfers between devices with their start and end apart: 7, of which 6 were waited for; matrix products, arithmetic and copies ran while one was open for 27% of the time, Pallas kernels for 0%

commit v1 on v0

v1 whole, which is shorter than its diff:
```python
import functools
import math

import jax
import jax.numpy as jnp
from jax import lax
from jax.experimental import pallas as pl
from jax.experimental.pallas import tpu as pltpu
from jax.sharding import Mesh
from jax.sharding import PartitionSpec as P

QR = 1536
KVR = 512
NOPE = 128
ROPE = 64
WIDE = 640
NS_STEPS = 3
NS_A = 3.4445
NS_B = -4.775
NS_C = 2.0315
MOMENTUM = 0.95
LEARN_RATE = 0.05
DECAY = 0.1
CLIP_TAU = 6.0
ROPE_THETA = 50000.0
HEAD = NOPE + ROPE
SCALE = HEAD ** (-0.5)
LOG2E = math.log2(math.e)
FULL = lax.Precision.HIGHEST
F32 = jnp.float32
BF16 = jnp.bfloat16
LOW = -1e30
ANY = pl.BlockSpec(memory_space=pl.ANY)
VMEM = pl.BlockSpec(memory_space=pltpu.VMEM)
SMEM = pl.BlockSpec(memory_space=pltpu.SMEM)
TILE = 512


def shift_first(k):
    pairs = []
    for z in range(4):
        for x in range(4):
            pairs.append(((z * 4 + x) * 2, (((z + k) % 4) * 4 + x) * 2))
            pairs.append(((z * 4 + x) * 2 + 1, (z * 4 + (x + k) % 4) * 2 + 1))
    return pairs


def shift_second(k):
    pairs = []
    for z in range(4):
        for x in range(4):
            pairs.append(((z * 4 + x) * 2, (z * 4 + (x + k) % 4) * 2))
            pairs.append(((z * 4 + x) * 2 + 1, (((z + k) % 4) * 4 + x) * 2 + 1))
    return pairs


def move_first(value, k):
    return lax.ppermute(value, ("z", "x", "c"), shift_first(k))


def move_second(value, k):
    return lax.ppermute(value, ("z", "x", "c"), shift_second(k))


def move_z(value, k):
    return lax.ppermute(value, "z", [(i, (i + k) % 4) for i in range(4)])


def flip(value, k):
    pairs = []
    for yl in range(2):
        for yh in range(2):
            pairs.append((yl * 2 + yh, (yl ^ (k & 1)) * 2 + (yh ^ (k >> 1))))
    return lax.ppermute(value, ("yl", "yh"), pairs)


def swap_core(value):
    return lax.ppermute(value, "c", [(0, 1), (1, 0)])


def attention_kernel(count_ref, place_ref, spos_ref, qpos_ref, q_ref, wv_ref, *rest):
    pieces = rest[:8]
    out_ref, peak_ref = rest[8:10]
    keys, acc, top, total, sem = rest[10:]
    for side in range(2):
        for part in range(4):
            piece = pieces[side * 4 + part]

            @pl.loop(0, 16)
            def _(s, piece=piece, side=side, part=part):
                row = pl.multiple_of(place_ref[side * 64 + part * 16 + s], 64)
                pltpu.make_async_copy(piece.at[s], keys.at[pl.ds(row, 64)], sem).start()

    pltpu.make_async_copy(keys, keys, sem).wait()
    factor = SCALE * LOG2E
    for half in range(2):
        top[...] = jnp.full(top.shape, LOW, F32)
        total[...] = jnp.zeros(total.shape, F32)
        acc[...] = jnp.zeros(acc.shape, F32)
        tiles = lax.div(count_ref[half] + 3, 4)

        def tile(j, masked, half=half):
            row0 = pl.multiple_of(j * TILE, TILE)
            for chunk in range(4):
                rows = pl.ds(chunk * 256, 256)
                q = q_ref[half, rows, :]
                k = keys[pl.ds(row0, TILE), :]
                s = lax.dot_general(q, k, (((1,), (1,)), ((), ())), preferred_element_type=F32)
                if masked:
                    row_pos = qpos_ref[half] * 128 + (
                        lax.broadcasted_iota(jnp.int32, (256, 128), 0) & 127
                    )
                    col = lax.broadcasted_iota(jnp.int32, (256, 128), 1)
                    parts = []
                    for b in range(4):
                        ok = spos_ref[j * 4 + b] * 128 + col <= row_pos
                        parts.append(jnp.where(ok, s[:, b * 128 : (b + 1) * 128], LOW))
                    s = jnp.concatenate(parts, axis=1)
                old = top[rows, :]
                new = jnp.maximum(old, jnp.max(s, axis=1, keepdims=True))
                p = jnp.exp2((s - new[:, :1]) * factor)
                keep = jnp.exp2((old - new) * factor)
                top[rows, :] = new
                total[rows, :] = total[rows, :] * keep + jnp.sum(p, axis=1, keepdims=True)
                acc[rows, :] = acc[rows, :] * keep[:, :1] + jnp.dot(
                    p.astype(BF16), k[:, :KVR], preferred_element_type=F32
                )

        @pl.loop(0, tiles - 1)
        def _(j):
            tile(j, False)

        tile(tiles - 1, True)
        for h in range(8):
            rows = pl.ds(h * 128, 128)
            latent = (acc[rows, :] / total[rows, :1]).astype(BF16)
            o = jnp.dot(latent, wv_ref[:, h * 128 : (h + 1) * 128], preferred_element_type=F32)
            out_ref[half * 128 : (half + 1) * 128, h * 128 : (h + 1) * 128] = (
                o * KVR ** (-0.5)
            ).astype(BF16)
            peak = jnp.max(top[rows, :], axis=0, keepdims=True) * SCALE
            if half == 0:
                peak_ref[h : h + 1, :] = peak
            else:
                peak_ref[h : h + 1, :] = jnp.maximum(peak_ref[h : h + 1, :], peak)


def attention(count, place, spos, qpos, queries, w_value, pieces):
    return pl.pallas_call(
        attention_kernel,
        out_shape=(
            jax.ShapeDtypeStruct((256, 1024), BF16),
            jax.ShapeDtypeStruct((8, 128), F32),
        ),
        in_specs=[SMEM] * 4 + [VMEM] * 2 + [ANY] * 8,
        out_specs=(VMEM, VMEM),
        scratch_shapes=[
            pltpu.VMEM((8192, WIDE), BF16),
            pltpu.VMEM((1024, KVR), F32),
            pltpu.VMEM((1024, 128), F32),
            pltpu.VMEM((1024, 128), F32),
            pltpu.SemaphoreType.DMA,
        ],
        compiler_params=pltpu.CompilerParams(vmem_limit_bytes=48 * 2**20),
        cost_estimate=pl.CostEstimate(
            flops=20 * 10**9, bytes_accessed=14 * 2**20, transcendentals=9 * 10**6
        ),
        name="attention",
    )(count, place, spos, qpos, queries, w_value, *pieces)


def gradient_kernel(zb_ref, xb_ref, g_own, g_other, l_own, l_other, *outs):
    for k in range(4):

        @pl.loop(0, 4)
        def _(j, k=k):
            zb = zb_ref[4 * k + j]
            xb = xb_ref[4 * k + j]

            def block(row0, height, col0, width):
                rows = pl.ds(pl.multiple_of(row0, 64), height)
                cols = pl.ds(pl.multiple_of(col0, 128), width)
                return jnp.dot(
                    g_own[rows, :], l_own[:, cols], preferred_element_type=F32
                ) + jnp.dot(g_other[rows, :], l_other[:, cols], preferred_element_type=F32)

            m = block(xb * HEAD, HEAD, zb * 384, 384)
            for t in range(3):
                outs[k][j, t * HEAD : (t + 1) * HEAD, :] = m[:, t * 128 : (t + 1) * 128]
            outs[k][j, 3 * HEAD : 704, :] = block(768 + xb * 128, 128, QR + zb * 128, 128)


def gradient_terms(zb, xb, g_own, g_other, l_own, l_other):
    return pl.pallas_call(
        gradient_kernel,
        out_shape=tuple(jax.ShapeDtypeStruct((4, 704, 128), F32) for _ in range(4)),
        in_specs=[SMEM] * 2 + [VMEM] * 4,
        out_specs=tuple(VMEM for _ in range(4)),
        compiler_params=pltpu.CompilerParams(vmem_limit_bytes=32 * 2**20),
        cost_estimate=pl.CostEstimate(
            flops=15 * 10**8, bytes_accessed=10 * 2**20, transcendentals=0
        ),
        name="gradient_terms",
    )(zb, xb, g_own, g_other, l_own, l_other)


def nt(a, b):
    return lax.dot_general(
        a, b, (((1,), (1,)), ((), ())), precision=FULL, preferred_element_type=F32
    )


def gram_kernel(a_ref, b_ref, c_ref, d_ref, mom_ref, m_ref, g_ref):
    m_ref[...] = (a_ref[...] + b_ref[...]) + (c_ref[...] + d_ref[...]) + MOMENTUM * mom_ref[...]
    g_ref[...] = jnp.zeros(g_ref.shape, F32)
    gram = None
    for t in range(3):
        block = m_ref[t * HEAD : (t + 1) * HEAD, :]
        term = nt(block, block)
        gram = term if gram is None else gram + term
    g_ref[:, :HEAD] = gram
    block = m_ref[3 * HEAD : 704, :]
    g_ref[:128, 256:384] = nt(block, block)


def moment_and_gram(parts, mom):
    return pl.pallas_call(
        gram_kernel,
        out_shape=(
            jax.ShapeDtypeStruct((704, 128), F32),
            jax.ShapeDtypeStruct((HEAD, 384), F32),
        ),
        in_specs=[VMEM] * 5,
        out_specs=(VMEM, VMEM),
        cost_estimate=pl.CostEstimate(
            flops=2 * 10**8, bytes_accessed=3 * 2**20, transcendentals=0
        ),
        name="moment_and_gram",
    )(*parts, mom)


def full_dot(a, b):
    return jnp.dot(a, b, precision=FULL, preferred_element_type=F32)


def newton_factor(gram):
    size = gram.shape[0]
    eye = (
        lax.broadcasted_iota(jnp.int32, (size, size), 0)
        == lax.broadcasted_iota(jnp.int32, (size, size), 1)
    ).astype(F32)
    square = jnp.sum(jnp.sum(gram * eye, axis=1, keepdims=True), axis=0, keepdims=True)
    inverse = 1.0 / (jnp.sqrt(square) + 1e-07)
    a = gram * inverse * inverse
    product = None
    for step in range(NS_STEPS):
        factor = NS_A * eye + NS_B * a + NS_C * full_dot(a, a)
        product = factor if product is None else full_dot(product, factor)
        if step + 1 < NS_STEPS:
            a = full_dot(full_dot(factor, a), factor)
    return product * inverse


def newton_kernel(m_ref, a_ref, b_ref, c_ref, d_ref, out_ref):
    gram = (a_ref[...] + b_ref[...]) + (c_ref[...] + d_ref[...])
    factor_q = newton_factor(gram[:, :HEAD]) * (0.2 * math.sqrt(QR))
    factor_k = newton_factor(gram[:128, 256:384]) * (0.2 * math.sqrt(KVR))
    rows = []
    for t in range(3):
        block = m_ref[t * HEAD : (t + 1) * HEAD, :]
        rows.append(
            lax.dot_general(
                block, factor_q, (((0,), (0,)), ((), ())), precision=FULL, preferred_element_type=F32
            )
        )
    step = jnp.concatenate(rows, axis=0)
    step_k = lax.dot_general(
        m_ref[3 * HEAD : 704, :],
        factor_k,
        (((0,), (0,)), ((), ())),
        precision=FULL,
        preferred_element_type=F32,
    )
    out_ref[...] = jnp.zeros(out_ref.shape, F32)
    for i in range(8):
        out_ref[i, :48, :HEAD] = step[i * 48 : (i + 1) * 48, :]
        out_ref[i, 48:, :128] = step_k[i * 16 : (i + 1) * 16, :]


def newton(moment, grams):
    return pl.pallas_call(
        newton_kernel,
        out_shape=jax.ShapeDtypeStruct((8, 64, 256), F32),
        in_specs=[VMEM] * 5,
        out_specs=VMEM,
        cost_estimate=pl.CostEstimate(
            flops=10**9, bytes_accessed=3 * 2**20, transcendentals=0
        ),
        name="newton",
    )(moment, *grams)


def rotate_rope(rope_part, positions):
    pair_count = ROPE // 2
    frequency = ROPE_THETA ** (-2.0 * jnp.arange(pair_count, dtype=F32) / ROPE)
    angles = positions.astype(F32)[:, None] * frequency[None, :]
    cosine = jnp.cos(angles)
    sine_part = jnp.sin(angles)
    first_half = rope_part[..., :pair_count]
    second_half = rope_part[..., pair_count:]
    return jnp.concatenate(
        [
            first_half * cosine - second_half * sine_part,
            second_half * cosine + first_half * sine_part,
        ],
        axis=-1,
    )


def look_up(table, index):
    hit = index[:, None] == jnp.arange(table.shape[0], dtype=jnp.int32)[None, :]
    return jnp.sum(jnp.where(hit, table[None, :], 0), axis=1)


def shards(
    q_latent,
    kv_latent,
    key_rope,
    block_order,
    w_query,
    w_key,
    w_value,
    grad_query,
    grad_key,
    mom_query,
    mom_key,
    clip_flags,
):
    z, x, c = lax.axis_index("z"), lax.axis_index("x"), lax.axis_index("c")
    yl, yh = lax.axis_index("yl"), lax.axis_index("yh")
    ctx = z * 8 + x * 2 + yl
    rows_in = jnp.concatenate(
        [q_latent, kv_latent, key_rope, jnp.zeros((64, 64), BF16)], axis=1
    )
    key_rows = rows_in[:, QR:]
    flips = [rows_in] + [flip(rows_in, k) for k in (1, 2, 3)]
    swapped = swap_core(jnp.stack(flips))
    shared = [
        [jnp.where(c == side, flips[k], swapped[k]) for side in range(2)] for k in range(4)
    ]

    def token_rows(low):
        halves = []
        for block in range(2):
            for side in range(2):
                halves.append(jnp.where(yh == block, shared[low][side], shared[low + 2][side]))
        return jnp.concatenate(halves, axis=0)

    l_own, l_other = token_rows(0), token_rows(1)
    grad_q_t = grad_query.T.reshape(2, 768, 256)
    grad_k_t = grad_key.T.reshape(2, 512, 256)

    def head_half(which):
        return jnp.concatenate(
            [
                jnp.where(which == 0, grad_q_t[0], grad_q_t[1]),
                jnp.where(which == 0, grad_k_t[0], grad_k_t[1]),
            ],
            axis=0,
        )

    g_own = head_half(yl)
    g_other = lax.ppermute(head_half(1 - yl), "yl", [(0, 1), (1, 0)])
    step_a = jnp.stack([key_rows] + [move_first(key_rows, k) for k in (1, 2, 3)])
    plane = jnp.stack([step_a] + [move_second(step_a, k) for k in (1, 2, 3)])
    plane = plane.reshape(16, 64, WIDE)
    mine = [plane] + [flip(plane, k) for k in (1, 2, 3)]
    theirs = [swap_core(piece) for piece in mine]
    mom_q = mom_query.reshape(48, 2, 4, HEAD).transpose(2, 1, 0, 3).reshape(8, 72, 128)
    mom_k = mom_key.reshape(16, 2, 4, 128).transpose(2, 1, 0, 3).reshape(8, 16, 128)
    mom = lax.all_to_all(jnp.concatenate([mom_q, mom_k], axis=1), ("x", "yl"), 0, 0)
    mom_q = mom[:, :72].reshape(3, 128, HEAD).transpose(0, 2, 1).reshape(576, 128)
    mom_k = mom[:, 72:].reshape(128, 128).T
    mom = jnp.concatenate([mom_q, mom_k], axis=0)
    k_index = jnp.arange(16, dtype=jnp.int32) // 4
    j_index = jnp.arange(16, dtype=jnp.int32) % 4
    zb = jnp.where(c == 0, z + k_index, z + j_index) % 4
    xb = jnp.where(c == 0, x + j_index, x + k_index) % 4
    terms = gradient_terms(zb, xb, g_own, g_other, l_own, l_other)
    stage = [terms[0]] + [move_first(terms[k], k) for k in (1, 2, 3)]
    sums = [(stage[0][j] + stage[1][j]) + (stage[2][j] + stage[3][j]) for j in range(4)]
    parts = [sums[0]] + [move_second(sums[k], k) for k in (1, 2, 3)]
    moment, gram = moment_and_gram(parts, mom)
    steps = newton(moment, [gram] + [move_z(gram, k) for k in (1, 2, 3)])
    steps = lax.all_to_all(steps, ("x", "yl"), 0, 0)
    step_query = (
        steps[:, :48, :HEAD].reshape(4, 2, 48, HEAD).transpose(2, 1, 0, 3).reshape(48, QR)
    )
    step_key = steps[:, 48:, :128].reshape(4, 2, 16, 128).transpose(2, 1, 0, 3).reshape(16, 1024)
    local_rows = jnp.arange(256, dtype=jnp.int32)
    qpos = look_up(block_order, 2 * ctx + jnp.arange(2, dtype=jnp.int32))
    query_pos = jnp.where(local_rows < 128, qpos[0], qpos[1]) * 128 + local_rows % 128
    queries = jnp.dot(l_own[:, :QR], w_query, preferred_element_type=F32) * QR ** (-0.5)
    queries = queries.reshape(256, 8, HEAD)
    query_nope = jnp.transpose(queries[:, :, :NOPE], (1, 0, 2)).astype(BF16)
    query_rope = rotate_rope(jnp.transpose(queries[:, :, NOPE:], (1, 0, 2)), query_pos).astype(
        BF16
    )
    absorbed = (
        jnp.einsum(
            "htn,khn->htk",
            query_nope,
            w_key.reshape(KVR, 8, NOPE),
            preferred_element_type=F32,
        )
        * KVR ** (-0.5)
    ).astype(BF16)
    wide = jnp.concatenate([absorbed, query_rope, jnp.zeros((8, 256, 64), BF16)], axis=2)
    wide = wide.reshape(8, 2, 128, WIDE).transpose(1, 0, 2, 3).reshape(2, 1024, WIDE)
    slot = jnp.arange(64, dtype=jnp.int32)
    part, b, a = slot // 16, (slot // 4) % 4, slot % 4
    part_yl, part_yh = (yl + part) % 2, (yh + part // 2) % 2

    def ranks(core):
        zz = jnp.where(core == 0, z - a, z - b) % 4
        xx = jnp.where(core == 0, x - b, x - a) % 4
        return look_up(block_order, 2 * (zz * 8 + xx * 2 + part_yl) + part_yh)

    place = jnp.concatenate([ranks(c) * 128 + c * 64, ranks(1 - c) * 128 + (1 - c) * 64])
    attn_out, peaks = attention(
        qpos + 1, place.astype(jnp.int32), slot, qpos, wide, w_value, mine + theirs
    )
    peaks = lax.all_to_all(jnp.broadcast_to(peaks[None], (32, 8, 128)), ("z", "x", "yl"), 0, 0)
    head_peaks = jnp.max(peaks, axis=0)[:, 0]
    clip_gamma = jnp.where(clip_flags > 0, CLIP_TAU / jnp.maximum(head_peaks, CLIP_TAU), 1.0)
    root_gamma = jnp.sqrt(clip_gamma)
    query_factor = jnp.concatenate(
        [
            jnp.broadcast_to(root_gamma[:, None], (8, NOPE)),
            jnp.broadcast_to(clip_gamma[:, None], (8, ROPE)),
        ],
        axis=1,
    ).reshape(-1)
    key_factor = jnp.repeat(root_gamma, NOPE)
    owned_query = lax.dynamic_slice_in_dim(w_query, ctx * 48, 48, 0).astype(F32)
    owned_key = lax.dynamic_slice_in_dim(w_key, ctx * 16, 16, 0).astype(F32)
    keep = 1.0 - LEARN_RATE * DECAY
    new_query = (owned_query * keep - LEARN_RATE * step_query) * query_factor[None, :]
    new_key = (owned_key * keep - LEARN_RATE * step_key) * key_factor[None, :]
    return (attn_out, head_peaks, step_query, step_key, new_query, new_key)


def solution(mesh):
    fine = Mesh(mesh.devices.reshape(4, 4, 2, 2, 2), ("z", "x", "yl", "yh", "c"))
    ctx, dp = ("z", "x", "yl"), ("yh", "c")
    tokens = P(ctx + dp, None)
    columns = P(None, dp)
    both = P(ctx, dp)
    in_specs = (
        tokens,
        tokens,
        tokens,
        P(),
        columns,
        columns,
        columns,
        both,
        both,
        both,
        both,
        P(dp),
    )
    out_specs = (both, P(dp), both, both, both, both)
    return jax.shard_map(shards, mesh=fine, in_specs=in_specs, out_specs=out_specs, check_vma=False)
```

time: 2320 us -> 293 us (0.13)
  waiting for transfers between devices: 1280 us -> 112 us
  matrix products: 383 us -> 7.26 us
  blocking collectives: 192 us -> 0 us
  local copies, waits for them, and re-layouts: 199 us -> 13.7 us
  loops' own time: 173 us -> 0 us
  Pallas kernels: 0 us -> 75 us
  starting transfers between devices: 0.69 us -> 65.4 us
  other arithmetic: 64.2 us -> 18.3 us
    psum x3 -> x0, waiting for transfers between devices: 619 us -> none  [shards(): gram_q, gram_k = lax.psum((gram_of(matrices_q), gram_of(matrices_k)), 'ctx')]
    dot_general x218 -> x2, matrix products: 383 us -> 7.26 us  [the longest x1 4.9 us: shards(): jnp.dot(l_own[:, :QR], w_query, preferred_element_type=F32) * QR ** (-0.5)]
    reduce_scatter x2 -> x0, waiting for transfers between devices: 356 us -> none  [the longest x1 211 us: shards(): lax.psum_scatter(contract_rows(q_block, grad_query), 'ctx', scatter_dimen...]
    all_gather x2 -> x0, waiting for transfers between devices: 308 us -> none  [the longest x1 178 us: shards(): kv_piece = lax.all_gather(kv_block, 'ctx', axis=0, tiled=True)]
    another operation x129 -> x0, loops' own time: 173 us -> none  [the longest x1 168 us: shards(): states = lax.fori_loop(0, piece_rows // block_rows, one_block, start_states)]
    dynamic_slice x128 -> x0, local copies, waits for them, and re-layouts: 105 us -> none  [the longest x64 58.4 us: one_block(): kv_part = lax.dynamic_slice_in_dim(kv_piece, offset, block_rows, 0)]
    ppermute x0 -> x27, waiting for transfers between devices: none -> 96.8 us  [the longest x6 54.1 us: flip(): return lax.ppermute(value, ('yl', 'yh'), pairs)]
    pmax x1 -> x0, blocking collectives: 86.7 us -> none  [shards(): head_peaks = lax.pmax(local_peak, 'ctx')]
  transfers between devices with their start and end apart: 7 -> 30, of which waited for: 6 -> 17; matrix products, arithmetic and copies ran while one was open for 27% -> 11% of each run, Pallas kernels for 0% -> 21%
where the time goes in v1:
time: 293 us; the launch traced here: 292 us
  waiting for transfers between devices  112 us (38%)
  Pallas kernels  75 us (26%)
  starting transfers between devices  65.4 us (22%)
  other arithmetic  18.3 us (6%)
  local copies, waits for them, and re-layouts  13.7 us (5%)
  matrix products  7.26 us (2%)
    pallas_call x1, Pallas kernels, attention(): pl.pallas_call(attention_kernel, out_shape=(jax.ShapeDtypeStruct((256, 10...  57.9 us
    ppermute x6, waiting for transfers between devices, flip(): return lax.ppermute(value, ('yl', 'yh'), pairs)  54.1 us
    ppermute x6, waiting for transfers between devices, move_second(): return lax.ppermute(value, ('z', 'x', 'c'), shift_second(k))  19.7 us
    ppermute x1, waiting for transfers between devices, shards(): g_other = lax.ppermute(head_half(1 - yl), 'yl', [(0, 1), (1, 0)])  13.9 us
    ppermute x3, starting transfers between devices, move_z(): return lax.ppermute(value, 'z', [(i, (i + k) % 4) for i in range(4)])  10.9 us
    ppermute x5, starting transfers between devices, swap_core(): return lax.ppermute(value, 'c', [(0, 1), (1, 0)])  10.3 us
    ppermute x6, starting transfers between devices, move_first(): return lax.ppermute(value, ('z', 'x', 'c'), shift_first(k))  10.2 us
    ppermute x6, starting transfers between devices, flip(): return lax.ppermute(value, ('yl', 'yh'), pairs)  9.56 us
  transfers between devices with their start and end apart: 30, of which 17 were waited for; matrix products, arithmetic and copies ran while one was open for 11% of the time, Pallas kernels for 21%

profile of v1, /device:TPU:24, one launch (start us, length us, event | category | flops | bytes accessed | tf_op | source)
XLA Modules:
  0.0 292.4 jit_solution(18328514279249718426)
XLA Ops:
  3.5 3.1 %collective-permute-start.2 = (bf16[64,2176]{1,0:T(8,128)(2,1)S(1)}, bf16[64,2176]{1,0:T(8,128)(2,1)S(1)}, u32[]{:S(2)}, u32[]{:S(2)}) collective-permute-start(bf16[64,2176]{1,0:T(8,128)(2,1)S(1)} %concatenate.37), channel_id=1, source_target_pairs={{0,6},{2,4},{4,2},{6,0},{1,7},{3,5},{5,3},{7,1},{8,14},{10,12},{12... | collective-permute-start | bytes 835592 | tf_op jit(solution)/shard_map/ppermute | solution.py:74
  6.6 4.8 %collective-permute-done = bf16[64,2176]{1,0:T(8,128)(2,1)S(1)} collective-permute-done((bf16[64,2176]{1,0:T(8,128)(2,1)S(1)}, bf16[64,2176]{1,0:T(8,128)(2,1)S(1)}, u32[]{:S(2)}, u32[]{:S(2)}) %collective-permute-start) | collective-permute-done | bytes 278560 | tf_op jit(solution)/shard_map/ppermute | solution.py:74
  11.4 4.4 %collective-permute-done.1 = bf16[64,2176]{1,0:T(8,128)(2,1)S(1)} collective-permute-done((bf16[64,2176]{1,0:T(8,128)(2,1)S(1)}, bf16[64,2176]{1,0:T(8,128)(2,1)S(1)}, u32[]{:S(2)}, u32[]{:S(2)}) %collective-permute-start.1) | collective-permute-done | bytes 278560 | tf_op jit(solution)/shard_map/ppermute | solution.py:74
  25.5 13.9 %collective-permute-done.17.g_other = bf16[1280,256]{1,0:T(8,128)(2,1)S(1)} collective-permute-done((bf16[1280,256]{1,0:T(8,128)(2,1)}, bf16[1280,256]{1,0:T(8,128)(2,1)S(1)}, u32[]{:S(2)}, u32[]{:S(2)}) %collective-permute-start.17) | collective-permute-done | bytes 655392 | tf_op jit(solution)/shard_map/ppermute | solution.py:373
  39.4 7.2 %gradient_terms.1 = (f32[4,704,128]{2,1,0:T(8,128)S(1)}, f32[4,704,128]{2,1,0:T(8,128)}, f32[4,704,128]{2,1,0:T(8,128)}, f32[4,704,128]{2,1,0:T(8,128)}) custom-call(s32[16]{0:T(128)S(1)} %get-tuple-element.53.zb_ref, s32[16]{0:T(128)S(1)} %get-tuple-element.52.xb_ref, bf16[1280,256]{1,0:T(8,128)(2,1)S(1)} %pad_maximum_fusion.4.g_own, ...), custom_call_target="tpu_custom_call" | custom-call | flops 1500000000 | bytes 10485760 | tf_op jit(solution)/shard_map/gradient_terms/pallas_call | solution.py:194
  56.3 5.8 %all-to-all-start.1 = ((f32[8,88,128]{2,1,0:T(8,128)}), f32[8,88,128]{2,1,0:T(8,128)S(1)}, u32[]{:S(2)}, u32[]{:S(2)}) async-start(f32[8,88,128]{2,1,0:T(8,128)} %pad_maximum_fusion.6), calls=%async_computation.1 | async-start | bytes 720896 | tf_op jit(solution)/shard_map/all_to_all | solution.py:381
  62.2 6.5 %collective-permute-done.4 = bf16[64,640]{1,0:T(8,128)(2,1)S(1)} collective-permute-done((bf16[64,640]{1,0:T(8,128)(2,1)S(1)}, bf16[64,640]{1,0:T(8,128)(2,1)S(1)}, u32[]{:S(2)}, u32[]{:S(2)}) %collective-permute-start.4) | collective-permute-done | bytes 81952 | tf_op jit(solution)/shard_map/ppermute | solution.py:58
  77.7 7.8 %collective-permute-done.7 = bf16[4,64,640]{2,1,0:T(8,128)(2,1)S(1)} collective-permute-done((bf16[4,64,640]{2,1,0:T(8,128)(2,1)S(1)}, bf16[4,64,640]{2,1,0:T(8,128)(2,1)S(1)}, u32[]{:S(2)}, u32[]{:S(2)}) %collective-permute-start.7) | collective-permute-done | bytes 327712 | tf_op jit(solution)/shard_map/ppermute | solution.py:62
  87.7 5.0 %collective-permute-done.8 = bf16[4,64,640]{2,1,0:T(8,128)(2,1)S(1)} collective-permute-done((bf16[4,64,640]{2,1,0:T(8,128)(2,1)S(1)}, bf16[4,64,640]{2,1,0:T(8,128)(2,1)S(1)}, u32[]{:S(2)}, u32[]{:S(2)}) %collective-permute-start.8) | collective-permute-done | bytes 327712 | tf_op jit(solution)/shard_map/ppermute | solution.py:62
  92.6 3.6 %collective-permute-done.9 = bf16[4,64,640]{2,1,0:T(8,128)(2,1)S(1)} collective-permute-done((bf16[4,64,640]{2,1,0:T(8,128)(2,1)S(1)}, bf16[4,64,640]{2,1,0:T(8,128)(2,1)S(1)}, u32[]{:S(2)}, u32[]{:S(2)}) %collective-permute-start.9) | collective-permute-done | bytes 327712 | tf_op jit(solution)/shard_map/ppermute | solution.py:62
  96.8 4.1 %collective-permute-start.11 = (bf16[16,64,640]{2,1,0:T(8,128)(2,1)S(1)}, bf16[16,64,640]{2,1,0:T(8,128)(2,1)}, u32[]{:S(2)}, u32[]{:S(2)}) collective-permute-start(bf16[16,64,640]{2,1,0:T(8,128)(2,1)S(1)} %bitcast.121), channel_id=1, source_target_pairs={{0,2},{2,0},{4,6},{6,4},{1,3},{3,1},{5,7},{7,5},{8,10},{10,8},{12,... | collective-permute-start | bytes 3932168 | tf_op jit(solution)/shard_map/ppermute | solution.py:74
  111.1 14.8 %collective-permute-done.10.rest_1_ = bf16[16,64,640]{2,1,0:T(8,128)(2,1)} collective-permute-done((bf16[16,64,640]{2,1,0:T(8,128)(2,1)S(1)}, bf16[16,64,640]{2,1,0:T(8,128)(2,1)}, u32[]{:S(2)}, u32[]{:S(2)}) %collective-permute-start.10) | collective-permute-done | bytes 1310752 | tf_op jit(solution)/shard_map/ppermute | solution.py:74
  125.9 4.8 %collective-permute-start.14 = (bf16[16,64,640]{2,1,0:T(8,128)(2,1)}, bf16[16,64,640]{2,1,0:T(8,128)(2,1)}, u32[]{:S(2)}, u32[]{:S(2)}) collective-permute-start(bf16[16,64,640]{2,1,0:T(8,128)(2,1)} %collective-permute-done.10.rest_1_), channel_id=1, source_target_pairs={{0,1},{1,0},{2,3},{3,2},{4,5},{5,4},{6,7},{7,6},{8,9},{9,8},{10,11... | collective-permute-start | bytes 3932168 | tf_op jit(solution)/shard_map/ppermute | solution.py:78
  130.8 25.8 %collective-permute-done.11.rest_2_ = bf16[16,64,640]{2,1,0:T(8,128)(2,1)} collective-permute-done((bf16[16,64,640]{2,1,0:T(8,128)(2,1)S(1)}, bf16[16,64,640]{2,1,0:T(8,128)(2,1)}, u32[]{:S(2)}, u32[]{:S(2)}) %collective-permute-start.11) | collective-permute-done | bytes 1310752 | tf_op jit(solution)/shard_map/ppermute | solution.py:74
  162.8 4.9 %convolution_multiply_fusion = f32[256,1536]{1,0:T(8,128)} fusion(bf16[1536,1536]{1,0:T(8,128)(2,1)} %param.16, bf16[256,2176]{1,0:T(8,128)(2,1)S(1)} %copy-done.1), kind=kOutput, calls=%fused_computation.1 | convolution fusion | flops 1208352768 | bytes 7077888 | tf_op jit(solution)/shard_map/dot_general | solution.py:403
  167.7 3.0 %copy.66 = f32[256,1536]{0,1:T(8,128)} copy(f32[256,1536]{1,0:T(8,128)} %convolution_multiply_fusion) | data formatting | bytes 3145728 | tf_op jit(solution)/shard_map/mul | solution.py:403
  178.8 3.3 %collective-permute-done.23.d_ref = f32[704,128]{1,0:T(8,128)S(1)} collective-permute-done((f32[704,128]{1,0:T(8,128)S(1)}, f32[704,128]{1,0:T(8,128)S(1)}, u32[]{:S(2)}, u32[]{:S(2)}) %collective-permute-start.23) | collective-permute-done | bytes 360480 | tf_op jit(solution)/shard_map/ppermute | solution.py:62
  185.7 6.5 %collective-permute-start.24 = (f32[192,384]{1,0:T(8,128)}, f32[192,384]{1,0:T(8,128)S(1)}, u32[]{:S(2)}, u32[]{:S(2)}) collective-permute-start(f32[192,384]{1,0:T(8,128)} %get-tuple-element.21.a_ref), channel_id=1, source_target_pairs={{0,32},{32,64},{64,96},{96,0},{1,33},{33,65},{65,97},{97,1},{2,34}... | collective-permute-start | bytes 884744 | tf_op jit(solution)/shard_map/ppermute | solution.py:66
  196.6 57.9 %attention.1 = (bf16[256,1024]{1,0:T(8,128)(2,1)}, f32[8,128]{1,0:T(8,128)S(1)}) custom-call(s32[2]{0:T(128)S(1)} %broadcast_add_fusion.count_ref, s32[128]{0:T(128)S(1)} %pad_add_fusion.place_ref, s32[64]{0:T(128)S(1)} %iota.57.spos_ref, s32[2]{0:T(128)S(1)} %fusion.14.qpos_ref, bf16[2,1024,640]{2,1,0:T(8,128)(2,1)} %bitcast.130, ...), custom_call_target="tpu_custom_call" | custom-call | flops 20000000000 | bytes 14680064 | tf_op jit(solution)/shard_map/attention/pallas_call | solution.py:149
  255.2 5.3 %all-to-all-start = ((f32[32,8,128]{2,1,0:T(8,128)}), f32[32,8,128]{2,1,0:T(8,128)S(1)}, u32[]{:S(2)}, u32[]{:S(2)}) async-start(f32[32,8,128]{2,1,0:T(8,128)} %broadcast_in_dim.88), calls=%async_computation | async-start | bytes 262144 | tf_op jit(solution)/shard_map/all_to_all | solution.py:433
  260.5 7.6 %all-to-all-done = f32[32,8,128]{2,1,0:T(8,128)S(1)} async-done(((f32[32,8,128]{2,1,0:T(8,128)}), f32[32,8,128]{2,1,0:T(8,128)S(1)}, u32[]{:S(2)}, u32[]{:S(2)}) %all-to-all-start) | async-done | bytes 131104 | tf_op jit(solution)/shard_map/all_to_all | solution.py:433
  269.2 7.1 %newton.1 = f32[8,64,256]{2,1,0:T(8,128)} custom-call(f32[704,128]{1,0:T(8,128)} %get-tuple-element.20.m_ref, f32[192,384]{1,0:T(8,128)} %get-tuple-element.21.a_ref, f32[192,384]{1,0:T(8,128)} %copy-done.22, f32[192,384]{1,0:T(8,128)} %copy-done.23, f32[192,384]{1,0:T(8,128)} %copy-done.24), custom_call_target="tpu_custom_call" | custom-call | flops 1000000000 | bytes 3145728 | tf_op jit(solution)/shard_map/newton/pallas_call | solution.py:291
  276.3 4.8 %all-to-all-start.2 = ((f32[8,64,256]{2,1,0:T(8,128)}), f32[8,64,256]{2,1,0:T(8,128)S(1)}, u32[]{:S(2)}, u32[]{:S(2)}) async-start(f32[8,64,256]{2,1,0:T(8,128)} %newton.1), calls=%async_computation.2 | async-start | bytes 1048576 | tf_op jit(solution)/shard_map/all_to_all | solution.py:395
  281.3 7.2 %all-to-all-done.2 = f32[8,64,256]{2,1,0:T(8,128)S(1)} async-done(((f32[8,64,256]{2,1,0:T(8,128)}), f32[8,64,256]{2,1,0:T(8,128)S(1)}, u32[]{:S(2)}, u32[]{:S(2)}) %all-to-all-start.2) | async-done | bytes 524320 | tf_op jit(solution)/shard_map/all_to_all | solution.py:395
  (159 shorter events, 72.3 us)
Async XLA Ops:
  2.6 13.2 %collective-permute-start.1 = (bf16[64,2176]{1,0:T(8,128)(2,1)S(1)}, bf16[64,2176]{1,0:T(8,128)(2,1)S(1)}, u32[]{:S(2)}, u32[]{:S(2)}) collective-permute-start(bf16[64,2176]{1,0:T(8,128)(2,1)S(1)} %concatenate.37), channel_id=1, source_target_pairs={{0,2},{2,0},{4,6},{6,4},{1,3},{3,1},{5,7},{7,5},{8,10},{10,8},{12,... | collective-permute-start | bytes 835592 | tf_op jit(solution)/shard_map/ppermute | solution.py:74
  3.5 15.2 %collective-permute-start.2 = (bf16[64,2176]{1,0:T(8,128)(2,1)S(1)}, bf16[64,2176]{1,0:T(8,128)(2,1)S(1)}, u32[]{:S(2)}, u32[]{:S(2)}) collective-permute-start(bf16[64,2176]{1,0:T(8,128)(2,1)S(1)} %concatenate.37), channel_id=1, source_target_pairs={{0,6},{2,4},{4,2},{6,0},{1,7},{3,5},{5,3},{7,1},{8,14},{10,12},{12... | collective-permute-start | bytes 835592 | tf_op jit(solution)/shard_map/ppermute | solution.py:74
  22.0 17.4 %collective-permute-start.17 = (bf16[1280,256]{1,0:T(8,128)(2,1)}, bf16[1280,256]{1,0:T(8,128)(2,1)S(1)}, u32[]{:S(2)}, u32[]{:S(2)}) collective-permute-start(bf16[1280,256]{1,0:T(8,128)(2,1)} %pad_maximum_fusion.5), channel_id=1, source_target_pairs={{0,4},{4,0},{1,5},{5,1},{2,6},{6,2},{3,7},{7,3},{8,12},{12,8},{9,1... | collective-permute-start | bytes 1966088 | tf_op jit(solution)/shard_map/ppermute | solution.py:373
  46.6 54.4 %collective-permute-start.18 = (f32[4,704,128]{2,1,0:T(8,128)}, f32[4,704,128]{2,1,0:T(8,128)}, u32[]{:S(2)}, u32[]{:S(2)}) collective-permute-start(f32[4,704,128]{2,1,0:T(8,128)} %get-tuple-element.17), channel_id=1, source_target_pairs={{0,32},{1,9},{8,40},{9,17},{16,48},{17,25},{24,56},{25,1},{32,64},... | collective-permute-start | bytes 4325384 | tf_op jit(solution)/shard_map/ppermute | solution.py:58
  48.6 20.1 %collective-permute-start.4 = (bf16[64,640]{1,0:T(8,128)(2,1)S(1)}, bf16[64,640]{1,0:T(8,128)(2,1)S(1)}, u32[]{:S(2)}, u32[]{:S(2)}) collective-permute-start(bf16[64,640]{1,0:T(8,128)(2,1)S(1)} %get-tuple-element.47), channel_id=1, source_target_pairs={{0,32},{1,9},{8,40},{9,17},{16,48},{17,25},{24,56},{25,1},{32,64},... | collective-permute-start | bytes 245768 | tf_op jit(solution)/shard_map/ppermute | solution.py:58
  50.5 20.5 %collective-permute-start.5 = (bf16[64,640]{1,0:T(8,128)(2,1)S(1)}, bf16[64,640]{1,0:T(8,128)(2,1)S(1)}, u32[]{:S(2)}, u32[]{:S(2)}) collective-permute-start(bf16[64,640]{1,0:T(8,128)(2,1)S(1)} %get-tuple-element.47), channel_id=1, source_target_pairs={{0,64},{1,17},{8,72},{9,25},{16,80},{17,1},{24,88},{25,9},{32,96},... | collective-permute-start | bytes 245768 | tf_op jit(solution)/shard_map/ppermute | solution.py:58
  52.2 18.8 %collective-permute-start.6 = (bf16[64,640]{1,0:T(8,128)(2,1)S(1)}, bf16[64,640]{1,0:T(8,128)(2,1)S(1)}, u32[]{:S(2)}, u32[]{:S(2)}) collective-permute-start(bf16[64,640]{1,0:T(8,128)(2,1)S(1)} %get-tuple-element.47), channel_id=1, source_target_pairs={{0,96},{1,25},{8,104},{9,1},{16,112},{17,9},{24,120},{25,17},{32,0... | collective-permute-start | bytes 245768 | tf_op jit(solution)/shard_map/ppermute | solution.py:58
  56.3 51.9 %all-to-all-start.1 = ((f32[8,88,128]{2,1,0:T(8,128)}), f32[8,88,128]{2,1,0:T(8,128)S(1)}, u32[]{:S(2)}, u32[]{:S(2)}) async-start(f32[8,88,128]{2,1,0:T(8,128)} %pad_maximum_fusion.6), calls=%async_computation.1 | async-start | bytes 720896 | tf_op jit(solution)/shard_map/all_to_all | solution.py:381
  62.1 39.2 %collective-permute-start.19 = (f32[4,704,128]{2,1,0:T(8,128)}, f32[4,704,128]{2,1,0:T(8,128)S(1)}, u32[]{:S(2)}, u32[]{:S(2)}) collective-permute-start(f32[4,704,128]{2,1,0:T(8,128)} %get-tuple-element.18), channel_id=1, source_target_pairs={{0,64},{1,17},{8,72},{9,25},{16,80},{17,1},{24,88},{25,9},{32,96},... | collective-permute-start | bytes 4325384 | tf_op jit(solution)/shard_map/ppermute | solution.py:58
  68.6 34.1 %collective-permute-start.20 = (f32[4,704,128]{2,1,0:T(8,128)}, f32[4,704,128]{2,1,0:T(8,128)S(1)}, u32[]{:S(2)}, u32[]{:S(2)}) collective-permute-start(f32[4,704,128]{2,1,0:T(8,128)} %get-tuple-element.19), channel_id=1, source_target_pairs={{0,96},{1,25},{8,104},{9,1},{16,112},{17,9},{24,120},{25,17},{32,0... | collective-permute-start | bytes 4325384 | tf_op jit(solution)/shard_map/ppermute | solution.py:58
  72.7 12.9 %collective-permute-start.7 = (bf16[4,64,640]{2,1,0:T(8,128)(2,1)S(1)}, bf16[4,64,640]{2,1,0:T(8,128)(2,1)S(1)}, u32[]{:S(2)}, u32[]{:S(2)}) collective-permute-start(bf16[4,64,640]{2,1,0:T(8,128)(2,1)S(1)} %get-tuple-element.45), channel_id=1, source_target_pairs={{0,8},{1,33},{8,16},{9,41},{16,24},{17,49},{24,0},{25,57},{32,40},... | collective-permute-start | bytes 983048 | tf_op jit(solution)/shard_map/ppermute | solution.py:62
  75.0 17.6 %collective-permute-start.8 = (bf16[4,64,640]{2,1,0:T(8,128)(2,1)S(1)}, bf16[4,64,640]{2,1,0:T(8,128)(2,1)S(1)}, u32[]{:S(2)}, u32[]{:S(2)}) collective-permute-start(bf16[4,64,640]{2,1,0:T(8,128)(2,1)S(1)} %get-tuple-element.45), channel_id=1, source_target_pairs={{0,16},{1,65},{8,24},{9,73},{16,0},{17,81},{24,8},{25,89},{32,48},... | collective-permute-start | bytes 983048 | tf_op jit(solution)/shard_map/ppermute | solution.py:62
  96.4 29.5 %collective-permute-start.10 = (bf16[16,64,640]{2,1,0:T(8,128)(2,1)S(1)}, bf16[16,64,640]{2,1,0:T(8,128)(2,1)}, u32[]{:S(2)}, u32[]{:S(2)}) collective-permute-start(bf16[16,64,640]{2,1,0:T(8,128)(2,1)S(1)} %bitcast.120), channel_id=1, source_target_pairs={{0,4},{2,6},{4,0},{6,2},{1,5},{3,7},{5,1},{7,3},{8,12},{10,14},{12... | collective-permute-start | bytes 3932168 | tf_op jit(solution)/shard_map/ppermute | solution.py:74
  96.8 59.7 %collective-permute-start.11 = (bf16[16,64,640]{2,1,0:T(8,128)(2,1)S(1)}, bf16[16,64,640]{2,1,0:T(8,128)(2,1)}, u32[]{:S(2)}, u32[]{:S(2)}) collective-permute-start(bf16[16,64,640]{2,1,0:T(8,128)(2,1)S(1)} %bitcast.121), channel_id=1, source_target_pairs={{0,2},{2,0},{4,6},{6,4},{1,3},{3,1},{5,7},{7,5},{8,10},{10,8},{12,... | collective-permute-start | bytes 3932168 | tf_op jit(solution)/shard_map/ppermute | solution.py:74
  100.9 59.3 %collective-permute-start.12 = (bf16[16,64,640]{2,1,0:T(8,128)(2,1)S(1)}, bf16[16,64,640]{2,1,0:T(8,128)(2,1)}, u32[]{:S(2)}, u32[]{:S(2)}) collective-permute-start(bf16[16,64,640]{2,1,0:T(8,128)(2,1)S(1)} %bitcast.122), channel_id=1, source_target_pairs={{0,6},{2,4},{4,2},{6,0},{1,7},{3,5},{5,3},{7,1},{8,14},{10,12},{12... | collective-permute-start | bytes 3932168 | tf_op jit(solution)/shard_map/ppermute | solution.py:74
  105.4 56.5 %collective-permute-start.21 = (f32[704,128]{1,0:T(8,128)}, f32[704,128]{1,0:T(8,128)}, u32[]{:S(2)}, u32[]{:S(2)}) collective-permute-start(f32[704,128]{1,0:T(8,128)} %get-tuple-element.28), channel_id=1, source_target_pairs={{0,8},{1,33},{8,16},{9,41},{16,24},{17,49},{24,0},{25,57},{32,40},... | collective-permute-start | bytes 1081352 | tf_op jit(solution)/shard_map/ppermute | solution.py:62
  109.4 82.7 %collective-permute-start.13 = (bf16[16,64,640]{2,1,0:T(8,128)(2,1)S(1)}, bf16[16,64,640]{2,1,0:T(8,128)(2,1)}, u32[]{:S(2)}, u32[]{:S(2)}) collective-permute-start(bf16[16,64,640]{2,1,0:T(8,128)(2,1)S(1)} %bitcast.123), channel_id=1, source_target_pairs={{0,1},{1,0},{2,3},{3,2},{4,5},{5,4},{6,7},{7,6},{8,9},{9,8},{10,11... | collective-permute-start | bytes 3932168 | tf_op jit(solution)/shard_map/ppermute | solution.py:78
  125.9 68.1 %collective-permute-start.14 = (bf16[16,64,640]{2,1,0:T(8,128)(2,1)}, bf16[16,64,640]{2,1,0:T(8,128)(2,1)}, u32[]{:S(2)}, u32[]{:S(2)}) collective-permute-start(bf16[16,64,640]{2,1,0:T(8,128)(2,1)} %collective-permute-done.10.rest_1_), channel_id=1, source_target_pairs={{0,1},{1,0},{2,3},{3,2},{4,5},{5,4},{6,7},{7,6},{8,9},{9,8},{10,11... | collective-permute-start | bytes 3932168 | tf_op jit(solution)/shard_map/ppermute | solution.py:78
  156.5 40.1 %collective-permute-start.15 = (bf16[16,64,640]{2,1,0:T(8,128)(2,1)}, bf16[16,64,640]{2,1,0:T(8,128)(2,1)}, u32[]{:S(2)}, u32[]{:S(2)}) collective-permute-start(bf16[16,64,640]{2,1,0:T(8,128)(2,1)} %collective-permute-done.11.rest_2_), channel_id=1, source_target_pairs={{0,1},{1,0},{2,3},{3,2},{4,5},{5,4},{6,7},{7,6},{8,9},{9,8},{10,11... | collective-permute-start | bytes 3932168 | tf_op jit(solution)/shard_map/ppermute | solution.py:78
  160.2 36.4 %collective-permute-start.16 = (bf16[16,64,640]{2,1,0:T(8,128)(2,1)}, bf16[16,64,640]{2,1,0:T(8,128)(2,1)}, u32[]{:S(2)}, u32[]{:S(2)}) collective-permute-start(bf16[16,64,640]{2,1,0:T(8,128)(2,1)} %collective-permute-done.12.rest_3_), channel_id=1, source_target_pairs={{0,1},{1,0},{2,3},{3,2},{4,5},{5,4},{6,7},{7,6},{8,9},{9,8},{10,11... | collective-permute-start | bytes 3932168 | tf_op jit(solution)/shard_map/ppermute | solution.py:78
  185.7 82.5 %collective-permute-start.24 = (f32[192,384]{1,0:T(8,128)}, f32[192,384]{1,0:T(8,128)S(1)}, u32[]{:S(2)}, u32[]{:S(2)}) collective-permute-start(f32[192,384]{1,0:T(8,128)} %get-tuple-element.21.a_ref), channel_id=1, source_target_pairs={{0,32},{32,64},{64,96},{96,0},{1,33},{33,65},{65,97},{97,1},{2,34}... | collective-permute-start | bytes 884744 | tf_op jit(solution)/shard_map/ppermute | solution.py:66
  192.2 76.1 %collective-permute-start.25 = (f32[192,384]{1,0:T(8,128)}, f32[192,384]{1,0:T(8,128)S(1)}, u32[]{:S(2)}, u32[]{:S(2)}) collective-permute-start(f32[192,384]{1,0:T(8,128)} %get-tuple-element.21.a_ref), channel_id=1, source_target_pairs={{0,64},{32,96},{64,0},{96,32},{1,65},{33,97},{65,1},{97,33},{2,66}... | collective-permute-start | bytes 884744 | tf_op jit(solution)/shard_map/ppermute | solution.py:66
  194.0 74.2 %collective-permute-start.26 = (f32[192,384]{1,0:T(8,128)}, f32[192,384]{1,0:T(8,128)S(1)}, u32[]{:S(2)}, u32[]{:S(2)}) collective-permute-start(f32[192,384]{1,0:T(8,128)} %get-tuple-element.21.a_ref), channel_id=1, source_target_pairs={{0,96},{32,0},{64,32},{96,64},{1,97},{33,1},{65,33},{97,65},{2,98}... | collective-permute-start | bytes 884744 | tf_op jit(solution)/shard_map/ppermute | solution.py:66
  255.2 12.9 %all-to-all-start = ((f32[32,8,128]{2,1,0:T(8,128)}), f32[32,8,128]{2,1,0:T(8,128)S(1)}, u32[]{:S(2)}, u32[]{:S(2)}) async-start(f32[32,8,128]{2,1,0:T(8,128)} %broadcast_in_dim.88), calls=%async_computation | async-start | bytes 262144 | tf_op jit(solution)/shard_map/all_to_all | solution.py:433
  (31 other events, 280.4 us)

commit v2 on v1

v2 whole, which is shorter than its diff:
```python
import functools
import math

import jax
import jax.numpy as jnp
from jax import lax
from jax.experimental import pallas as pl
from jax.experimental.pallas import tpu as pltpu
from jax.sharding import Mesh
from jax.sharding import PartitionSpec as P

QR = 1536
KVR = 512
NOPE = 128
ROPE = 64
WIDE = 640
NS_STEPS = 3
NS_A = 3.4445
NS_B = -4.775
NS_C = 2.0315
MOMENTUM = 0.95
LEARN_RATE = 0.05
DECAY = 0.1
CLIP_TAU = 6.0
ROPE_THETA = 50000.0
HEAD = NOPE + ROPE
SCALE = HEAD ** (-0.5)
LOG2E = math.log2(math.e)
FULL = lax.Precision.HIGHEST
F32 = jnp.float32
BF16 = jnp.bfloat16
LOW = -1e30
ANY = pl.BlockSpec(memory_space=pl.ANY)
VMEM = pl.BlockSpec(memory_space=pltpu.VMEM)
SMEM = pl.BlockSpec(memory_space=pltpu.SMEM)
TILE = 512


def place_of(z, x, c):
    return (z * 4 + x) * 2 + c


FOUR = range(4)
ALONG_Z = [[[place_of(z, x, c) for z in FOUR] for x in FOUR] for c in range(2)]
ALONG_X = [[[place_of(z, x, c) for x in FOUR] for z in FOUR] for c in range(2)]
FIRST = ALONG_Z[0] + ALONG_X[1]
SECOND = ALONG_X[0] + ALONG_Z[1]


def exchange(value, groups):
    return lax.all_to_all(value, ("z", "x", "c"), 0, 0, axis_index_groups=groups)


def move_z(value, k):
    return lax.ppermute(value, "z", [(i, (i + k) % 4) for i in range(4)])


def flip(value, k):
    pairs = []
    for yl in range(2):
        for yh in range(2):
            pairs.append((yl * 2 + yh, (yl ^ (k & 1)) * 2 + (yh ^ (k >> 1))))
    return lax.ppermute(value, ("yl", "yh"), pairs)


def swap_core(value):
    return lax.ppermute(value, "c", [(0, 1), (1, 0)])


def attention_kernel(head0, heads, count, *refs):
    place_ref, core_ref, qpos_ref, q_ref, wv_ref = refs[:5]
    pieces = refs[5 : 5 + count]
    out_ref, peak_ref, acc, top, total, keys, sem = refs[-7:]
    width = heads * 128
    slot = 0
    for index, piece in enumerate(pieces):
        side = 0 if index < count // 2 else 1
        if index == count // 2:
            slot = 0

        @pl.loop(0, piece.shape[0])
        def _(s, piece=piece, side=side, slot=slot):
            row = pl.multiple_of(place_ref[slot + s] * 128 + core_ref[side], 64)
            pltpu.make_async_copy(piece.at[s], keys.at[pl.ds(row, 64)], sem).start()

        slot += piece.shape[0]
    pltpu.make_async_copy(keys, keys, sem).wait()
    factor = SCALE * LOG2E
    for half in range(2):
        acc[...] = jnp.zeros(acc.shape, F32)
        top[...] = jnp.full(top.shape, LOW, F32)
        total[...] = jnp.zeros(total.shape, F32)
        tiles = lax.div(qpos_ref[half] + 4, 4)

        def tile(j, masked, half=half):
            row0 = pl.multiple_of(j * TILE, TILE)
            k = keys[pl.ds(row0, TILE), :]
            s = lax.dot_general(
                q_ref[half, head0 * 128 : head0 * 128 + width, :],
                k,
                (((1,), (1,)), ((), ())),
                preferred_element_type=F32,
            )
            s = [s[:, b * 128 : (b + 1) * 128] for b in range(4)]
            if masked:
                row_pos = qpos_ref[half] * 128 + (
                    lax.broadcasted_iota(jnp.int32, (width, 128), 0) & 127
                )
                col = lax.broadcasted_iota(jnp.int32, (width, 128), 1)
                s = [
                    jnp.where((j * 4 + b) * 128 + col <= row_pos, s[b], LOW) for b in range(4)
                ]
            old = top[...]
            peak = jnp.maximum(jnp.maximum(s[0], s[1]), jnp.maximum(s[2], s[3]))
            new = jnp.maximum(old, jnp.max(peak, axis=1, keepdims=True))
            p = [jnp.exp2((part - new) * factor) for part in s]
            keep = jnp.exp2((old - new) * factor)
            top[...] = new
            total[...] = total[...] * keep + ((p[0] + p[1]) + (p[2] + p[3]))
            weights = jnp.concatenate(p, axis=1).astype(BF16)
            acc[...] = acc[...] * jnp.concatenate([keep] * 4, axis=1) + jnp.dot(
                weights, k[:, :KVR], preferred_element_type=F32
            )

        @pl.loop(0, tiles - 1)
        def _(j):
            tile(j, False)

        tile(tiles - 1, True)
        for h in range(heads):
            rows = pl.ds(h * 128, 128)
            latent = acc[rows, :] / jnp.sum(total[rows, :], axis=1, keepdims=True)
            first = (head0 + h) * 128
            o = jnp.dot(
                latent.astype(BF16), wv_ref[:, first : first + 128], preferred_element_type=F32
            )
            out_ref[half * 128 : (half + 1) * 128, h * 128 : (h + 1) * 128] = (
                o * KVR ** (-0.5)
            ).astype(BF16)
            peak = jnp.max(top[rows, :], axis=0, keepdims=True) * SCALE
            if half == 0:
                peak_ref[h : h + 1, :] = peak
            else:
                peak_ref[h : h + 1, :] = jnp.maximum(peak_ref[h : h + 1, :], peak)


def attention(head0, heads, place, core_rows, qpos, queries, w_value, pieces, ties):
    width = heads * 128
    return pl.pallas_call(
        functools.partial(attention_kernel, head0, heads, len(pieces)),
        out_shape=(
            jax.ShapeDtypeStruct((256, width), BF16),
            jax.ShapeDtypeStruct((heads, 128), F32),
        ),
        in_specs=[SMEM] * 3 + [VMEM] * 2 + [ANY] * (len(pieces) + len(ties)),
        out_specs=(VMEM, VMEM),
        scratch_shapes=[
            pltpu.VMEM((width, KVR), F32),
            pltpu.VMEM((width, 128), F32),
            pltpu.VMEM((width, 128), F32),
            pltpu.VMEM((8192, WIDE), BF16),
            pltpu.SemaphoreType.DMA,
        ],
        compiler_params=pltpu.CompilerParams(vmem_limit_bytes=52 * 2**20),
        cost_estimate=pl.CostEstimate(
            flops=20 * heads // 8 * 10**9,
            bytes_accessed=14 * 2**20,
            transcendentals=heads * 10**6,
        ),
        name="attention",
    )(place, core_rows, qpos, queries, w_value, *pieces, *ties)


def query_kernel(l_ref, wq_ref, wk_ref, cos_ref, low_ref, high_ref, out_ref):
    for pair in range(4):
        both = (
            jnp.dot(
                l_ref[:, :QR],
                wq_ref[:, pair * 384 : (pair + 1) * 384],
                preferred_element_type=F32,
            )
            * QR ** (-0.5)
        )
        for odd in range(2):
            q = pltpu.roll(both, HEAD, 1) if odd else both
            h = 2 * pair + odd
            nope = q[:, :NOPE].astype(BF16)
            turn = q[:, NOPE : 2 * NOPE]
            turned = (
                turn * cos_ref[...]
                + pltpu.roll(turn, 96, 1) * low_ref[...]
                + pltpu.roll(turn, 32, 1) * high_ref[...]
            ).astype(BF16)
            absorbed = (
                lax.dot_general(
                    nope,
                    wk_ref[:, h * NOPE : (h + 1) * NOPE],
                    (((1,), (1,)), ((), ())),
                    preferred_element_type=F32,
                )
                * KVR ** (-0.5)
            ).astype(BF16)
            for half in range(2):
                rows = slice(half * 128, (half + 1) * 128)
                out_ref[half, h * 128 : (h + 1) * 128, :KVR] = absorbed[rows]
                out_ref[half, h * 128 : (h + 1) * 128, KVR:] = turned[rows]


def project_queries(l_own, w_query, w_key, cosine, low, high):
    return pl.pallas_call(
        query_kernel,
        out_shape=jax.ShapeDtypeStruct((2, 1024, WIDE), BF16),
        in_specs=[VMEM] * 6,
        out_specs=VMEM,
        compiler_params=pltpu.CompilerParams(vmem_limit_bytes=32 * 2**20),
        cost_estimate=pl.CostEstimate(flops=1000, bytes_accessed=1000, transcendentals=0),
        name="queries",
    )(l_own, w_query, w_key, cosine, low, high)


def gradient_kernel(at_ref, gq_ref, gk_ref, g_other, mq_ref, mk_ref, m_other, *rest):
    shards_own, shards_swapped = rest[:4], rest[4:8]
    out_ref, l_own, l_other, gq_t, gk_t, mq_t, mk_t = rest[-7:]
    core, z, x, yl, yh = (at_ref[i] for i in range(5))
    for k in range(4):
        target = l_other if k & 1 else l_own
        block = jnp.bitwise_xor(yh, k >> 1) * 128
        for side, shard in ((core, shards_own[k]), (1 - core, shards_swapped[k])):
            target[pl.ds(pl.multiple_of(block + side * 64, 64), 64), :] = shard[...]
    wide_q = pl.ds(pl.multiple_of(yl * 768, 128), 768)
    wide_k = pl.ds(pl.multiple_of(yl * 512, 128), 512)
    gq_t[0] = gq_ref[:, wide_q].T
    gk_t[0] = gk_ref[:, wide_k].T
    gq_t[1] = g_other[:, :768].T
    gk_t[1] = g_other[:, 768:].T

    def spread(own, other):
        low = jnp.where(yl == 0, own, other)
        high = jnp.where(yl == 0, other, own)
        pair = jnp.concatenate([low, high], axis=0)
        rows = [jnp.where(x == i, MOMENTUM, 0.0) * pair for i in range(4)]
        return jnp.concatenate(rows, axis=0).T

    mq_t[...] = spread(mq_ref[:, wide_q], m_other[:48, :])
    mk_t[...] = spread(mk_ref[:, wide_k], m_other[48:, :512])
    for zb in range(4):
        mine = jnp.where(z == zb, 1.0, 0.0)

        def block(g, cols):
            return jnp.dot(g[0], l_own[:, cols], preferred_element_type=F32) + jnp.dot(
                g[1], l_other[:, cols], preferred_element_type=F32
            )

        m = block(gq_t, slice(zb * 384, (zb + 1) * 384)) + mine * mq_t[...]
        mk = block(gk_t, slice(QR + zb * 128, QR + (zb + 1) * 128)) + mine * mk_t[...]
        for xb in range(4):
            k = jnp.where(core == 0, zb, xb)
            j = jnp.where(core == 0, xb, zb)
            for t in range(3):
                out_ref[k, j, t * HEAD : (t + 1) * HEAD, :] = m[
                    xb * HEAD : (xb + 1) * HEAD, t * 128 : (t + 1) * 128
                ]
            out_ref[k, j, 3 * HEAD : 704, :] = mk[xb * 128 : (xb + 1) * 128, :]


def gradient_terms(at, grad_query, grad_key, g_other, mom_query, mom_key, m_other, shards, ties):
    return pl.pallas_call(
        gradient_kernel,
        out_shape=(
            jax.ShapeDtypeStruct((4, 4, 704, 128), F32),
            jax.ShapeDtypeStruct((256, QR + WIDE), BF16),
        ),
        in_specs=[SMEM] + [VMEM] * 14 + [ANY] * len(ties),
        out_specs=(VMEM, VMEM),
        scratch_shapes=[
            pltpu.VMEM((256, QR + WIDE), BF16),
            pltpu.VMEM((2, 768, 256), BF16),
            pltpu.VMEM((2, 512, 256), BF16),
            pltpu.VMEM((768, 384), F32),
            pltpu.VMEM((512, 128), F32),
        ],
        compiler_params=pltpu.CompilerParams(vmem_limit_bytes=32 * 2**20),
        cost_estimate=pl.CostEstimate(flops=1000, bytes_accessed=1000, transcendentals=0),
        name="gradient_terms",
    )(at, grad_query, grad_key, g_other, mom_query, mom_key, m_other, *shards, *ties)


def sum_kernel(a_ref, *rest):
    rest[-1][0] = (a_ref[0, 0] + a_ref[1, 0]) + (a_ref[2, 0] + a_ref[3, 0])


def sum_first(terms, ties):
    return pl.pallas_call(
        sum_kernel,
        grid=(4,),
        out_shape=jax.ShapeDtypeStruct((4, 704, 128), F32),
        in_specs=[pl.BlockSpec((4, 1, 704, 128), lambda j: (0, j, 0, 0))] + [ANY] * len(ties),
        out_specs=pl.BlockSpec((1, 704, 128), lambda j: (j, 0, 0)),
        compiler_params=pltpu.CompilerParams(vmem_limit_bytes=16 * 2**20),
        cost_estimate=pl.CostEstimate(flops=1000, bytes_accessed=1000, transcendentals=0),
        name="sum_first",
    )(terms, *ties)


def nt(a, b):
    return lax.dot_general(
        a, b, (((1,), (1,)), ((), ())), precision=FULL, preferred_element_type=F32
    )


def gram_kernel(p_ref, peak_ref, m_ref, g_ref):
    m_ref[...] = (p_ref[0] + p_ref[1]) + (p_ref[2] + p_ref[3])
    g_ref[...] = jnp.zeros(g_ref.shape, F32)
    gram = None
    for t in range(3):
        block = m_ref[t * HEAD : (t + 1) * HEAD, :]
        term = nt(block, block)
        gram = term if gram is None else gram + term
    g_ref[:, :HEAD] = gram
    block = m_ref[3 * HEAD : 704, :]
    g_ref[:128, 256:384] = nt(block, block)
    g_ref[128:136, 256:384] = peak_ref[...]


def moment_and_gram(parts, peaks):
    return pl.pallas_call(
        gram_kernel,
        out_shape=(
            jax.ShapeDtypeStruct((704, 128), F32),
            jax.ShapeDtypeStruct((HEAD, 384), F32),
        ),
        in_specs=[VMEM, VMEM],
        out_specs=(VMEM, VMEM),
        cost_estimate=pl.CostEstimate(flops=1000, bytes_accessed=1000, transcendentals=0),
        name="moment_and_gram",
    )(parts, peaks)


def full_dot(a, b):
    return jnp.dot(a, b, precision=FULL, preferred_element_type=F32)


def newton_factor(gram):
    size = gram.shape[0]
    eye = (
        lax.broadcasted_iota(jnp.int32, (size, size), 0)
        == lax.broadcasted_iota(jnp.int32, (size, size), 1)
    ).astype(F32)
    square = jnp.sum(jnp.sum(gram * eye, axis=1, keepdims=True), axis=0, keepdims=True)
    inverse = 1.0 / (jnp.sqrt(square) + 1e-07)
    a = gram * inverse * inverse
    product = None
    for step in range(NS_STEPS):
        factor = NS_A * eye + NS_B * a + NS_C * full_dot(a, a)
        product = factor if product is None else full_dot(product, factor)
        if step + 1 < NS_STEPS:
            a = full_dot(full_dot(factor, a), factor)
    return product * inverse


def newton_kernel(m_ref, a_ref, b_ref, c_ref, d_ref, *rest):
    out_ref = rest[-1]
    spot = (slice(128, 136), slice(256, 384))
    peaks = jnp.maximum(
        jnp.maximum(a_ref[spot], b_ref[spot]), jnp.maximum(c_ref[spot], d_ref[spot])
    )
    gram = (a_ref[...] + b_ref[...]) + (c_ref[...] + d_ref[...])
    factor_q = newton_factor(gram[:, :HEAD]) * (0.2 * math.sqrt(QR))
    factor_k = newton_factor(gram[:128, 256:384]) * (0.2 * math.sqrt(KVR))
    rows = []
    for t in range(3):
        block = m_ref[t * HEAD : (t + 1) * HEAD, :]
        rows.append(
            lax.dot_general(
                block, factor_q, (((0,), (0,)), ((), ())), precision=FULL, preferred_element_type=F32
            )
        )
    step = jnp.concatenate(rows, axis=0)
    step_k = lax.dot_general(
        m_ref[3 * HEAD : 704, :],
        factor_k,
        (((0,), (0,)), ((), ())),
        precision=FULL,
        preferred_element_type=F32,
    )
    out_ref[...] = jnp.zeros(out_ref.shape, F32)
    for i in range(8):
        out_ref[i, :48, :HEAD] = step[i * 48 : (i + 1) * 48, :]
        out_ref[i, 48:, :128] = step_k[i * 16 : (i + 1) * 16, :]
        out_ref[i, 48:56, 128:] = peaks


def newton(moment, grams, ties):
    return pl.pallas_call(
        newton_kernel,
        out_shape=jax.ShapeDtypeStruct((8, 64, 256), F32),
        in_specs=[VMEM] * 5 + [ANY] * len(ties),
        out_specs=VMEM,
        cost_estimate=pl.CostEstimate(flops=1000, bytes_accessed=1000, transcendentals=0),
        name="newton",
    )(moment, *grams, *ties)


def turn_tables(positions):
    frequency = ROPE_THETA ** (-2.0 * jnp.arange(ROPE // 2, dtype=F32) / ROPE)
    angles = positions.astype(F32)[:, None] * frequency[None, :]
    cosine, sine = jnp.cos(angles), jnp.sin(angles)
    none = jnp.zeros_like(cosine)
    return (
        jnp.concatenate([cosine, cosine, none, none], axis=1),
        jnp.concatenate([-sine, none, none, none], axis=1),
        jnp.concatenate([none, sine, none, none], axis=1),
    )


def look_up(table, index):
    hit = index[:, None] == jnp.arange(table.shape[0], dtype=jnp.int32)[None, :]
    return jnp.sum(jnp.where(hit, table[None, :], 0), axis=1)


def shards(
    q_latent,
    kv_latent,
    key_rope,
    block_order,
    w_query,
    w_key,
    w_value,
    grad_query,
    grad_key,
    mom_query,
    mom_key,
    clip_flags,
):
    z, x, c = lax.axis_index("z"), lax.axis_index("x"), lax.axis_index("c")
    yl, yh = lax.axis_index("yl"), lax.axis_index("yh")
    ctx = z * 8 + x * 2 + yl
    rows_in = jnp.concatenate(
        [q_latent, kv_latent, key_rope, jnp.zeros((64, 64), BF16)], axis=1
    )
    key_rows = rows_in[:, QR:]
    flips = [rows_in] + [flip(rows_in, k) for k in (1, 2, 3)]
    swapped = [swap_core(piece) for piece in flips]

    def other_half(first, second):
        def pick(array):
            width = array.shape[1] // 2
            return jnp.where(yl == 0, array[:, width:], array[:, :width])

        return pick(first), pick(second)

    g_other = jnp.concatenate(other_half(grad_query, grad_key), axis=1)
    g_other = lax.ppermute(g_other, "yl", [(0, 1), (1, 0)])
    mom_q, mom_k = other_half(mom_query, mom_key)
    m_other = jnp.concatenate([mom_q, jnp.pad(mom_k, ((0, 0), (0, 256)))], axis=0)
    m_other = lax.ppermute(m_other, "yl", [(0, 1), (1, 0)])
    plane = lax.all_to_all(
        jnp.broadcast_to(key_rows[None], (16, 64, WIDE)), ("z", "x"), 0, 0
    )
    at = jnp.stack([c, z, x, yl, yh]).astype(jnp.int32)
    terms, l_own = gradient_terms(
        at, grad_query, grad_key, g_other, mom_query, mom_key, m_other, flips + swapped, [plane]
    )
    terms = exchange(terms, FIRST)
    near = [flip(plane, k) for k in (1, 3)]
    local_rows = jnp.arange(256, dtype=jnp.int32)
    qpos = look_up(block_order, 2 * ctx + jnp.arange(2, dtype=jnp.int32))
    query_pos = jnp.where(local_rows < 128, qpos[0], qpos[1]) * 128 + local_rows % 128
    wide = project_queries(l_own, w_query, w_key, *turn_tables(query_pos))
    after = wide[0, 0, WIDE - 1]
    far = [flip(near[1][:8] + after, 1), flip(near[0][8:] + after, 3)]
    slot = jnp.arange(16, dtype=jnp.int32)
    place = jnp.concatenate(
        [
            look_up(
                block_order,
                2 * (slot // 4 * 8 + slot % 4 * 2 + (yl ^ (k & 1))) + (yh ^ (k >> 1)),
            )
            for k in (0, 1, 3, 2)
        ]
    )
    core_rows = jnp.stack([c * 64, 64 - c * 64]).astype(jnp.int32)

    terms = sum_first(terms, [wide])
    later = (terms[0, 0, 0] * 0).astype(BF16)
    far = [piece + later for piece in far]
    mine = [plane, *near, *far]
    pieces = mine + [swap_core(piece) for piece in mine]
    parts = exchange(terms, SECOND)
    attn_out, peaks = attention(
        0, 8, place, core_rows, qpos, wide, w_value, pieces, []
    )
    moment, gram = moment_and_gram(parts, peaks)
    grams = [gram] + [move_z(gram, k) for k in (1, 2, 3)]
    steps = newton(moment, grams, [])
    steps = lax.all_to_all(steps, ("x", "yl"), 0, 0)
    step_query = (
        steps[:, :48, :HEAD].reshape(4, 2, 48, HEAD).transpose(2, 1, 0, 3).reshape(48, QR)
    )
    step_key = steps[:, 48:, :128].reshape(4, 2, 16, 128).transpose(2, 1, 0, 3).reshape(16, 1024)
    head_peaks = jnp.max(steps[:, 48:56, 128], axis=0)
    clip_gamma = jnp.where(clip_flags > 0, CLIP_TAU / jnp.maximum(head_peaks, CLIP_TAU), 1.0)
    root_gamma = jnp.sqrt(clip_gamma)
    query_factor = jnp.concatenate(
        [
            jnp.broadcast_to(root_gamma[:, None], (8, NOPE)),
            jnp.broadcast_to(clip_gamma[:, None], (8, ROPE)),
        ],
        axis=1,
    ).reshape(-1)
    key_factor = jnp.repeat(root_gamma, NOPE)
    owned_query = lax.dynamic_slice_in_dim(w_query, ctx * 48, 48, 0).astype(F32)
    owned_key = lax.dynamic_slice_in_dim(w_key, ctx * 16, 16, 0).astype(F32)
    keep = 1.0 - LEARN_RATE * DECAY
    new_query = (owned_query * keep - LEARN_RATE * step_query) * query_factor[None, :]
    new_key = (owned_key * keep - LEARN_RATE * step_key) * key_factor[None, :]
    return (attn_out, head_peaks, step_query, step_key, new_query, new_key)


def solution(mesh):
    fine = Mesh(mesh.devices.reshape(4, 4, 2, 2, 2), ("z", "x", "yl", "yh", "c"))
    ctx, dp = ("z", "x", "yl"), ("yh", "c")
    tokens = P(ctx + dp, None)
    columns = P(None, dp)
    both = P(ctx, dp)
    in_specs = (
        tokens,
        tokens,
        tokens,
        P(),
        columns,
        columns,
        columns,
        both,
        both,
        both,
        both,
        P(dp),
    )
    out_specs = (both, P(dp), both, both, both, both)
    return jax.shard_map(shards, mesh=fine, in_specs=in_specs, out_specs=out_specs, check_vma=False)
```

time: 293 us -> 201 us (0.69)
  waiting for transfers between devices: 112 us -> 69.2 us
  starting transfers between devices: 65.4 us -> 39.4 us
  Pallas kernels: 75 us -> 57.3 us
  matrix products: 7.26 us -> 0 us
  other arithmetic: 18.3 us -> 14.4 us
  local copies, waits for them, and re-layouts: 13.7 us -> 16.7 us
    ppermute x6 -> x7, waiting for transfers between devices: 54.1 us -> 29.2 us  [flip(): return lax.ppermute(value, ('yl', 'yh'), pairs)]
    ppermute x13 -> x2, waiting for transfers between devices: 41.8 us -> 17.6 us  [the longest x1 17.6 us: shards(): m_other = lax.ppermute(m_other, 'yl', [(0, 1), (1, 0)])]
    pallas_call x2 -> x4, Pallas kernels: 65 us -> 47.4 us  [the longest x1 37.5 us: attention(): pl.pallas_call(functools.partial(attention_kernel, head0, heads, len(piec...]
    ppermute x13 -> x2, starting transfers between devices: 18.8 us -> 2.09 us  [the longest x1 2.09 us: shards(): m_other = lax.ppermute(m_other, 'yl', [(0, 1), (1, 0)])]
    ppermute x3, waiting for transfers between devices: 0.01 us -> 12.3 us  [move_z(): return lax.ppermute(value, 'z', [(i, (i + k) % 4) for i in range(4)])]
    unnamed x53 -> x44, local copies, waits for them, and re-layouts: 3.23 us -> 11.4 us
    ppermute x5 -> x9, starting transfers between devices: 10.3 us -> 2.53 us  [swap_core(): return lax.ppermute(value, 'c', [(0, 1), (1, 0)])]
    all_to_all x2 -> x3, waiting for transfers between devices: 7.59 us -> 0.01 us  [the longest x2 0.01 us: exchange(): lax.all_to_all(value, ('z', 'x', 'c'), 0, 0, axis_index_groups=groups)]
  transfers between devices with their start and end apart: 30 -> 25, of which waited for: 17 -> 10; matrix products, arithmetic and copies ran while one was open for 11% -> 7% of each run, Pallas kernels for 21% -> 22%
where the time goes in v2:
time: 201 us; the launch traced here: 199 us
  waiting for transfers between devices  69.2 us (34%)
  Pallas kernels  57.3 us (29%)
  starting transfers between devices  39.4 us (20%)
  local copies, waits for them, and re-layouts  16.7 us (8%)
  other arithmetic  14.4 us (7%)
    pallas_call x1, Pallas kernels, attention(): pl.pallas_call(functools.partial(attention_kernel, head0, heads, len(piec...  37.5 us
    ppermute x7, waiting for transfers between devices, flip(): return lax.ppermute(value, ('yl', 'yh'), pairs)  29.2 us
    ppermute x1, waiting for transfers between devices, shards(): m_other = lax.ppermute(m_other, 'yl', [(0, 1), (1, 0)])  17.6 us
    ppermute x3, waiting for transfers between devices, move_z(): return lax.ppermute(value, 'z', [(i, (i + k) % 4) for i in range(4)])  12.3 us
    unnamed x44, local copies, waits for them, and re-layouts  11.4 us
    all_to_all x2, starting transfers between devices, exchange(): lax.all_to_all(value, ('z', 'x', 'c'), 0, 0, axis_index_groups=groups)  9.69 us
    all_to_all x1, waiting for transfers between devices, shards(): steps = lax.all_to_all(steps, ('x', 'yl'), 0, 0)  8.27 us
    all_to_all x1, starting transfers between devices, shards(): lax.all_to_all(jnp.broadcast_to(key_rows[None], (16, 64, WIDE)), ('z', 'x...  8.05 us
  transfers between devices with their start and end apart: 25, of which 10 were waited for; matrix products, arithmetic and copies ran while one was open for 7% of the time, Pallas kernels for 22%

profile of v2, /device:TPU:24, one launch (start us, length us, event | category | flops | bytes accessed | tf_op | source)
XLA Modules:
  0.0 199.0 jit_solution(2128509458259779693)
XLA Ops:
  3.4 3.1 %collective-permute-start.4 = (bf16[64,2176]{1,0:T(8,128)(2,1)S(1)}, bf16[64,2176]{1,0:T(8,128)(2,1)S(1)}, u32[]{:S(2)}, u32[]{:S(2)}) collective-permute-start(bf16[64,2176]{1,0:T(8,128)(2,1)S(1)} %concatenate.31.rest_0_), channel_id=1, source_target_pairs={{0,6},{2,4},{4,2},{6,0},{1,7},{3,5},{5,3},{7,1},{8,14},{10,12},{12... | collective-permute-start | bytes 835592 | tf_op jit(solution)/shard_map/ppermute | solution.py:63
  8.7 8.1 %all-to-all-start = ((bf16[16,64,640]{2,1,0:T(8,128)(2,1)}), bf16[16,64,640]{2,1,0:T(8,128)(2,1)}, u32[]{:S(2)}, u32[]{:S(2)}) async-start(bf16[16,64,640]{2,1,0:T(8,128)(2,1)} %broadcast_in_dim.95), calls=%async_computation | async-start | bytes 2621440 | tf_op jit(solution)/shard_map/all_to_all | solution.py:457
  17.9 2.1 %collective-permute-start.1 = (f32[64,768]{1,0:T(8,128)S(1)}, f32[64,768]{1,0:T(8,128)S(1)}, u32[]{:S(2)}, u32[]{:S(2)}) collective-permute-start(f32[64,768]{1,0:T(8,128)S(1)} %select_maximum_fusion), channel_id=1, source_target_pairs={{0,4},{4,0},{1,5},{5,1},{2,6},{6,2},{3,7},{7,3},{8,12},{12,8},{9,1... | collective-permute-start | bytes 589832 | tf_op jit(solution)/shard_map/ppermute | solution.py:456
  19.9 17.6 %collective-permute-done.1.m_other = f32[64,768]{1,0:T(8,128)S(1)} collective-permute-done((f32[64,768]{1,0:T(8,128)S(1)}, f32[64,768]{1,0:T(8,128)S(1)}, u32[]{:S(2)}, u32[]{:S(2)}) %collective-permute-start.1) | collective-permute-done | bytes 196640 | tf_op jit(solution)/shard_map/ppermute | solution.py:456
  42.0 3.7 %gradient_terms.1 = (f32[4,4,704,128]{3,2,1,0:T(8,128)S(1)}, bf16[256,2176]{1,0:T(8,128)(2,1)S(1)}) custom-call(s32[5]{0:T(128)S(1)} %stack.35.at_ref, bf16[256,1536]{1,0:T(8,128)(2,1)S(1)} %copy-done.4, bf16[256,1024]{1,0:T(8,128)(2,1)S(1)} %copy-done.5, bf16[256,1280]{1,0:T(8,128)(2,1)S(1)} %collective-permute-done.g_other, f32[48,1536]{1,0:T(8,128)S(1)} %copy-done.6, ...), custom_call_target="tpu_custom_call" | custom-call | flops 1000 | bytes 1000 | tf_op jit(solution)/shard_map/gradient_terms/pallas_call | solution.py:267
  45.7 2.5 %copy-done.2 = f32[4,4,704,128]{3,2,1,0:T(8,128)} copy-done((f32[4,4,704,128]{3,2,1,0:T(8,128)}, f32[4,4,704,128]{3,2,1,0:T(8,128)S(1)}, u32[]{:S(2)}) %copy-start.2) | copy-done | bytes 5767192
  49.3 5.3 %all-to-all-start.1 = ((f32[4,4,704,128]{3,2,1,0:T(8,128)}), f32[4,4,704,128]{3,2,1,0:T(8,128)}, u32[]{:S(2)}, u32[]{:S(2)}) async-start(f32[4,4,704,128]{3,2,1,0:T(8,128)} %copy-done.2), calls=%async_computation.1 | async-start | bytes 11534336 | tf_op jit(solution)/shard_map/all_to_all | solution.py:51
  58.1 2.3 %copy-done.3 = bf16[1536,1536]{1,0:T(8,128)(2,1)S(1)} copy-done((bf16[1536,1536]{1,0:T(8,128)(2,1)S(1)}, bf16[1536,1536]{1,0:T(8,128)(2,1)}, u32[]{:S(2)}) %copy-start.3) | copy-done | bytes 4718616
  62.9 2.9 %queries.1.rest_0_.refs_3_ = bf16[2,1024,640]{2,1,0:T(8,128)(2,1)S(1)} custom-call(bf16[256,2176]{1,0:T(8,128)(2,1)S(1)} %copy-done.9, bf16[1536,1536]{1,0:T(8,128)(2,1)S(1)} %copy-done.3, bf16[512,1024]{1,0:T(8,128)(2,1)S(1)} %copy-done.7, f32[256,128]{1,0:T(8,128)S(1)} %get-tuple-element.28.cos_ref, f32[256,128]{1,0:T(8,128)S(1)} %concatenate.34.low_ref, ...), custom_call_target="tpu_custom_call" | custom-call | flops 1000 | bytes 1000 | tf_op jit(solution)/shard_map/queries/pallas_call | solution.py:210
  66.5 19.3 %collective-permute-done.9.refs_6_ = bf16[16,64,640]{2,1,0:T(8,128)(2,1)} collective-permute-done((bf16[16,64,640]{2,1,0:T(8,128)(2,1)}, bf16[16,64,640]{2,1,0:T(8,128)(2,1)}, u32[]{:S(2)}, u32[]{:S(2)}) %collective-permute-start.9) | collective-permute-done | bytes 1310752 | tf_op jit(solution)/shard_map/ppermute | solution.py:63
  85.7 2.7 %slice_add_fusion = bf16[8,64,640]{2,1,0:T(8,128)(2,1)} fusion(bf16[16,64,640]{2,1,0:T(8,128)(2,1)} %collective-permute-done.9.refs_6_, bf16[]{:T(256)} %bitcast.9), kind=kLoop, calls=%fused_computation | loop fusion | flops 327680 | bytes 1310722 | tf_op jit(solution)/shard_map/add | solution.py:471
  88.7 1.8 slice_add_fusion.1
  91.3 3.4 %sum_first.1 = f32[4,704,128]{2,1,0:T(8,128)S(1)} custom-call(f32[4,4,704,128]{3,2,1,0:T(8,128)} %all-to-all-done.1.a_ref, bf16[2,1024,640]{2,1,0:T(8,128)(2,1)S(1)} %queries.1.rest_0_.refs_3_), custom_call_target="tpu_custom_call" | custom-call | flops 1000 | bytes 1000 | tf_op jit(solution)/shard_map/sum_first/pallas_call | solution.py:293
  95.9 10.0 %collective-permute-done.12 = bf16[8,64,640]{2,1,0:T(8,128)(2,1)} collective-permute-done((bf16[8,64,640]{2,1,0:T(8,128)(2,1)}, bf16[8,64,640]{2,1,0:T(8,128)(2,1)}, u32[]{:S(2)}, u32[]{:S(2)}) %collective-permute-start.12) | collective-permute-done | bytes 655392 | tf_op jit(solution)/shard_map/ppermute | solution.py:63
  109.4 4.4 %all-to-all-start.2 = ((f32[4,704,128]{2,1,0:T(8,128)}), f32[4,704,128]{2,1,0:T(8,128)}, u32[]{:S(2)}, u32[]{:S(2)}) async-start(f32[4,704,128]{2,1,0:T(8,128)} %copy-done.1), calls=%async_computation.2 | async-start | bytes 2883584 | tf_op jit(solution)/shard_map/all_to_all | solution.py:51
  113.9 37.5 %attention.1 = (bf16[256,1024]{1,0:T(8,128)(2,1)}, f32[8,128]{1,0:T(8,128)S(1)}) custom-call(s32[64]{0:T(128)S(1)} %pad_add_fusion.refs_0_, s32[2]{0:T(128)S(1)} %pad_add_fusion.1.refs_1_, s32[2]{0:T(128)S(1)} %fusion.2.refs_2_, bf16[2,1024,640]{2,1,0:T(8,128)(2,1)} %copy-done, bf16[512,1024]{1,0:T(8,128)(2,1)} %refs_4_.1, ...), custom_call_target="tpu_custom_call" | custom-call | flops 20000000000 | bytes 14680064 | tf_op jit(solution)/shard_map/attention/pallas_call | solution.py:149
  152.0 2.9 %moment_and_gram.1 = (f32[704,128]{1,0:T(8,128)}, f32[192,384]{1,0:T(8,128)}) custom-call(f32[4,704,128]{2,1,0:T(8,128)} %all-to-all-done.2.p_ref, f32[8,128]{1,0:T(8,128)} %copy-done.13), custom_call_target="tpu_custom_call" | custom-call | flops 1000 | bytes 1000 | tf_op jit(solution)/shard_map/moment_and_gram/pallas_call | solution.py:326
  156.1 2.6 %collective-permute-start.19 = (f32[192,384]{1,0:T(8,128)}, f32[192,384]{1,0:T(8,128)S(1)}, u32[]{:S(2)}, u32[]{:S(2)}) collective-permute-start(f32[192,384]{1,0:T(8,128)} %get-tuple-element.17.a_ref), channel_id=1, source_target_pairs={{0,64},{32,96},{64,0},{96,32},{1,65},{33,97},{65,1},{97,33},{2,66}... | collective-permute-start | bytes 884744 | tf_op jit(solution)/shard_map/ppermute | solution.py:55
  160.2 4.9 %collective-permute-done.18.b_ref = f32[192,384]{1,0:T(8,128)S(1)} collective-permute-done((f32[192,384]{1,0:T(8,128)}, f32[192,384]{1,0:T(8,128)S(1)}, u32[]{:S(2)}, u32[]{:S(2)}) %collective-permute-start.18) | collective-permute-done | bytes 294944 | tf_op jit(solution)/shard_map/ppermute | solution.py:55
  165.1 7.4 %collective-permute-done.19.c_ref = f32[192,384]{1,0:T(8,128)S(1)} collective-permute-done((f32[192,384]{1,0:T(8,128)}, f32[192,384]{1,0:T(8,128)S(1)}, u32[]{:S(2)}, u32[]{:S(2)}) %collective-permute-start.19) | collective-permute-done | bytes 294944 | tf_op jit(solution)/shard_map/ppermute | solution.py:55
  173.3 7.0 %newton.1 = f32[8,64,256]{2,1,0:T(8,128)} custom-call(f32[704,128]{1,0:T(8,128)} %get-tuple-element.16.m_ref, f32[192,384]{1,0:T(8,128)} %get-tuple-element.17.a_ref, f32[192,384]{1,0:T(8,128)} %copy-done.15, f32[192,384]{1,0:T(8,128)} %copy-done.16, f32[192,384]{1,0:T(8,128)} %copy-done.17), custom_call_target="tpu_custom_call" | custom-call | flops 1000 | bytes 1000 | tf_op jit(solution)/shard_map/newton/pallas_call | solution.py:394
  180.4 5.9 %all-to-all-start.3 = ((f32[8,64,256]{2,1,0:T(8,128)}), f32[8,64,256]{2,1,0:T(8,128)S(1)}, u32[]{:S(2)}, u32[]{:S(2)}) async-start(f32[8,64,256]{2,1,0:T(8,128)} %newton.1), calls=%async_computation.3 | async-start | bytes 1048576 | tf_op jit(solution)/shard_map/all_to_all | solution.py:496
  186.3 8.3 %all-to-all-done.3 = f32[8,64,256]{2,1,0:T(8,128)S(1)} async-done(((f32[8,64,256]{2,1,0:T(8,128)}), f32[8,64,256]{2,1,0:T(8,128)S(1)}, u32[]{:S(2)}, u32[]{:S(2)}) %all-to-all-start.3) | async-done | bytes 524320 | tf_op jit(solution)/shard_map/all_to_all | solution.py:496
  197.1 1.7 subtract_multiply_fusion
  (125 shorter events, 30.1 us)
Async XLA Ops:
  1.7 36.5 %collective-permute-start.2 = (bf16[64,2176]{1,0:T(8,128)(2,1)S(1)}, bf16[64,2176]{1,0:T(8,128)(2,1)S(1)}, u32[]{:S(2)}, u32[]{:S(2)}) collective-permute-start(bf16[64,2176]{1,0:T(8,128)(2,1)S(1)} %concatenate.31.rest_0_), channel_id=1, source_target_pairs={{0,4},{2,6},{4,0},{6,2},{1,5},{3,7},{5,1},{7,3},{8,12},{10,14},{12... | collective-permute-start | bytes 835592 | tf_op jit(solution)/shard_map/ppermute | solution.py:63
  2.5 36.2 %collective-permute-start.3 = (bf16[64,2176]{1,0:T(8,128)(2,1)S(1)}, bf16[64,2176]{1,0:T(8,128)(2,1)S(1)}, u32[]{:S(2)}, u32[]{:S(2)}) collective-permute-start(bf16[64,2176]{1,0:T(8,128)(2,1)S(1)} %concatenate.31.rest_0_), channel_id=1, source_target_pairs={{0,2},{2,0},{4,6},{6,4},{1,3},{3,1},{5,7},{7,5},{8,10},{10,8},{12,... | collective-permute-start | bytes 835592 | tf_op jit(solution)/shard_map/ppermute | solution.py:63
  3.4 35.4 %collective-permute-start.4 = (bf16[64,2176]{1,0:T(8,128)(2,1)S(1)}, bf16[64,2176]{1,0:T(8,128)(2,1)S(1)}, u32[]{:S(2)}, u32[]{:S(2)}) collective-permute-start(bf16[64,2176]{1,0:T(8,128)(2,1)S(1)} %concatenate.31.rest_0_), channel_id=1, source_target_pairs={{0,6},{2,4},{4,2},{6,0},{1,7},{3,5},{5,3},{7,1},{8,14},{10,12},{12... | collective-permute-start | bytes 835592 | tf_op jit(solution)/shard_map/ppermute | solution.py:63
  8.7 32.4 %all-to-all-start = ((bf16[16,64,640]{2,1,0:T(8,128)(2,1)}), bf16[16,64,640]{2,1,0:T(8,128)(2,1)}, u32[]{:S(2)}, u32[]{:S(2)}) async-start(bf16[16,64,640]{2,1,0:T(8,128)(2,1)} %broadcast_in_dim.95), calls=%async_computation | async-start | bytes 2621440 | tf_op jit(solution)/shard_map/all_to_all | solution.py:457
  17.8 23.3 %collective-permute-start = (bf16[256,1280]{1,0:T(8,128)(2,1)}, bf16[256,1280]{1,0:T(8,128)(2,1)S(1)}, u32[]{:S(2)}, u32[]{:S(2)}) collective-permute-start(bf16[256,1280]{1,0:T(8,128)(2,1)} %pad_maximum_fusion), channel_id=1, source_target_pairs={{0,4},{4,0},{1,5},{5,1},{2,6},{6,2},{3,7},{7,3},{8,12},{12,8},{9,1... | collective-permute-start | bytes 1966088 | tf_op jit(solution)/shard_map/ppermute | solution.py:453
  17.9 19.7 %collective-permute-start.1 = (f32[64,768]{1,0:T(8,128)S(1)}, f32[64,768]{1,0:T(8,128)S(1)}, u32[]{:S(2)}, u32[]{:S(2)}) collective-permute-start(f32[64,768]{1,0:T(8,128)S(1)} %select_maximum_fusion), channel_id=1, source_target_pairs={{0,4},{4,0},{1,5},{5,1},{2,6},{6,2},{3,7},{7,3},{8,12},{12,8},{9,1... | collective-permute-start | bytes 589832 | tf_op jit(solution)/shard_map/ppermute | solution.py:456
  38.2 2.1 %collective-permute-start.6 = (bf16[64,2176]{1,0:T(8,128)(2,1)S(1)}, bf16[64,2176]{1,0:T(8,128)(2,1)}, u32[]{:S(2)}, u32[]{:S(2)}) collective-permute-start(bf16[64,2176]{1,0:T(8,128)(2,1)S(1)} %collective-permute-done.2.rest_1_), channel_id=1, source_target_pairs={{0,1},{1,0},{2,3},{3,2},{4,5},{5,4},{6,7},{7,6},{8,9},{9,8},{10,11... | collective-permute-start | bytes 835592 | tf_op jit(solution)/shard_map/ppermute | solution.py:67
  38.7 2.0 collective-permute-start.7
  38.8 2.3 %collective-permute-start.8 = (bf16[64,2176]{1,0:T(8,128)(2,1)S(1)}, bf16[64,2176]{1,0:T(8,128)(2,1)}, u32[]{:S(2)}, u32[]{:S(2)}) collective-permute-start(bf16[64,2176]{1,0:T(8,128)(2,1)S(1)} %collective-permute-done.4.rest_3_), channel_id=1, source_target_pairs={{0,1},{1,0},{2,3},{3,2},{4,5},{5,4},{6,7},{7,6},{8,9},{9,8},{10,11... | collective-permute-start | bytes 835592 | tf_op jit(solution)/shard_map/ppermute | solution.py:67
  49.3 42.0 %all-to-all-start.1 = ((f32[4,4,704,128]{3,2,1,0:T(8,128)}), f32[4,4,704,128]{3,2,1,0:T(8,128)}, u32[]{:S(2)}, u32[]{:S(2)}) async-start(f32[4,4,704,128]{3,2,1,0:T(8,128)} %copy-done.2), calls=%async_computation.1 | async-start | bytes 11534336 | tf_op jit(solution)/shard_map/all_to_all | solution.py:51
  54.5 31.2 %collective-permute-start.9 = (bf16[16,64,640]{2,1,0:T(8,128)(2,1)}, bf16[16,64,640]{2,1,0:T(8,128)(2,1)}, u32[]{:S(2)}, u32[]{:S(2)}) collective-permute-start(bf16[16,64,640]{2,1,0:T(8,128)(2,1)} %all-to-all-done.rest_8_.refs_5_), channel_id=1, source_target_pairs={{0,4},{2,6},{4,0},{6,2},{1,5},{3,7},{5,1},{7,3},{8,12},{10,14},{12... | collective-permute-start | bytes 3932168 | tf_op jit(solution)/shard_map/ppermute | solution.py:63
  54.9 33.8 %collective-permute-start.10 = (bf16[16,64,640]{2,1,0:T(8,128)(2,1)}, bf16[16,64,640]{2,1,0:T(8,128)(2,1)}, u32[]{:S(2)}, u32[]{:S(2)}) collective-permute-start(bf16[16,64,640]{2,1,0:T(8,128)(2,1)} %all-to-all-done.rest_8_.refs_5_), channel_id=1, source_target_pairs={{0,6},{2,4},{4,2},{6,0},{1,7},{3,5},{5,3},{7,1},{8,14},{10,12},{12... | collective-permute-start | bytes 3932168 | tf_op jit(solution)/shard_map/ppermute | solution.py:63
  88.4 17.5 %collective-permute-start.12 = (bf16[8,64,640]{2,1,0:T(8,128)(2,1)}, bf16[8,64,640]{2,1,0:T(8,128)(2,1)}, u32[]{:S(2)}, u32[]{:S(2)}) collective-permute-start(bf16[8,64,640]{2,1,0:T(8,128)(2,1)} %slice_add_fusion), channel_id=1, source_target_pairs={{0,6},{2,4},{4,2},{6,0},{1,7},{3,5},{5,3},{7,1},{8,14},{10,12},{12... | collective-permute-start | bytes 1966088 | tf_op jit(solution)/shard_map/ppermute | solution.py:63
  90.5 16.8 %collective-permute-start.11 = (bf16[8,64,640]{2,1,0:T(8,128)(2,1)S(1)}, bf16[8,64,640]{2,1,0:T(8,128)(2,1)}, u32[]{:S(2)}, u32[]{:S(2)}) collective-permute-start(bf16[8,64,640]{2,1,0:T(8,128)(2,1)S(1)} %slice_add_fusion.1), channel_id=1, source_target_pairs={{0,4},{2,6},{4,0},{6,2},{1,5},{3,7},{5,1},{7,3},{8,12},{10,14},{12... | collective-permute-start | bytes 1966088 | tf_op jit(solution)/shard_map/ppermute | solution.py:63
  90.6 23.3 %collective-permute-start.13 = (bf16[16,64,640]{2,1,0:T(8,128)(2,1)}, bf16[16,64,640]{2,1,0:T(8,128)(2,1)}, u32[]{:S(2)}, u32[]{:S(2)}) collective-permute-start(bf16[16,64,640]{2,1,0:T(8,128)(2,1)} %all-to-all-done.rest_8_.refs_5_), channel_id=1, source_target_pairs={{0,1},{1,0},{2,3},{3,2},{4,5},{5,4},{6,7},{7,6},{8,9},{9,8},{10,11... | collective-permute-start | bytes 3932168 | tf_op jit(solution)/shard_map/ppermute | solution.py:67
  90.7 23.2 %collective-permute-start.14 = (bf16[16,64,640]{2,1,0:T(8,128)(2,1)}, bf16[16,64,640]{2,1,0:T(8,128)(2,1)}, u32[]{:S(2)}, u32[]{:S(2)}) collective-permute-start(bf16[16,64,640]{2,1,0:T(8,128)(2,1)} %collective-permute-done.9.refs_6_), channel_id=1, source_target_pairs={{0,1},{1,0},{2,3},{3,2},{4,5},{5,4},{6,7},{7,6},{8,9},{9,8},{10,11... | collective-permute-start | bytes 3932168 | tf_op jit(solution)/shard_map/ppermute | solution.py:67
  91.2 22.7 %collective-permute-start.15 = (bf16[16,64,640]{2,1,0:T(8,128)(2,1)}, bf16[16,64,640]{2,1,0:T(8,128)(2,1)}, u32[]{:S(2)}, u32[]{:S(2)}) collective-permute-start(bf16[16,64,640]{2,1,0:T(8,128)(2,1)} %collective-permute-done.10.refs_7_), channel_id=1, source_target_pairs={{0,1},{1,0},{2,3},{3,2},{4,5},{5,4},{6,7},{7,6},{8,9},{9,8},{10,11... | collective-permute-start | bytes 3932168 | tf_op jit(solution)/shard_map/ppermute | solution.py:67
  107.0 6.9 %collective-permute-start.17 = (bf16[8,64,640]{2,1,0:T(8,128)(2,1)S(1)}, bf16[8,64,640]{2,1,0:T(8,128)(2,1)}, u32[]{:S(2)}, u32[]{:S(2)}) collective-permute-start(bf16[8,64,640]{2,1,0:T(8,128)(2,1)S(1)} %broadcast_add_fusion.refs_9_), channel_id=1, source_target_pairs={{0,1},{1,0},{2,3},{3,2},{4,5},{5,4},{6,7},{7,6},{8,9},{9,8},{10,11... | collective-permute-start | bytes 1966088 | tf_op jit(solution)/shard_map/ppermute | solution.py:67
  108.5 5.4 %collective-permute-start.16 = (bf16[8,64,640]{2,1,0:T(8,128)(2,1)S(1)}, bf16[8,64,640]{2,1,0:T(8,128)(2,1)S(1)}, u32[]{:S(2)}, u32[]{:S(2)}) collective-permute-start(bf16[8,64,640]{2,1,0:T(8,128)(2,1)S(1)} %broadcast_add_fusion.1.refs_8_), channel_id=1, source_target_pairs={{0,1},{1,0},{2,3},{3,2},{4,5},{5,4},{6,7},{7,6},{8,9},{9,8},{10,11... | collective-permute-start | bytes 1966088 | tf_op jit(solution)/shard_map/ppermute | solution.py:67
  109.4 42.5 %all-to-all-start.2 = ((f32[4,704,128]{2,1,0:T(8,128)}), f32[4,704,128]{2,1,0:T(8,128)}, u32[]{:S(2)}, u32[]{:S(2)}) async-start(f32[4,704,128]{2,1,0:T(8,128)} %copy-done.1), calls=%async_computation.2 | async-start | bytes 2883584 | tf_op jit(solution)/shard_map/all_to_all | solution.py:51
  154.8 10.3 %collective-permute-start.18 = (f32[192,384]{1,0:T(8,128)}, f32[192,384]{1,0:T(8,128)S(1)}, u32[]{:S(2)}, u32[]{:S(2)}) collective-permute-start(f32[192,384]{1,0:T(8,128)} %get-tuple-element.17.a_ref), channel_id=1, source_target_pairs={{0,32},{32,64},{64,96},{96,0},{1,33},{33,65},{65,97},{97,1},{2,34}... | collective-permute-start | bytes 884744 | tf_op jit(solution)/shard_map/ppermute | solution.py:55
  156.1 16.3 %collective-permute-start.19 = (f32[192,384]{1,0:T(8,128)}, f32[192,384]{1,0:T(8,128)S(1)}, u32[]{:S(2)}, u32[]{:S(2)}) collective-permute-start(f32[192,384]{1,0:T(8,128)} %get-tuple-element.17.a_ref), channel_id=1, source_target_pairs={{0,64},{32,96},{64,0},{96,32},{1,65},{33,97},{65,1},{97,33},{2,66}... | collective-permute-start | bytes 884744 | tf_op jit(solution)/shard_map/ppermute | solution.py:55
  158.7 13.8 %collective-permute-start.20 = (f32[192,384]{1,0:T(8,128)}, f32[192,384]{1,0:T(8,128)S(1)}, u32[]{:S(2)}, u32[]{:S(2)}) collective-permute-start(f32[192,384]{1,0:T(8,128)} %get-tuple-element.17.a_ref), channel_id=1, source_target_pairs={{0,96},{32,0},{64,32},{96,64},{1,97},{33,1},{65,33},{97,65},{2,98}... | collective-permute-start | bytes 884744 | tf_op jit(solution)/shard_map/ppermute | solution.py:55
  180.4 14.2 %all-to-all-start.3 = ((f32[8,64,256]{2,1,0:T(8,128)}), f32[8,64,256]{2,1,0:T(8,128)S(1)}, u32[]{:S(2)}, u32[]{:S(2)}) async-start(f32[8,64,256]{2,1,0:T(8,128)} %newton.1), calls=%async_computation.3 | async-start | bytes 1048576 | tf_op jit(solution)/shard_map/all_to_all | solution.py:496
  (23 other events, 117.4 us)

commit v3 on v2

--- a/solution.py
+++ b/solution.py
@@ -169,6 +169,22 @@
         ),
         name="attention",
     )(place, core_rows, qpos, queries, w_value, *pieces, *ties)
+
+
+def mark_kernel(*refs):
+    refs[-1][...] = jnp.zeros((8, 128), F32)
+
+
+def mark_after(ties):
+    return pl.pallas_call(
+        mark_kernel,
+        out_shape=jax.ShapeDtypeStruct((8, 128), F32),
+        in_specs=[ANY] * len(ties),
+        out_specs=VMEM,
+        compiler_params=pltpu.CompilerParams(vmem_limit_bytes=2**20),
+        cost_estimate=pl.CostEstimate(flops=34 * 10**9, bytes_accessed=1000, transcendentals=0),
+        name="mark",
+    )(*ties)
 
 
 def query_kernel(l_ref, wq_ref, wk_ref, cos_ref, low_ref, high_ref, out_ref):
@@ -279,7 +295,7 @@
             pltpu.VMEM((768, 384), F32),
             pltpu.VMEM((512, 128), F32),
         ],
-        compiler_params=pltpu.CompilerParams(vmem_limit_bytes=32 * 2**20),
+        compiler_params=pltpu.CompilerParams(vmem_limit_bytes=56 * 2**20),
         cost_estimate=pl.CostEstimate(flops=1000, bytes_accessed=1000, transcendentals=0),
         name="gradient_terms",
     )(at, grad_query, grad_key, g_other, mom_query, mom_key, m_other, *shards, *ties)
@@ -316,10 +332,12 @@
         block = m_ref[t * HEAD : (t + 1) * HEAD, :]
         term = nt(block, block)
         gram = term if gram is None else gram + term
-    g_ref[:, :HEAD] = gram
+    g_ref[:128, :] = gram[:128, :128]
+    g_ref[256:320, :64] = gram[128:, 128:]
+    g_ref[320:384, :] = gram[128:, :128]
     block = m_ref[3 * HEAD : 704, :]
-    g_ref[:128, 256:384] = nt(block, block)
-    g_ref[128:136, 256:384] = peak_ref[...]
+    g_ref[128:256, :] = nt(block, block)
+    g_ref[384:392, :] = peak_ref[...]
 
 
 def moment_and_gram(parts, peaks):
@@ -327,7 +345,7 @@
         gram_kernel,
         out_shape=(
             jax.ShapeDtypeStruct((704, 128), F32),
-            jax.ShapeDtypeStruct((HEAD, 384), F32),
+            jax.ShapeDtypeStruct((392, 128), F32),
         ),
         in_specs=[VMEM, VMEM],
         out_specs=(VMEM, VMEM),
@@ -360,13 +378,21 @@
 
 def newton_kernel(m_ref, a_ref, b_ref, c_ref, d_ref, *rest):
     out_ref = rest[-1]
-    spot = (slice(128, 136), slice(256, 384))
+    spot = (slice(384, 392), slice(0, 128))
     peaks = jnp.maximum(
         jnp.maximum(a_ref[spot], b_ref[spot]), jnp.maximum(c_ref[spot], d_ref[spot])
     )
     gram = (a_ref[...] + b_ref[...]) + (c_ref[...] + d_ref[...])
-    factor_q = newton_factor(gram[:, :HEAD]) * (0.2 * math.sqrt(QR))
-    factor_k = newton_factor(gram[:128, 256:384]) * (0.2 * math.sqrt(KVR))
+    low = gram[320:384, :]
+    gram_q = jnp.concatenate(
+        [
+            jnp.concatenate([gram[:128, :], low.T], axis=1),
+            jnp.concatenate([low, gram[256:320, :64]], axis=1),
+        ],
+        axis=0,
+    )
+    factor_q = newton_factor(gram_q) * (0.2 * math.sqrt(QR))
+    factor_k = newton_factor(gram[128:256, :]) * (0.2 * math.sqrt(KVR))
     rows = []
     for t in range(3):
         block = m_ref[t * HEAD : (t + 1) * HEAD, :]
@@ -399,6 +425,62 @@
         cost_estimate=pl.CostEstimate(flops=1000, bytes_accessed=1000, transcendentals=0),
         name="newton",
     )(moment, *grams, *ties)
+
+
+def update_kernel(step_ref, wq_ref, wk_ref, flag_ref, sq_ref, sk_ref, nq_ref, nk_ref, peak_ref):
+    peaks = step_ref[0, 48:56, 128:]
+    for source in range(1, 8):
+        peaks = jnp.maximum(peaks, step_ref[source, 48:56, 128:])
+    peak_ref[...] = peaks
+    ratio = CLIP_TAU / jnp.maximum(peaks, CLIP_TAU)
+    gamma = jnp.concatenate(
+        [jnp.where(flag_ref[h] > 0, ratio[h : h + 1], 1.0) for h in range(8)], axis=0
+    )
+    root = jnp.sqrt(gamma)
+    keep = 1.0 - LEARN_RATE * DECAY
+    lane = lax.broadcasted_iota(jnp.int32, (1, 384), 1)
+    none = jnp.zeros((48, 128), F32)
+
+    def source_of(head):
+        return head % 4 * 2 + head // 4
+
+    def thrice(row):
+        return jnp.concatenate([row] * 3, axis=1)
+
+    for pair in range(4):
+        even, odd = 2 * pair, 2 * pair + 1
+        step = jnp.concatenate([step_ref[source_of(even), :48, :], none], axis=1) + pltpu.roll(
+            jnp.concatenate([step_ref[source_of(odd), :48, :], none], axis=1), HEAD, 1
+        )
+        columns = slice(pair * 384, (pair + 1) * 384)
+        sq_ref[:, columns] = step
+        factor = jnp.where(
+            lane < HEAD,
+            jnp.where(lane < NOPE, thrice(root[even : even + 1]), thrice(gamma[even : even + 1])),
+            jnp.where(
+                lane < HEAD + NOPE, thrice(root[odd : odd + 1]), thrice(gamma[odd : odd + 1])
+            ),
+        )
+        nq_ref[:, columns] = (wq_ref[:, columns].astype(F32) * keep - LEARN_RATE * step) * factor
+    for head in range(8):
+        columns = slice(head * 128, (head + 1) * 128)
+        step = step_ref[source_of(head), 48:, :128]
+        sk_ref[:, columns] = step
+        nk_ref[:, columns] = (
+            wk_ref[:, columns].astype(F32) * keep - LEARN_RATE * step
+        ) * root[head : head + 1]
+
+
+def update(steps, owned_query, owned_key, flags):
+    shapes = ((48, QR), (16, 1024), (48, QR), (16, 1024), (8, 128))
+    return pl.pallas_call(
+        update_kernel,
+        out_shape=tuple(jax.ShapeDtypeStruct(shape, F32) for shape in shapes),
+        in_specs=[VMEM] * 3 + [SMEM],
+        out_specs=tuple(VMEM for _ in shapes),
+        cost_estimate=pl.CostEstimate(flops=1000, bytes_accessed=1000, transcendentals=0),
+        name="update",
+    )(steps, owned_query, owned_key, flags)
 
 
 def turn_tables(positions):
@@ -457,18 +539,19 @@
     plane = lax.all_to_all(
         jnp.broadcast_to(key_rows[None], (16, 64, WIDE)), ("z", "x"), 0, 0
     )
+    near = [flip(plane[:8], 1), flip(plane[:8], 3), flip(plane[8:], 1), flip(plane[8:], 3)]
     at = jnp.stack([c, z, x, yl, yh]).astype(jnp.int32)
     terms, l_own = gradient_terms(
-        at, grad_query, grad_key, g_other, mom_query, mom_key, m_other, flips + swapped, [plane]
+        at, grad_query, grad_key, g_other, mom_query, mom_key, m_other, flips + swapped, []
     )
     terms = exchange(terms, FIRST)
-    near = [flip(plane, k) for k in (1, 3)]
     local_rows = jnp.arange(256, dtype=jnp.int32)
     qpos = look_up(block_order, 2 * ctx + jnp.arange(2, dtype=jnp.int32))
     query_pos = jnp.where(local_rows < 128, qpos[0], qpos[1]) * 128 + local_rows % 128
     wide = project_queries(l_own, w_query, w_key, *turn_tables(query_pos))
-    after = wide[0, 0, WIDE - 1]
-    far = [flip(near[1][:8] + after, 1), flip(near[0][8:] + after, 3)]
+    far = [flip(near[1], 1), flip(near[2], 3)]
+    mine = [plane, *near, *far]
+    pieces = mine + [swap_core(piece) for piece in mine]
     slot = jnp.arange(16, dtype=jnp.int32)
     place = jnp.concatenate(
         [
@@ -479,42 +562,25 @@
             for k in (0, 1, 3, 2)
         ]
     )
+    place = jnp.concatenate([place[:24], place[32:40], place[24:32], place[40:]])
     core_rows = jnp.stack([c * 64, 64 - c * 64]).astype(jnp.int32)
 
-    terms = sum_first(terms, [wide])
-    later = (terms[0, 0, 0] * 0).astype(BF16)
-    far = [piece + later for piece in far]
-    mine = [plane, *near, *far]
-    pieces = mine + [swap_core(piece) for piece in mine]
+    terms = sum_first(terms, [])
     parts = exchange(terms, SECOND)
     attn_out, peaks = attention(
-        0, 8, place, core_rows, qpos, wide, w_value, pieces, []
+        0, 8, place, core_rows, qpos, wide, w_value, pieces, [mark_after([*near, wide])]
     )
     moment, gram = moment_and_gram(parts, peaks)
     grams = [gram] + [move_z(gram, k) for k in (1, 2, 3)]
     steps = newton(moment, grams, [])
     steps = lax.all_to_all(steps, ("x", "yl"), 0, 0)
-    step_query = (
-        steps[:, :48, :HEAD].reshape(4, 2, 48, HEAD).transpose(2, 1, 0, 3).reshape(48, QR)
-    )
-    step_key = steps[:, 48:, :128].reshape(4, 2, 16, 128).transpose(2, 1, 0, 3).reshape(16, 1024)
-    head_peaks = jnp.max(steps[:, 48:56, 128], axis=0)
-    clip_gamma = jnp.where(clip_flags > 0, CLIP_TAU / jnp.maximum(head_peaks, CLIP_TAU), 1.0)
-    root_gamma = jnp.sqrt(clip_gamma)
-    query_factor = jnp.concatenate(
-        [
-            jnp.broadcast_to(root_gamma[:, None], (8, NOPE)),
-            jnp.broadcast_to(clip_gamma[:, None], (8, ROPE)),
-        ],
-        axis=1,
-    ).reshape(-1)
-    key_factor = jnp.repeat(root_gamma, NOPE)
-    owned_query = lax.dynamic_slice_in_dim(w_query, ctx * 48, 48, 0).astype(F32)
-    owned_key = lax.dynamic_slice_in_dim(w_key, ctx * 16, 16, 0).astype(F32)
-    keep = 1.0 - LEARN_RATE * DECAY
-    new_query = (owned_query * keep - LEARN_RATE * step_query) * query_factor[None, :]
-    new_key = (owned_key * keep - LEARN_RATE * step_key) * key_factor[None, :]
-    return (attn_out, head_peaks, step_query, step_key, new_query, new_key)
+    step_query, step_key, new_query, new_key, head_peaks = update(
+        steps,
+        lax.dynamic_slice_in_dim(w_query, ctx * 48, 48, 0),
+        lax.dynamic_slice_in_dim(w_key, ctx * 16, 16, 0),
+        clip_flags,
+    )
+    return (attn_out, head_peaks[:, 0], step_query, step_key, new_query, new_key)
 
 
 def solution(mesh):

time: 201 us -> 186 us (0.925)
  waiting for transfers between devices: 69.2 us -> 54.2 us
  other arithmetic: 14.4 us -> 4.66 us
  Pallas kernels: 57.3 us -> 64.1 us
  starting transfers between devices: 39.4 us -> 42.1 us
  local copies, waits for them, and re-layouts: 16.7 us -> 19.4 us
    ppermute x7 -> x9, waiting for transfers between devices: 29.2 us -> 22.5 us  [flip(): return lax.ppermute(value, ('yl', 'yh'), pairs)]
    add x4 -> x0, other arithmetic: 6.75 us -> none  [the longest x2 4.45 us: shards(): far = [flip(near[1][:8] + after, 1), flip(near[0][8:] + after, 3)]]
    ppermute x7 -> x9, starting transfers between devices: 5.81 us -> 10.3 us  [flip(): return lax.ppermute(value, ('yl', 'yh'), pairs)]
    ppermute x3, waiting for transfers between devices: 12.3 us -> 8.36 us  [move_z(): return lax.ppermute(value, 'z', [(i, (i + k) % 4) for i in range(4)])]
    pallas_call x1, Pallas kernels: 3.67 us -> 7.28 us  [gradient_terms(): pl.pallas_call(gradient_kernel, out_shape=(jax.ShapeDtypeStruct((4, 4, 70...]
    all_to_all x1, waiting for transfers between devices: 8.27 us -> 5.17 us  [shards(): steps = lax.all_to_all(steps, ('x', 'yl'), 0, 0)]
    mul x2 -> x0, other arithmetic: 3.08 us -> none  [the longest x1 1.67 us: shards(): (owned_query * keep - LEARN_RATE * step_query) * query_factor[None, :]]
    dynamic_slice x0 -> x2, local copies, waits for them, and re-layouts: none -> 2.95 us  [the longest x1 1.58 us: shards(): lax.dynamic_slice_in_dim(w_query, ctx * 48, 48, 0)]
  transfers between devices with their start and end apart: 25 -> 29, of which waited for: 10 -> 8; matrix products, arithmetic and copies ran while one was open for 7% -> 7% of each run, Pallas kernels for 22% -> 28%
where the time goes in v3:
time: 186 us; the launch traced here: 185 us
  Pallas kernels  64.1 us (34%)
  waiting for transfers between devices  54.2 us (29%)
  starting transfers between devices  42.1 us (23%)
  local copies, waits for them, and re-layouts  19.4 us (10%)
  other arithmetic  4.66 us (3%)
    pallas_call x1, Pallas kernels, attention(): pl.pallas_call(functools.partial(attention_kernel, head0, heads, len(piec...  37.4 us
    ppermute x9, waiting for transfers between devices, flip(): return lax.ppermute(value, ('yl', 'yh'), pairs)  22.5 us
    ppermute x1, waiting for transfers between devices, shards(): m_other = lax.ppermute(m_other, 'yl', [(0, 1), (1, 0)])  16.8 us
    ppermute x9, starting transfers between devices, flip(): return lax.ppermute(value, ('yl', 'yh'), pairs)  10.3 us
    all_to_all x2, starting transfers between devices, exchange(): lax.all_to_all(value, ('z', 'x', 'c'), 0, 0, axis_index_groups=groups)  9.48 us
    unnamed x44, local copies, waits for them, and re-layouts  9.02 us
    ppermute x3, waiting for transfers between devices, move_z(): return lax.ppermute(value, 'z', [(i, (i + k) % 4) for i in range(4)])  8.36 us
    all_to_all x1, starting transfers between devices, shards(): lax.all_to_all(jnp.broadcast_to(key_rows[None], (16, 64, WIDE)), ('z', 'x...  8.05 us
  transfers between devices with their start and end apart: 29, of which 8 were waited for; matrix products, arithmetic and copies ran while one was open for 7% of the time, Pallas kernels for 28%

profile of v3, /device:TPU:24, one launch (start us, length us, event | category | flops | bytes accessed | tf_op | source)
XLA Modules:
  0.0 185.4 jit_solution(12699218879786450190)
XLA Ops:
  3.4 3.1 %collective-permute-start.4 = (bf16[64,2176]{1,0:T(8,128)(2,1)S(1)}, bf16[64,2176]{1,0:T(8,128)(2,1)}, u32[]{:S(2)}, u32[]{:S(2)}) collective-permute-start(bf16[64,2176]{1,0:T(8,128)(2,1)S(1)} %concatenate.37.rest_0_), channel_id=1, source_target_pairs={{0,6},{2,4},{4,2},{6,0},{1,7},{3,5},{5,3},{7,1},{8,14},{10,12},{12... | collective-permute-start | bytes 835592 | tf_op jit(solution)/shard_map/ppermute | solution.py:63
  8.7 8.1 %all-to-all-start = ((bf16[16,64,640]{2,1,0:T(8,128)(2,1)}), bf16[16,64,640]{2,1,0:T(8,128)(2,1)}, u32[]{:S(2)}, u32[]{:S(2)}) async-start(bf16[16,64,640]{2,1,0:T(8,128)(2,1)} %broadcast_in_dim.81), calls=%async_computation | async-start | bytes 2621440 | tf_op jit(solution)/shard_map/all_to_all | solution.py:539
  17.9 2.1 %collective-permute-start.1 = (f32[64,768]{1,0:T(8,128)S(1)}, f32[64,768]{1,0:T(8,128)S(1)}, u32[]{:S(2)}, u32[]{:S(2)}) collective-permute-start(f32[64,768]{1,0:T(8,128)S(1)} %select_maximum_fusion), channel_id=1, source_target_pairs={{0,4},{4,0},{1,5},{5,1},{2,6},{6,2},{3,7},{7,3},{8,12},{12,8},{9,1... | collective-permute-start | bytes 589832 | tf_op jit(solution)/shard_map/ppermute | solution.py:538
  20.8 16.8 %collective-permute-done.1.m_other = f32[64,768]{1,0:T(8,128)S(1)} collective-permute-done((f32[64,768]{1,0:T(8,128)S(1)}, f32[64,768]{1,0:T(8,128)S(1)}, u32[]{:S(2)}, u32[]{:S(2)}) %collective-permute-start.1) | collective-permute-done | bytes 196640 | tf_op jit(solution)/shard_map/ppermute | solution.py:538
  40.6 2.3 %fusion.8 = (bf16[8,64,640]{2,1,0:T(8,128)(2,1)S(1)}, bf16[8,64,640]{2,1,0:T(8,128)(2,1)}) fusion(bf16[16,64,640]{2,1,0:T(8,128)(2,1)} %all-to-all-done.refs_5_), kind=kLoop, calls=%fused_computation.51 | loop fusion | bytes 2621440 | tf_op jit(solution)/shard_map/slice | solution.py:542
  43.6 2.9 %collective-permute-start.10 = (bf16[8,64,640]{2,1,0:T(8,128)(2,1)}, bf16[8,64,640]{2,1,0:T(8,128)(2,1)}, u32[]{:S(2)}, u32[]{:S(2)}) collective-permute-start(bf16[8,64,640]{2,1,0:T(8,128)(2,1)} %get-tuple-element.33), channel_id=1, source_target_pairs={{0,6},{2,4},{4,2},{6,0},{1,7},{3,5},{5,3},{7,1},{8,14},{10,12},{12... | collective-permute-start | bytes 1966088 | tf_op jit(solution)/shard_map/ppermute | solution.py:63
  47.4 7.3 %gradient_terms.1 = (f32[4,4,704,128]{3,2,1,0:T(8,128)}, bf16[256,2176]{1,0:T(8,128)(2,1)}) custom-call(s32[5]{0:T(128)} %stack.35.at_ref, bf16[256,1536]{1,0:T(8,128)(2,1)} %gq_ref.1, bf16[256,1024]{1,0:T(8,128)(2,1)} %gk_ref.1, bf16[256,1280]{1,0:T(8,128)(2,1)} %copy-done.11, f32[48,1536]{1,0:T(8,128)} %mq_ref.1, f32[16,1024]{1,0:T(8,128)} %mk_ref.1, ...), custom_call_target="tpu_custom_call" | custom-call | flops 1000 | bytes 1000 | tf_op jit(solution)/shard_map/gradient_terms/pallas_call | solution.py:283
  54.7 5.1 %all-to-all-start.1 = ((f32[4,4,704,128]{3,2,1,0:T(8,128)}), f32[4,4,704,128]{3,2,1,0:T(8,128)}, u32[]{:S(2)}, u32[]{:S(2)}) async-start(f32[4,4,704,128]{3,2,1,0:T(8,128)} %get-tuple-element.19), calls=%async_computation.1 | async-start | bytes 11534336 | tf_op jit(solution)/shard_map/all_to_all | solution.py:51
  61.3 13.9 %collective-permute-done.10.refs_1_.refs_7_ = bf16[8,64,640]{2,1,0:T(8,128)(2,1)} collective-permute-done((bf16[8,64,640]{2,1,0:T(8,128)(2,1)}, bf16[8,64,640]{2,1,0:T(8,128)(2,1)}, u32[]{:S(2)}, u32[]{:S(2)}) %collective-permute-start.10) | collective-permute-done | bytes 655392 | tf_op jit(solution)/shard_map/ppermute | solution.py:63
  77.4 2.3 %copy-done = bf16[1536,1536]{1,0:T(8,128)(2,1)S(1)} copy-done((bf16[1536,1536]{1,0:T(8,128)(2,1)S(1)}, bf16[1536,1536]{1,0:T(8,128)(2,1)}, u32[]{:S(2)}) %copy-start) | copy-done | bytes 4718616
  82.2 2.9 %queries.1.refs_4_.refs_3_ = bf16[2,1024,640]{2,1,0:T(8,128)(2,1)S(1)} custom-call(bf16[256,2176]{1,0:T(8,128)(2,1)S(1)} %copy-done.3, bf16[1536,1536]{1,0:T(8,128)(2,1)S(1)} %copy-done, bf16[512,1024]{1,0:T(8,128)(2,1)S(1)} %copy-done.2, f32[256,128]{1,0:T(8,128)S(1)} %get-tuple-element.38.cos_ref, f32[256,128]{1,0:T(8,128)S(1)} %concatenate.39.low_ref, ...), custom_call_target="tpu_custom_call" | custom-call | flops 1000 | bytes 1000 | tf_op jit(solution)/shard_map/queries/pallas_call | solution.py:226
  85.5 5.7 %collective-permute-done.13.refs_10_ = bf16[8,64,640]{2,1,0:T(8,128)(2,1)} collective-permute-done((bf16[8,64,640]{2,1,0:T(8,128)(2,1)}, bf16[8,64,640]{2,1,0:T(8,128)(2,1)}, u32[]{:S(2)}, u32[]{:S(2)}) %collective-permute-start.13) | collective-permute-done | bytes 655392 | tf_op jit(solution)/shard_map/ppermute | solution.py:63
  91.2 2.9 %collective-permute-done.14.refs_11_ = bf16[8,64,640]{2,1,0:T(8,128)(2,1)} collective-permute-done((bf16[8,64,640]{2,1,0:T(8,128)(2,1)S(1)}, bf16[8,64,640]{2,1,0:T(8,128)(2,1)}, u32[]{:S(2)}, u32[]{:S(2)}) %collective-permute-start.14) | collective-permute-done | bytes 655392 | tf_op jit(solution)/shard_map/ppermute | solution.py:63
  96.0 4.4 %sum_first.1 = f32[4,704,128]{2,1,0:T(8,128)} custom-call(f32[4,4,704,128]{3,2,1,0:T(8,128)} %all-to-all-done.1.a_ref), custom_call_target="tpu_custom_call" | custom-call | flops 1000 | bytes 1000 | tf_op jit(solution)/shard_map/sum_first/pallas_call | solution.py:309
  100.5 4.4 %all-to-all-start.2 = ((f32[4,704,128]{2,1,0:T(8,128)}), f32[4,704,128]{2,1,0:T(8,128)S(1)}, u32[]{:S(2)}, u32[]{:S(2)}) async-start(f32[4,704,128]{2,1,0:T(8,128)} %sum_first.1), calls=%async_computation.2 | async-start | bytes 2883584 | tf_op jit(solution)/shard_map/all_to_all | solution.py:51
  104.9 37.4 %attention.1 = (bf16[256,1024]{1,0:T(8,128)(2,1)}, f32[8,128]{1,0:T(8,128)S(1)}) custom-call(s32[64]{0:T(128)S(1)} %pad_add_fusion.2.refs_0_, s32[2]{0:T(128)S(1)} %pad_add_fusion.3.refs_1_, s32[2]{0:T(128)S(1)} %fusion.2.refs_2_, bf16[2,1024,640]{2,1,0:T(8,128)(2,1)} %copy-done.1, bf16[512,1024]{1,0:T(8,128)(2,1)} %refs_4_.1, ...), custom_call_target="tpu_custom_call" | custom-call | flops 20000000000 | bytes 14680064 | tf_op jit(solution)/shard_map/attention/pallas_call | solution.py:149
  144.1 2.8 %moment_and_gram.1 = (f32[704,128]{1,0:T(8,128)}, f32[392,128]{1,0:T(8,128)}) custom-call(f32[4,704,128]{2,1,0:T(8,128)} %copy-done.5, f32[8,128]{1,0:T(8,128)} %copy-done.4), custom_call_target="tpu_custom_call" | custom-call | flops 1000 | bytes 1000 | tf_op jit(solution)/shard_map/moment_and_gram/pallas_call | solution.py:344
  147.5 2.2 %collective-permute-start.23 = (f32[392,128]{1,0:T(8,128)}, f32[392,128]{1,0:T(8,128)S(1)}, u32[]{:S(2)}, u32[]{:S(2)}) collective-permute-start(f32[392,128]{1,0:T(8,128)} %get-tuple-element.22.a_ref), channel_id=1, source_target_pairs={{0,64},{32,96},{64,0},{96,32},{1,65},{33,97},{65,1},{97,33},{2,66}... | collective-permute-start | bytes 602120 | tf_op jit(solution)/shard_map/ppermute | solution.py:55
  151.2 2.9 %collective-permute-done.22.b_ref = f32[392,128]{1,0:T(8,128)S(1)} collective-permute-done((f32[392,128]{1,0:T(8,128)}, f32[392,128]{1,0:T(8,128)S(1)}, u32[]{:S(2)}, u32[]{:S(2)}) %collective-permute-start.22) | collective-permute-done | bytes 200736 | tf_op jit(solution)/shard_map/ppermute | solution.py:55
  154.0 5.5 %collective-permute-done.23.c_ref = f32[392,128]{1,0:T(8,128)S(1)} collective-permute-done((f32[392,128]{1,0:T(8,128)}, f32[392,128]{1,0:T(8,128)S(1)}, u32[]{:S(2)}, u32[]{:S(2)}) %collective-permute-start.23) | collective-permute-done | bytes 200736 | tf_op jit(solution)/shard_map/ppermute | solution.py:55
  160.3 7.1 %newton.1 = f32[8,64,256]{2,1,0:T(8,128)} custom-call(f32[704,128]{1,0:T(8,128)} %get-tuple-element.21.m_ref, f32[392,128]{1,0:T(8,128)} %get-tuple-element.22.a_ref, f32[392,128]{1,0:T(8,128)} %copy-done.17, f32[392,128]{1,0:T(8,128)} %copy-done.18, f32[392,128]{1,0:T(8,128)} %copy-done.19), custom_call_target="tpu_custom_call" | custom-call | flops 1000 | bytes 1000 | tf_op jit(solution)/shard_map/newton/pallas_call | solution.py:420
  167.4 5.7 %all-to-all-start.3 = ((f32[8,64,256]{2,1,0:T(8,128)}), f32[8,64,256]{2,1,0:T(8,128)S(1)}, u32[]{:S(2)}, u32[]{:S(2)}) async-start(f32[8,64,256]{2,1,0:T(8,128)} %newton.1), calls=%async_computation.3 | async-start | bytes 1048576 | tf_op jit(solution)/shard_map/all_to_all | solution.py:576
  176.0 5.2 %all-to-all-done.3.step_ref = f32[8,64,256]{2,1,0:T(8,128)S(1)} async-done(((f32[8,64,256]{2,1,0:T(8,128)}), f32[8,64,256]{2,1,0:T(8,128)S(1)}, u32[]{:S(2)}, u32[]{:S(2)}) %all-to-all-start.3) | async-done | bytes 524320 | tf_op jit(solution)/shard_map/all_to_all | solution.py:576
  182.0 2.1 %update.1 = (f32[48,1536]{1,0:T(8,128)}, f32[16,1024]{1,0:T(8,128)}, f32[48,1536]{1,0:T(8,128)}, f32[16,1024]{1,0:T(8,128)}, f32[8,128]{1,0:T(8,128)}) custom-call(f32[8,64,256]{2,1,0:T(8,128)} %copy-done.8, bf16[48,1536]{1,0:T(8,128)(2,1)} %constant_dynamic-slice_fusion.1.wq_ref, bf16[16,1024]{1,0:T(8,128)(2,1)} %constant_dynamic-slice_fusion.wk_ref, s32[8]{0:T(128)} %flag_ref.1), custom_call_target="tpu_custom_call" | custom-call | flops 1000 | bytes 1000 | tf_op jit(solution)/shard_map/update/pallas_call | solution.py:476
  (122 shorter events, 29.3 us)
Async XLA Ops:
  1.7 35.9 %collective-permute-start.2 = (bf16[64,2176]{1,0:T(8,128)(2,1)S(1)}, bf16[64,2176]{1,0:T(8,128)(2,1)S(1)}, u32[]{:S(2)}, u32[]{:S(2)}) collective-permute-start(bf16[64,2176]{1,0:T(8,128)(2,1)S(1)} %concatenate.37.rest_0_), channel_id=1, source_target_pairs={{0,4},{2,6},{4,0},{6,2},{1,5},{3,7},{5,1},{7,3},{8,12},{10,14},{12... | collective-permute-start | bytes 835592 | tf_op jit(solution)/shard_map/ppermute | solution.py:63
  2.5 35.6 %collective-permute-start.3 = (bf16[64,2176]{1,0:T(8,128)(2,1)S(1)}, bf16[64,2176]{1,0:T(8,128)(2,1)S(1)}, u32[]{:S(2)}, u32[]{:S(2)}) collective-permute-start(bf16[64,2176]{1,0:T(8,128)(2,1)S(1)} %concatenate.37.rest_0_), channel_id=1, source_target_pairs={{0,2},{2,0},{4,6},{6,4},{1,3},{3,1},{5,7},{7,5},{8,10},{10,8},{12,... | collective-permute-start | bytes 835592 | tf_op jit(solution)/shard_map/ppermute | solution.py:63
  3.4 36.8 %collective-permute-start.4 = (bf16[64,2176]{1,0:T(8,128)(2,1)S(1)}, bf16[64,2176]{1,0:T(8,128)(2,1)}, u32[]{:S(2)}, u32[]{:S(2)}) collective-permute-start(bf16[64,2176]{1,0:T(8,128)(2,1)S(1)} %concatenate.37.rest_0_), channel_id=1, source_target_pairs={{0,6},{2,4},{4,2},{6,0},{1,7},{3,5},{5,3},{7,1},{8,14},{10,12},{12... | collective-permute-start | bytes 835592 | tf_op jit(solution)/shard_map/ppermute | solution.py:63
  8.7 31.9 %all-to-all-start = ((bf16[16,64,640]{2,1,0:T(8,128)(2,1)}), bf16[16,64,640]{2,1,0:T(8,128)(2,1)}, u32[]{:S(2)}, u32[]{:S(2)}) async-start(bf16[16,64,640]{2,1,0:T(8,128)(2,1)} %broadcast_in_dim.81), calls=%async_computation | async-start | bytes 2621440 | tf_op jit(solution)/shard_map/all_to_all | solution.py:539
  17.8 28.7 %collective-permute-start = (bf16[256,1280]{1,0:T(8,128)(2,1)}, bf16[256,1280]{1,0:T(8,128)(2,1)S(1)}, u32[]{:S(2)}, u32[]{:S(2)}) collective-permute-start(bf16[256,1280]{1,0:T(8,128)(2,1)} %pad_maximum_fusion), channel_id=1, source_target_pairs={{0,4},{4,0},{1,5},{5,1},{2,6},{6,2},{3,7},{7,3},{8,12},{12,8},{9,1... | collective-permute-start | bytes 1966088 | tf_op jit(solution)/shard_map/ppermute | solution.py:535
  17.9 19.7 %collective-permute-start.1 = (f32[64,768]{1,0:T(8,128)S(1)}, f32[64,768]{1,0:T(8,128)S(1)}, u32[]{:S(2)}, u32[]{:S(2)}) collective-permute-start(f32[64,768]{1,0:T(8,128)S(1)} %select_maximum_fusion), channel_id=1, source_target_pairs={{0,4},{4,0},{1,5},{5,1},{2,6},{6,2},{3,7},{7,3},{8,12},{12,8},{9,1... | collective-permute-start | bytes 589832 | tf_op jit(solution)/shard_map/ppermute | solution.py:538
  42.9 32.7 %collective-permute-start.11 = (bf16[8,64,640]{2,1,0:T(8,128)(2,1)S(1)}, bf16[8,64,640]{2,1,0:T(8,128)(2,1)S(1)}, u32[]{:S(2)}, u32[]{:S(2)}) collective-permute-start(bf16[8,64,640]{2,1,0:T(8,128)(2,1)S(1)} %get-tuple-element.32), channel_id=1, source_target_pairs={{0,4},{2,6},{4,0},{6,2},{1,5},{3,7},{5,1},{7,3},{8,12},{10,14},{12... | collective-permute-start | bytes 1966088 | tf_op jit(solution)/shard_map/ppermute | solution.py:63
  43.3 33.3 %collective-permute-start.12 = (bf16[8,64,640]{2,1,0:T(8,128)(2,1)S(1)}, bf16[8,64,640]{2,1,0:T(8,128)(2,1)}, u32[]{:S(2)}, u32[]{:S(2)}) collective-permute-start(bf16[8,64,640]{2,1,0:T(8,128)(2,1)S(1)} %get-tuple-element.32), channel_id=1, source_target_pairs={{0,6},{2,4},{4,2},{6,0},{1,7},{3,5},{5,3},{7,1},{8,14},{10,12},{12... | collective-permute-start | bytes 1966088 | tf_op jit(solution)/shard_map/ppermute | solution.py:63
  43.6 31.6 %collective-permute-start.10 = (bf16[8,64,640]{2,1,0:T(8,128)(2,1)}, bf16[8,64,640]{2,1,0:T(8,128)(2,1)}, u32[]{:S(2)}, u32[]{:S(2)}) collective-permute-start(bf16[8,64,640]{2,1,0:T(8,128)(2,1)} %get-tuple-element.33), channel_id=1, source_target_pairs={{0,6},{2,4},{4,2},{6,0},{1,7},{3,5},{5,3},{7,1},{8,14},{10,12},{12... | collective-permute-start | bytes 1966088 | tf_op jit(solution)/shard_map/ppermute | solution.py:63
  54.7 41.4 %all-to-all-start.1 = ((f32[4,4,704,128]{3,2,1,0:T(8,128)}), f32[4,4,704,128]{3,2,1,0:T(8,128)}, u32[]{:S(2)}, u32[]{:S(2)}) async-start(f32[4,4,704,128]{3,2,1,0:T(8,128)} %get-tuple-element.19), calls=%async_computation.1 | async-start | bytes 11534336 | tf_op jit(solution)/shard_map/all_to_all | solution.py:51
  60.7 24.4 %collective-permute-start.9 = (bf16[8,64,640]{2,1,0:T(8,128)(2,1)}, bf16[8,64,640]{2,1,0:T(8,128)(2,1)}, u32[]{:S(2)}, u32[]{:S(2)}) collective-permute-start(bf16[8,64,640]{2,1,0:T(8,128)(2,1)} %get-tuple-element.33), channel_id=1, source_target_pairs={{0,4},{2,6},{4,0},{6,2},{1,5},{3,7},{5,1},{7,3},{8,12},{10,14},{12... | collective-permute-start | bytes 1966088 | tf_op jit(solution)/shard_map/ppermute | solution.py:63
  75.2 16.0 %collective-permute-start.13 = (bf16[8,64,640]{2,1,0:T(8,128)(2,1)}, bf16[8,64,640]{2,1,0:T(8,128)(2,1)}, u32[]{:S(2)}, u32[]{:S(2)}) collective-permute-start(bf16[8,64,640]{2,1,0:T(8,128)(2,1)} %collective-permute-done.10.refs_1_.refs_7_), channel_id=1, source_target_pairs={{0,4},{2,6},{4,0},{6,2},{1,5},{3,7},{5,1},{7,3},{8,12},{10,14},{12... | collective-permute-start | bytes 1966088 | tf_op jit(solution)/shard_map/ppermute | solution.py:63
  75.6 18.5 %collective-permute-start.17 = (bf16[8,64,640]{2,1,0:T(8,128)(2,1)}, bf16[8,64,640]{2,1,0:T(8,128)(2,1)}, u32[]{:S(2)}, u32[]{:S(2)}) collective-permute-start(bf16[8,64,640]{2,1,0:T(8,128)(2,1)} %collective-permute-done.10.refs_1_.refs_7_), channel_id=1, source_target_pairs={{0,1},{1,0},{2,3},{3,2},{4,5},{5,4},{6,7},{7,6},{8,9},{9,8},{10,11... | collective-permute-start | bytes 1966088 | tf_op jit(solution)/shard_map/ppermute | solution.py:67
  75.6 18.5 %collective-permute-start.14 = (bf16[8,64,640]{2,1,0:T(8,128)(2,1)S(1)}, bf16[8,64,640]{2,1,0:T(8,128)(2,1)}, u32[]{:S(2)}, u32[]{:S(2)}) collective-permute-start(bf16[8,64,640]{2,1,0:T(8,128)(2,1)S(1)} %collective-permute-done.11.refs_2_.refs_8_), channel_id=1, source_target_pairs={{0,6},{2,4},{4,2},{6,0},{1,7},{3,5},{5,3},{7,1},{8,14},{10,12},{12... | collective-permute-start | bytes 1966088 | tf_op jit(solution)/shard_map/ppermute | solution.py:63
  76.5 18.1 %collective-permute-start.18 = (bf16[8,64,640]{2,1,0:T(8,128)(2,1)S(1)}, bf16[8,64,640]{2,1,0:T(8,128)(2,1)}, u32[]{:S(2)}, u32[]{:S(2)}) collective-permute-start(bf16[8,64,640]{2,1,0:T(8,128)(2,1)S(1)} %collective-permute-done.11.refs_2_.refs_8_), channel_id=1, source_target_pairs={{0,1},{1,0},{2,3},{3,2},{4,5},{5,4},{6,7},{7,6},{8,9},{9,8},{10,11... | collective-permute-start | bytes 1966088 | tf_op jit(solution)/shard_map/ppermute | solution.py:67
  85.1 19.7 %collective-permute-start.15 = (bf16[16,64,640]{2,1,0:T(8,128)(2,1)}, bf16[16,64,640]{2,1,0:T(8,128)(2,1)}, u32[]{:S(2)}, u32[]{:S(2)}) collective-permute-start(bf16[16,64,640]{2,1,0:T(8,128)(2,1)} %all-to-all-done.refs_5_), channel_id=1, source_target_pairs={{0,1},{1,0},{2,3},{3,2},{4,5},{5,4},{6,7},{7,6},{8,9},{9,8},{10,11... | collective-permute-start | bytes 3932168 | tf_op jit(solution)/shard_map/ppermute | solution.py:67
  91.2 13.6 %collective-permute-start.16 = (bf16[8,64,640]{2,1,0:T(8,128)(2,1)}, bf16[8,64,640]{2,1,0:T(8,128)(2,1)}, u32[]{:S(2)}, u32[]{:S(2)}) collective-permute-start(bf16[8,64,640]{2,1,0:T(8,128)(2,1)} %collective-permute-done.9.refs_0_.refs_6_), channel_id=1, source_target_pairs={{0,1},{1,0},{2,3},{3,2},{4,5},{5,4},{6,7},{7,6},{8,9},{9,8},{10,11... | collective-permute-start | bytes 1966088 | tf_op jit(solution)/shard_map/ppermute | solution.py:67
  94.1 10.8 %collective-permute-start.19 = (bf16[8,64,640]{2,1,0:T(8,128)(2,1)}, bf16[8,64,640]{2,1,0:T(8,128)(2,1)}, u32[]{:S(2)}, u32[]{:S(2)}) collective-permute-start(bf16[8,64,640]{2,1,0:T(8,128)(2,1)} %collective-permute-done.12.refs_3_.refs_9_), channel_id=1, source_target_pairs={{0,1},{1,0},{2,3},{3,2},{4,5},{5,4},{6,7},{7,6},{8,9},{9,8},{10,11... | collective-permute-start | bytes 1966088 | tf_op jit(solution)/shard_map/ppermute | solution.py:67
  94.1 10.8 %collective-permute-start.20 = (bf16[8,64,640]{2,1,0:T(8,128)(2,1)}, bf16[8,64,640]{2,1,0:T(8,128)(2,1)}, u32[]{:S(2)}, u32[]{:S(2)}) collective-permute-start(bf16[8,64,640]{2,1,0:T(8,128)(2,1)} %collective-permute-done.13.refs_10_), channel_id=1, source_target_pairs={{0,1},{1,0},{2,3},{3,2},{4,5},{5,4},{6,7},{7,6},{8,9},{9,8},{10,11... | collective-permute-start | bytes 1966088 | tf_op jit(solution)/shard_map/ppermute | solution.py:67
  94.6 10.3 %collective-permute-start.21 = (bf16[8,64,640]{2,1,0:T(8,128)(2,1)}, bf16[8,64,640]{2,1,0:T(8,128)(2,1)}, u32[]{:S(2)}, u32[]{:S(2)}) collective-permute-start(bf16[8,64,640]{2,1,0:T(8,128)(2,1)} %collective-permute-done.14.refs_11_), channel_id=1, source_target_pairs={{0,1},{1,0},{2,3},{3,2},{4,5},{5,4},{6,7},{7,6},{8,9},{9,8},{10,11... | collective-permute-start | bytes 1966088 | tf_op jit(solution)/shard_map/ppermute | solution.py:67
  100.5 42.4 %all-to-all-start.2 = ((f32[4,704,128]{2,1,0:T(8,128)}), f32[4,704,128]{2,1,0:T(8,128)S(1)}, u32[]{:S(2)}, u32[]{:S(2)}) async-start(f32[4,704,128]{2,1,0:T(8,128)} %sum_first.1), calls=%async_computation.2 | async-start | bytes 2883584 | tf_op jit(solution)/shard_map/all_to_all | solution.py:51
  147.5 12.1 %collective-permute-start.23 = (f32[392,128]{1,0:T(8,128)}, f32[392,128]{1,0:T(8,128)S(1)}, u32[]{:S(2)}, u32[]{:S(2)}) collective-permute-start(f32[392,128]{1,0:T(8,128)} %get-tuple-element.22.a_ref), channel_id=1, source_target_pairs={{0,64},{32,96},{64,0},{96,32},{1,65},{33,97},{65,1},{97,33},{2,66}... | collective-permute-start | bytes 602120 | tf_op jit(solution)/shard_map/ppermute | solution.py:55
  149.7 9.8 %collective-permute-start.24 = (f32[392,128]{1,0:T(8,128)}, f32[392,128]{1,0:T(8,128)S(1)}, u32[]{:S(2)}, u32[]{:S(2)}) collective-permute-start(f32[392,128]{1,0:T(8,128)} %get-tuple-element.22.a_ref), channel_id=1, source_target_pairs={{0,96},{32,0},{64,32},{96,64},{1,97},{33,1},{65,33},{97,65},{2,98}... | collective-permute-start | bytes 602120 | tf_op jit(solution)/shard_map/ppermute | solution.py:55
  167.4 13.8 %all-to-all-start.3 = ((f32[8,64,256]{2,1,0:T(8,128)}), f32[8,64,256]{2,1,0:T(8,128)S(1)}, u32[]{:S(2)}, u32[]{:S(2)}) async-start(f32[8,64,256]{2,1,0:T(8,128)} %newton.1), calls=%async_computation.3 | async-start | bytes 1048576 | tf_op jit(solution)/shard_map/all_to_all | solution.py:576
  (27 other events, 131.7 us)

commit v4 on v3

--- a/solution.py
+++ b/solution.py
@@ -349,6 +349,7 @@
         ),
         in_specs=[VMEM, VMEM],
         out_specs=(VMEM, VMEM),
+        compiler_params=pltpu.CompilerParams(vmem_limit_bytes=16 * 2**20),
         cost_estimate=pl.CostEstimate(flops=1000, bytes_accessed=1000, transcendentals=0),
         name="moment_and_gram",
     )(parts, peaks)
@@ -358,22 +359,32 @@
     return jnp.dot(a, b, precision=FULL, preferred_element_type=F32)
 
 
-def newton_factor(gram):
-    size = gram.shape[0]
-    eye = (
-        lax.broadcasted_iota(jnp.int32, (size, size), 0)
-        == lax.broadcasted_iota(jnp.int32, (size, size), 1)
-    ).astype(F32)
-    square = jnp.sum(jnp.sum(gram * eye, axis=1, keepdims=True), axis=0, keepdims=True)
-    inverse = 1.0 / (jnp.sqrt(square) + 1e-07)
-    a = gram * inverse * inverse
-    product = None
+def newton_factors(grams):
+    eyes, inverses, a = [], [], []
+    for gram in grams:
+        size = gram.shape[0]
+        eye = (
+            lax.broadcasted_iota(jnp.int32, (size, size), 0)
+            == lax.broadcasted_iota(jnp.int32, (size, size), 1)
+        ).astype(F32)
+        square = jnp.sum(jnp.sum(gram * eye, axis=1, keepdims=True), axis=0, keepdims=True)
+        inverse = 1.0 / (jnp.sqrt(square) + 1e-07)
+        eyes.append(eye)
+        inverses.append(inverse)
+        a.append(gram * inverse * inverse)
+    pairs = range(len(grams))
+    products = None
     for step in range(NS_STEPS):
-        factor = NS_A * eye + NS_B * a + NS_C * full_dot(a, a)
-        product = factor if product is None else full_dot(product, factor)
+        squares = [full_dot(a[i], a[i]) for i in pairs]
+        factors = [NS_A * eyes[i] + NS_B * a[i] + NS_C * squares[i] for i in pairs]
         if step + 1 < NS_STEPS:
-            a = full_dot(full_dot(factor, a), factor)
-    return product * inverse
+            halfway = [full_dot(factors[i], a[i]) for i in pairs]
+            a = [full_dot(halfway[i], factors[i]) for i in pairs]
+        if products is None:
+            products = factors
+        else:
+            products = [full_dot(products[i], factors[i]) for i in pairs]
+    return [products[i] * inverses[i] for i in pairs]
 
 
 def newton_kernel(m_ref, a_ref, b_ref, c_ref, d_ref, *rest):
@@ -391,8 +402,9 @@
         ],
         axis=0,
     )
-    factor_q = newton_factor(gram_q) * (0.2 * math.sqrt(QR))
-    factor_k = newton_factor(gram[128:256, :]) * (0.2 * math.sqrt(KVR))
+    factor_q, factor_k = newton_factors([gram_q, gram[128:256, :]])
+    factor_q = factor_q * (0.2 * math.sqrt(QR))
+    factor_k = factor_k * (0.2 * math.sqrt(KVR))
     rows = []
     for t in range(3):
         block = m_ref[t * HEAD : (t + 1) * HEAD, :]
@@ -422,6 +434,7 @@
         out_shape=jax.ShapeDtypeStruct((8, 64, 256), F32),
         in_specs=[VMEM] * 5 + [ANY] * len(ties),
         out_specs=VMEM,
+        compiler_params=pltpu.CompilerParams(vmem_limit_bytes=16 * 2**20),
         cost_estimate=pl.CostEstimate(flops=1000, bytes_accessed=1000, transcendentals=0),
         name="newton",
     )(moment, *grams, *ties)
@@ -431,7 +444,10 @@
     peaks = step_ref[0, 48:56, 128:]
     for source in range(1, 8):
         peaks = jnp.maximum(peaks, step_ref[source, 48:56, 128:])
-    peak_ref[...] = peaks
+    on_diagonal = lax.broadcasted_iota(jnp.int32, (8, 128), 0) == lax.broadcasted_iota(
+        jnp.int32, (8, 128), 1
+    )
+    peak_ref[...] = jnp.sum(jnp.where(on_diagonal, peaks, 0.0), axis=0, keepdims=True)[:, :8]
     ratio = CLIP_TAU / jnp.maximum(peaks, CLIP_TAU)
     gamma = jnp.concatenate(
         [jnp.where(flag_ref[h] > 0, ratio[h : h + 1], 1.0) for h in range(8)], axis=0
@@ -472,12 +488,13 @@
 
 
 def update(steps, owned_query, owned_key, flags):
-    shapes = ((48, QR), (16, 1024), (48, QR), (16, 1024), (8, 128))
+    shapes = ((48, QR), (16, 1024), (48, QR), (16, 1024), (1, 8))
     return pl.pallas_call(
         update_kernel,
         out_shape=tuple(jax.ShapeDtypeStruct(shape, F32) for shape in shapes),
         in_specs=[VMEM] * 3 + [SMEM],
         out_specs=tuple(VMEM for _ in shapes),
+        compiler_params=pltpu.CompilerParams(vmem_limit_bytes=16 * 2**20),
         cost_estimate=pl.CostEstimate(flops=1000, bytes_accessed=1000, transcendentals=0),
         name="update",
     )(steps, owned_query, owned_key, flags)
@@ -580,7 +597,7 @@
         lax.dynamic_slice_in_dim(w_key, ctx * 16, 16, 0),
         clip_flags,
     )
-    return (attn_out, head_peaks[:, 0], step_query, step_key, new_query, new_key)
+    return (attn_out, head_peaks.reshape(8), step_query, step_key, new_query, new_key)
 
 
 def solution(mesh):

time: 186 us -> 177 us (0.952)
  local copies, waits for them, and re-layouts: 19.4 us -> 12.7 us
  Pallas kernels: 64.1 us -> 58.8 us
  waiting for transfers between devices: 54.2 us -> 56.9 us
    unnamed x44 -> x32, local copies, waits for them, and re-layouts: 9.02 us -> 5.53 us
    ppermute x9, waiting for transfers between devices: 22.5 us -> 25 us  [flip(): return lax.ppermute(value, ('yl', 'yh'), pairs)]
    pallas_call x1, Pallas kernels: 7.09 us -> 4.9 us  [newton(): pl.pallas_call(newton_kernel, out_shape=jax.ShapeDtypeStruct((8, 64, 256)...]
    pallas_call x1, Pallas kernels: 2.82 us -> 0.77 us  [moment_and_gram(): pl.pallas_call(gram_kernel, out_shape=(jax.ShapeDtypeStruct((704, 128), F...]
    all_to_all x1, waiting for transfers between devices: 5.17 us -> 7.12 us  [shards(): steps = lax.all_to_all(steps, ('x', 'yl'), 0, 0)]
  transfers between devices with their start and end apart: 29 -> 29, of which waited for: 8 -> 7; matrix products, arithmetic and copies ran while one was open for 7% -> 6% of each run, Pallas kernels for 28% -> 29%
where the time goes in v4:
time: 177 us; the launch traced here: 176 us
  Pallas kernels  58.8 us (33%)
  waiting for transfers between devices  56.9 us (32%)
  starting transfers between devices  43 us (24%)
  local copies, waits for them, and re-layouts  12.7 us (7%)
  other arithmetic  3.79 us (2%)
    pallas_call x1, Pallas kernels, attention(): pl.pallas_call(functools.partial(attention_kernel, head0, heads, len(piec...  37.1 us
    ppermute x9, waiting for transfers between devices, flip(): return lax.ppermute(value, ('yl', 'yh'), pairs)  25 us
    ppermute x1, waiting for transfers between devices, shards(): m_other = lax.ppermute(m_other, 'yl', [(0, 1), (1, 0)])  16.6 us
    ppermute x9, starting transfers between devices, flip(): return lax.ppermute(value, ('yl', 'yh'), pairs)  10.3 us
    all_to_all x2, starting transfers between devices, exchange(): lax.all_to_all(value, ('z', 'x', 'c'), 0, 0, axis_index_groups=groups)  9.64 us
    ppermute x3, waiting for transfers between devices, move_z(): return lax.ppermute(value, 'z', [(i, (i + k) % 4) for i in range(4)])  8.12 us
    all_to_all x1, starting transfers between devices, shards(): lax.all_to_all(jnp.broadcast_to(key_rows[None], (16, 64, WIDE)), ('z', 'x...  8.05 us
    pallas_call x1, Pallas kernels, gradient_terms(): pl.pallas_call(gradient_kernel, out_shape=(jax.ShapeDtypeStruct((4, 4, 70...  7.27 us
  transfers between devices with their start and end apart: 29, of which 7 were waited for; matrix products, arithmetic and copies ran while one was open for 6% of the time, Pallas kernels for 29%

profile of v4, /device:TPU:24, one launch (start us, length us, event | category | flops | bytes accessed | tf_op | source)
XLA Modules:
  0.0 176.3 jit_solution(16970823453394647906)
XLA Ops:
  3.4 3.1 %collective-permute-start.4 = (bf16[64,2176]{1,0:T(8,128)(2,1)S(1)}, bf16[64,2176]{1,0:T(8,128)(2,1)}, u32[]{:S(2)}, u32[]{:S(2)}) collective-permute-start(bf16[64,2176]{1,0:T(8,128)(2,1)S(1)} %concatenate.37.rest_0_), channel_id=1, source_target_pairs={{0,6},{2,4},{4,2},{6,0},{1,7},{3,5},{5,3},{7,1},{8,14},{10,12},{12... | collective-permute-start | bytes 835592 | tf_op jit(solution)/shard_map/ppermute | solution.py:63
  8.7 8.1 %all-to-all-start = ((bf16[16,64,640]{2,1,0:T(8,128)(2,1)}), bf16[16,64,640]{2,1,0:T(8,128)(2,1)}, u32[]{:S(2)}, u32[]{:S(2)}) async-start(bf16[16,64,640]{2,1,0:T(8,128)(2,1)} %broadcast_in_dim.81), calls=%async_computation | async-start | bytes 2621440 | tf_op jit(solution)/shard_map/all_to_all | solution.py:556
  20.0 16.6 %collective-permute-done.1.m_other = f32[64,768]{1,0:T(8,128)S(1)} collective-permute-done((f32[64,768]{1,0:T(8,128)S(1)}, f32[64,768]{1,0:T(8,128)S(1)}, u32[]{:S(2)}, u32[]{:S(2)}) %collective-permute-start.1) | collective-permute-done | bytes 196640 | tf_op jit(solution)/shard_map/ppermute | solution.py:555
  39.6 2.4 %fusion.8 = (bf16[8,64,640]{2,1,0:T(8,128)(2,1)}, bf16[8,64,640]{2,1,0:T(8,128)(2,1)}) fusion(bf16[16,64,640]{2,1,0:T(8,128)(2,1)} %all-to-all-done.refs_5_), kind=kLoop, calls=%fused_computation.50 | loop fusion | bytes 2621440 | tf_op jit(solution)/shard_map/slice | solution.py:559
  42.8 2.9 %collective-permute-start.10 = (bf16[8,64,640]{2,1,0:T(8,128)(2,1)}, bf16[8,64,640]{2,1,0:T(8,128)(2,1)}, u32[]{:S(2)}, u32[]{:S(2)}) collective-permute-start(bf16[8,64,640]{2,1,0:T(8,128)(2,1)} %get-tuple-element.33), channel_id=1, source_target_pairs={{0,6},{2,4},{4,2},{6,0},{1,7},{3,5},{5,3},{7,1},{8,14},{10,12},{12... | collective-permute-start | bytes 1966088 | tf_op jit(solution)/shard_map/ppermute | solution.py:63
  46.6 7.3 %gradient_terms.1 = (f32[4,4,704,128]{3,2,1,0:T(8,128)}, bf16[256,2176]{1,0:T(8,128)(2,1)}) custom-call(s32[5]{0:T(128)} %stack.35.at_ref, bf16[256,1536]{1,0:T(8,128)(2,1)} %gq_ref.1, bf16[256,1024]{1,0:T(8,128)(2,1)} %gk_ref.1, bf16[256,1280]{1,0:T(8,128)(2,1)} %copy-done.9, f32[48,1536]{1,0:T(8,128)} %mq_ref.1, f32[16,1024]{1,0:T(8,128)} %mk_ref.1, ...), custom_call_target="tpu_custom_call" | custom-call | flops 1000 | bytes 1000 | tf_op jit(solution)/shard_map/gradient_terms/pallas_call | solution.py:283
  53.9 5.3 %all-to-all-start.1 = ((f32[4,4,704,128]{3,2,1,0:T(8,128)}), f32[4,4,704,128]{3,2,1,0:T(8,128)}, u32[]{:S(2)}, u32[]{:S(2)}) async-start(f32[4,4,704,128]{3,2,1,0:T(8,128)} %get-tuple-element.19), calls=%async_computation.1 | async-start | bytes 11534336 | tf_op jit(solution)/shard_map/all_to_all | solution.py:51
  60.7 13.9 %collective-permute-done.10.refs_1_.refs_7_ = bf16[8,64,640]{2,1,0:T(8,128)(2,1)} collective-permute-done((bf16[8,64,640]{2,1,0:T(8,128)(2,1)}, bf16[8,64,640]{2,1,0:T(8,128)(2,1)}, u32[]{:S(2)}, u32[]{:S(2)}) %collective-permute-start.10) | collective-permute-done | bytes 655392 | tf_op jit(solution)/shard_map/ppermute | solution.py:63
  76.8 2.3 %copy-done = bf16[1536,1536]{1,0:T(8,128)(2,1)S(1)} copy-done((bf16[1536,1536]{1,0:T(8,128)(2,1)S(1)}, bf16[1536,1536]{1,0:T(8,128)(2,1)}, u32[]{:S(2)}) %copy-start) | copy-done | bytes 4718616
  79.2 2.9 %queries.1.refs_4_.refs_3_ = bf16[2,1024,640]{2,1,0:T(8,128)(2,1)S(1)} custom-call(bf16[256,2176]{1,0:T(8,128)(2,1)S(1)} %copy-done.3, bf16[1536,1536]{1,0:T(8,128)(2,1)S(1)} %copy-done, bf16[512,1024]{1,0:T(8,128)(2,1)S(1)} %copy-done.2, f32[256,128]{1,0:T(8,128)S(1)} %get-tuple-element.38.cos_ref, f32[256,128]{1,0:T(8,128)S(1)} %concatenate.39.low_ref, ...), custom_call_target="tpu_custom_call" | custom-call | flops 1000 | bytes 1000 | tf_op jit(solution)/shard_map/queries/pallas_call | solution.py:226
  82.4 8.2 %collective-permute-done.13.refs_10_ = bf16[8,64,640]{2,1,0:T(8,128)(2,1)} collective-permute-done((bf16[8,64,640]{2,1,0:T(8,128)(2,1)}, bf16[8,64,640]{2,1,0:T(8,128)(2,1)}, u32[]{:S(2)}, u32[]{:S(2)}) %collective-permute-start.13) | collective-permute-done | bytes 655392 | tf_op jit(solution)/shard_map/ppermute | solution.py:63
  90.6 2.9 %collective-permute-done.14.refs_11_ = bf16[8,64,640]{2,1,0:T(8,128)(2,1)} collective-permute-done((bf16[8,64,640]{2,1,0:T(8,128)(2,1)S(1)}, bf16[8,64,640]{2,1,0:T(8,128)(2,1)}, u32[]{:S(2)}, u32[]{:S(2)}) %collective-permute-start.14) | collective-permute-done | bytes 655392 | tf_op jit(solution)/shard_map/ppermute | solution.py:63
  94.1 1.5 copy-done.1
  95.6 4.4 %sum_first.1 = f32[4,704,128]{2,1,0:T(8,128)} custom-call(f32[4,4,704,128]{3,2,1,0:T(8,128)} %all-to-all-done.1.a_ref), custom_call_target="tpu_custom_call" | custom-call | flops 1000 | bytes 1000 | tf_op jit(solution)/shard_map/sum_first/pallas_call | solution.py:309
  100.0 4.4 %all-to-all-start.2 = ((f32[4,704,128]{2,1,0:T(8,128)}), f32[4,704,128]{2,1,0:T(8,128)S(1)}, u32[]{:S(2)}, u32[]{:S(2)}) async-start(f32[4,704,128]{2,1,0:T(8,128)} %sum_first.1), calls=%async_computation.2 | async-start | bytes 2883584 | tf_op jit(solution)/shard_map/all_to_all | solution.py:51
  104.4 37.1 %attention.1 = (bf16[256,1024]{1,0:T(8,128)(2,1)}, f32[8,128]{1,0:T(8,128)S(1)}) custom-call(s32[64]{0:T(128)S(1)} %pad_add_fusion.2.refs_0_, s32[2]{0:T(128)S(1)} %pad_add_fusion.3.refs_1_, s32[2]{0:T(128)S(1)} %fusion.2.refs_2_, bf16[2,1024,640]{2,1,0:T(8,128)(2,1)} %copy-done.1, bf16[512,1024]{1,0:T(8,128)(2,1)} %refs_4_.1, ...), custom_call_target="tpu_custom_call" | custom-call | flops 20000000000 | bytes 14680064 | tf_op jit(solution)/shard_map/attention/pallas_call | solution.py:149
  142.4 1.5 collective-permute-start.22
  143.9 2.7 %collective-permute-start.23 = (f32[392,128]{1,0:T(8,128)S(1)}, f32[392,128]{1,0:T(8,128)S(1)}, u32[]{:S(2)}, u32[]{:S(2)}) collective-permute-start(f32[392,128]{1,0:T(8,128)S(1)} %get-tuple-element.22.a_ref), channel_id=1, source_target_pairs={{0,64},{32,96},{64,0},{96,32},{1,65},{33,97},{65,1},{97,33},{2,66}... | collective-permute-start | bytes 602120 | tf_op jit(solution)/shard_map/ppermute | solution.py:55
  146.6 1.6 collective-permute-start.24
  148.2 2.6 %collective-permute-done.22.b_ref = f32[392,128]{1,0:T(8,128)S(1)} collective-permute-done((f32[392,128]{1,0:T(8,128)S(1)}, f32[392,128]{1,0:T(8,128)S(1)}, u32[]{:S(2)}, u32[]{:S(2)}) %collective-permute-start.22) | collective-permute-done | bytes 200736 | tf_op jit(solution)/shard_map/ppermute | solution.py:55
  150.8 5.5 %collective-permute-done.23.c_ref = f32[392,128]{1,0:T(8,128)S(1)} collective-permute-done((f32[392,128]{1,0:T(8,128)S(1)}, f32[392,128]{1,0:T(8,128)S(1)}, u32[]{:S(2)}, u32[]{:S(2)}) %collective-permute-start.23) | collective-permute-done | bytes 200736 | tf_op jit(solution)/shard_map/ppermute | solution.py:55
  156.3 4.9 %newton.1 = f32[8,64,256]{2,1,0:T(8,128)} custom-call(f32[704,128]{1,0:T(8,128)S(1)} %get-tuple-element.21.m_ref, f32[392,128]{1,0:T(8,128)S(1)} %get-tuple-element.22.a_ref, f32[392,128]{1,0:T(8,128)S(1)} %collective-permute-done.22.b_ref, f32[392,128]{1,0:T(8,128)S(1)} %collective-permute-done.23.c_ref, f32[392,128]{1,0:T(8,128)S(1)} %collective-permute-done.24.d_ref), custom_call_target="tpu_custom_call" | custom-call | flops 1000 | bytes 1000 | tf_op jit(solution)/shard_map/newton/pallas_call | solution.py:432
  161.2 5.6 %all-to-all-start.3 = ((f32[8,64,256]{2,1,0:T(8,128)}), f32[8,64,256]{2,1,0:T(8,128)S(1)}, u32[]{:S(2)}, u32[]{:S(2)}) async-start(f32[8,64,256]{2,1,0:T(8,128)} %newton.1), calls=%async_computation.3 | async-start | bytes 1048576 | tf_op jit(solution)/shard_map/all_to_all | solution.py:593
  167.7 7.1 %all-to-all-done.3.step_ref = f32[8,64,256]{2,1,0:T(8,128)S(1)} async-done(((f32[8,64,256]{2,1,0:T(8,128)}), f32[8,64,256]{2,1,0:T(8,128)S(1)}, u32[]{:S(2)}, u32[]{:S(2)}) %all-to-all-start.3) | async-done | bytes 524320 | tf_op jit(solution)/shard_map/all_to_all | solution.py:593
  (109 shorter events, 20.5 us)
Async XLA Ops:
  1.7 34.9 %collective-permute-start.2 = (bf16[64,2176]{1,0:T(8,128)(2,1)S(1)}, bf16[64,2176]{1,0:T(8,128)(2,1)S(1)}, u32[]{:S(2)}, u32[]{:S(2)}) collective-permute-start(bf16[64,2176]{1,0:T(8,128)(2,1)S(1)} %concatenate.37.rest_0_), channel_id=1, source_target_pairs={{0,4},{2,6},{4,0},{6,2},{1,5},{3,7},{5,1},{7,3},{8,12},{10,14},{12... | collective-permute-start | bytes 835592 | tf_op jit(solution)/shard_map/ppermute | solution.py:63
  2.5 34.6 %collective-permute-start.3 = (bf16[64,2176]{1,0:T(8,128)(2,1)S(1)}, bf16[64,2176]{1,0:T(8,128)(2,1)}, u32[]{:S(2)}, u32[]{:S(2)}) collective-permute-start(bf16[64,2176]{1,0:T(8,128)(2,1)S(1)} %concatenate.37.rest_0_), channel_id=1, source_target_pairs={{0,2},{2,0},{4,6},{6,4},{1,3},{3,1},{5,7},{7,5},{8,10},{10,8},{12,... | collective-permute-start | bytes 835592 | tf_op jit(solution)/shard_map/ppermute | solution.py:63
  3.4 35.8 %collective-permute-start.4 = (bf16[64,2176]{1,0:T(8,128)(2,1)S(1)}, bf16[64,2176]{1,0:T(8,128)(2,1)}, u32[]{:S(2)}, u32[]{:S(2)}) collective-permute-start(bf16[64,2176]{1,0:T(8,128)(2,1)S(1)} %concatenate.37.rest_0_), channel_id=1, source_target_pairs={{0,6},{2,4},{4,2},{6,0},{1,7},{3,5},{5,3},{7,1},{8,14},{10,12},{12... | collective-permute-start | bytes 835592 | tf_op jit(solution)/shard_map/ppermute | solution.py:63
  8.7 30.9 %all-to-all-start = ((bf16[16,64,640]{2,1,0:T(8,128)(2,1)}), bf16[16,64,640]{2,1,0:T(8,128)(2,1)}, u32[]{:S(2)}, u32[]{:S(2)}) async-start(bf16[16,64,640]{2,1,0:T(8,128)(2,1)} %broadcast_in_dim.81), calls=%async_computation | async-start | bytes 2621440 | tf_op jit(solution)/shard_map/all_to_all | solution.py:556
  17.0 28.8 %collective-permute-start = (bf16[256,1280]{1,0:T(8,128)(2,1)S(1)}, bf16[256,1280]{1,0:T(8,128)(2,1)S(1)}, u32[]{:S(2)}, u32[]{:S(2)}) collective-permute-start(bf16[256,1280]{1,0:T(8,128)(2,1)S(1)} %pad_maximum_fusion), channel_id=1, source_target_pairs={{0,4},{4,0},{1,5},{5,1},{2,6},{6,2},{3,7},{7,3},{8,12},{12,8},{9,1... | collective-permute-start | bytes 1966088 | tf_op jit(solution)/shard_map/ppermute | solution.py:552
  17.9 18.7 %collective-permute-start.1 = (f32[64,768]{1,0:T(8,128)S(1)}, f32[64,768]{1,0:T(8,128)S(1)}, u32[]{:S(2)}, u32[]{:S(2)}) collective-permute-start(f32[64,768]{1,0:T(8,128)S(1)} %select_maximum_fusion), channel_id=1, source_target_pairs={{0,4},{4,0},{1,5},{5,1},{2,6},{6,2},{3,7},{7,3},{8,12},{12,8},{9,1... | collective-permute-start | bytes 589832 | tf_op jit(solution)/shard_map/ppermute | solution.py:555
  42.1 32.9 %collective-permute-start.11 = (bf16[8,64,640]{2,1,0:T(8,128)(2,1)}, bf16[8,64,640]{2,1,0:T(8,128)(2,1)S(1)}, u32[]{:S(2)}, u32[]{:S(2)}) collective-permute-start(bf16[8,64,640]{2,1,0:T(8,128)(2,1)} %get-tuple-element.32), channel_id=1, source_target_pairs={{0,4},{2,6},{4,0},{6,2},{1,5},{3,7},{5,1},{7,3},{8,12},{10,14},{12... | collective-permute-start | bytes 1966088 | tf_op jit(solution)/shard_map/ppermute | solution.py:63
  42.5 33.5 %collective-permute-start.12 = (bf16[8,64,640]{2,1,0:T(8,128)(2,1)}, bf16[8,64,640]{2,1,0:T(8,128)(2,1)}, u32[]{:S(2)}, u32[]{:S(2)}) collective-permute-start(bf16[8,64,640]{2,1,0:T(8,128)(2,1)} %get-tuple-element.32), channel_id=1, source_target_pairs={{0,6},{2,4},{4,2},{6,0},{1,7},{3,5},{5,3},{7,1},{8,14},{10,12},{12... | collective-permute-start | bytes 1966088 | tf_op jit(solution)/shard_map/ppermute | solution.py:63
  42.8 31.8 %collective-permute-start.10 = (bf16[8,64,640]{2,1,0:T(8,128)(2,1)}, bf16[8,64,640]{2,1,0:T(8,128)(2,1)}, u32[]{:S(2)}, u32[]{:S(2)}) collective-permute-start(bf16[8,64,640]{2,1,0:T(8,128)(2,1)} %get-tuple-element.33), channel_id=1, source_target_pairs={{0,6},{2,4},{4,2},{6,0},{1,7},{3,5},{5,3},{7,1},{8,14},{10,12},{12... | collective-permute-start | bytes 1966088 | tf_op jit(solution)/shard_map/ppermute | solution.py:63
  53.9 41.7 %all-to-all-start.1 = ((f32[4,4,704,128]{3,2,1,0:T(8,128)}), f32[4,4,704,128]{3,2,1,0:T(8,128)}, u32[]{:S(2)}, u32[]{:S(2)}) async-start(f32[4,4,704,128]{3,2,1,0:T(8,128)} %get-tuple-element.19), calls=%async_computation.1 | async-start | bytes 11534336 | tf_op jit(solution)/shard_map/all_to_all | solution.py:51
  60.1 21.9 %collective-permute-start.9 = (bf16[8,64,640]{2,1,0:T(8,128)(2,1)}, bf16[8,64,640]{2,1,0:T(8,128)(2,1)}, u32[]{:S(2)}, u32[]{:S(2)}) collective-permute-start(bf16[8,64,640]{2,1,0:T(8,128)(2,1)} %get-tuple-element.33), channel_id=1, source_target_pairs={{0,4},{2,6},{4,0},{6,2},{1,5},{3,7},{5,1},{7,3},{8,12},{10,14},{12... | collective-permute-start | bytes 1966088 | tf_op jit(solution)/shard_map/ppermute | solution.py:63
  74.6 16.0 %collective-permute-start.13 = (bf16[8,64,640]{2,1,0:T(8,128)(2,1)}, bf16[8,64,640]{2,1,0:T(8,128)(2,1)}, u32[]{:S(2)}, u32[]{:S(2)}) collective-permute-start(bf16[8,64,640]{2,1,0:T(8,128)(2,1)} %collective-permute-done.10.refs_1_.refs_7_), channel_id=1, source_target_pairs={{0,4},{2,6},{4,0},{6,2},{1,5},{3,7},{5,1},{7,3},{8,12},{10,14},{12... | collective-permute-start | bytes 1966088 | tf_op jit(solution)/shard_map/ppermute | solution.py:63
  75.0 18.5 %collective-permute-start.17 = (bf16[8,64,640]{2,1,0:T(8,128)(2,1)}, bf16[8,64,640]{2,1,0:T(8,128)(2,1)}, u32[]{:S(2)}, u32[]{:S(2)}) collective-permute-start(bf16[8,64,640]{2,1,0:T(8,128)(2,1)} %collective-permute-done.10.refs_1_.refs_7_), channel_id=1, source_target_pairs={{0,1},{1,0},{2,3},{3,2},{4,5},{5,4},{6,7},{7,6},{8,9},{9,8},{10,11... | collective-permute-start | bytes 1966088 | tf_op jit(solution)/shard_map/ppermute | solution.py:67
  75.1 18.5 %collective-permute-start.14 = (bf16[8,64,640]{2,1,0:T(8,128)(2,1)S(1)}, bf16[8,64,640]{2,1,0:T(8,128)(2,1)}, u32[]{:S(2)}, u32[]{:S(2)}) collective-permute-start(bf16[8,64,640]{2,1,0:T(8,128)(2,1)S(1)} %collective-permute-done.11.refs_2_.refs_8_), channel_id=1, source_target_pairs={{0,6},{2,4},{4,2},{6,0},{1,7},{3,5},{5,3},{7,1},{8,14},{10,12},{12... | collective-permute-start | bytes 1966088 | tf_op jit(solution)/shard_map/ppermute | solution.py:63
  76.0 18.1 %collective-permute-start.18 = (bf16[8,64,640]{2,1,0:T(8,128)(2,1)S(1)}, bf16[8,64,640]{2,1,0:T(8,128)(2,1)}, u32[]{:S(2)}, u32[]{:S(2)}) collective-permute-start(bf16[8,64,640]{2,1,0:T(8,128)(2,1)S(1)} %collective-permute-done.11.refs_2_.refs_8_), channel_id=1, source_target_pairs={{0,1},{1,0},{2,3},{3,2},{4,5},{5,4},{6,7},{7,6},{8,9},{9,8},{10,11... | collective-permute-start | bytes 1966088 | tf_op jit(solution)/shard_map/ppermute | solution.py:67
  82.0 22.4 %collective-permute-start.15 = (bf16[16,64,640]{2,1,0:T(8,128)(2,1)}, bf16[16,64,640]{2,1,0:T(8,128)(2,1)}, u32[]{:S(2)}, u32[]{:S(2)}) collective-permute-start(bf16[16,64,640]{2,1,0:T(8,128)(2,1)} %all-to-all-done.refs_5_), channel_id=1, source_target_pairs={{0,1},{1,0},{2,3},{3,2},{4,5},{5,4},{6,7},{7,6},{8,9},{9,8},{10,11... | collective-permute-start | bytes 3932168 | tf_op jit(solution)/shard_map/ppermute | solution.py:67
  90.6 13.8 %collective-permute-start.16 = (bf16[8,64,640]{2,1,0:T(8,128)(2,1)}, bf16[8,64,640]{2,1,0:T(8,128)(2,1)}, u32[]{:S(2)}, u32[]{:S(2)}) collective-permute-start(bf16[8,64,640]{2,1,0:T(8,128)(2,1)} %collective-permute-done.9.refs_0_.refs_6_), channel_id=1, source_target_pairs={{0,1},{1,0},{2,3},{3,2},{4,5},{5,4},{6,7},{7,6},{8,9},{9,8},{10,11... | collective-permute-start | bytes 1966088 | tf_op jit(solution)/shard_map/ppermute | solution.py:67
  93.5 10.9 %collective-permute-start.19 = (bf16[8,64,640]{2,1,0:T(8,128)(2,1)}, bf16[8,64,640]{2,1,0:T(8,128)(2,1)}, u32[]{:S(2)}, u32[]{:S(2)}) collective-permute-start(bf16[8,64,640]{2,1,0:T(8,128)(2,1)} %collective-permute-done.12.refs_3_.refs_9_), channel_id=1, source_target_pairs={{0,1},{1,0},{2,3},{3,2},{4,5},{5,4},{6,7},{7,6},{8,9},{9,8},{10,11... | collective-permute-start | bytes 1966088 | tf_op jit(solution)/shard_map/ppermute | solution.py:67
  93.5 10.9 %collective-permute-start.20 = (bf16[8,64,640]{2,1,0:T(8,128)(2,1)}, bf16[8,64,640]{2,1,0:T(8,128)(2,1)}, u32[]{:S(2)}, u32[]{:S(2)}) collective-permute-start(bf16[8,64,640]{2,1,0:T(8,128)(2,1)} %collective-permute-done.13.refs_10_), channel_id=1, source_target_pairs={{0,1},{1,0},{2,3},{3,2},{4,5},{5,4},{6,7},{7,6},{8,9},{9,8},{10,11... | collective-permute-start | bytes 1966088 | tf_op jit(solution)/shard_map/ppermute | solution.py:67
  94.0 10.4 %collective-permute-start.21 = (bf16[8,64,640]{2,1,0:T(8,128)(2,1)}, bf16[8,64,640]{2,1,0:T(8,128)(2,1)}, u32[]{:S(2)}, u32[]{:S(2)}) collective-permute-start(bf16[8,64,640]{2,1,0:T(8,128)(2,1)} %collective-permute-done.14.refs_11_), channel_id=1, source_target_pairs={{0,1},{1,0},{2,3},{3,2},{4,5},{5,4},{6,7},{7,6},{8,9},{9,8},{10,11... | collective-permute-start | bytes 1966088 | tf_op jit(solution)/shard_map/ppermute | solution.py:67
  100.0 41.5 %all-to-all-start.2 = ((f32[4,704,128]{2,1,0:T(8,128)}), f32[4,704,128]{2,1,0:T(8,128)S(1)}, u32[]{:S(2)}, u32[]{:S(2)}) async-start(f32[4,704,128]{2,1,0:T(8,128)} %sum_first.1), calls=%async_computation.2 | async-start | bytes 2883584 | tf_op jit(solution)/shard_map/all_to_all | solution.py:51
  143.9 12.4 %collective-permute-start.23 = (f32[392,128]{1,0:T(8,128)S(1)}, f32[392,128]{1,0:T(8,128)S(1)}, u32[]{:S(2)}, u32[]{:S(2)}) collective-permute-start(f32[392,128]{1,0:T(8,128)S(1)} %get-tuple-element.22.a_ref), channel_id=1, source_target_pairs={{0,64},{32,96},{64,0},{96,32},{1,65},{33,97},{65,1},{97,33},{2,66}... | collective-permute-start | bytes 602120 | tf_op jit(solution)/shard_map/ppermute | solution.py:55
  146.6 9.7 %collective-permute-start.24 = (f32[392,128]{1,0:T(8,128)S(1)}, f32[392,128]{1,0:T(8,128)S(1)}, u32[]{:S(2)}, u32[]{:S(2)}) collective-permute-start(f32[392,128]{1,0:T(8,128)S(1)} %get-tuple-element.22.a_ref), channel_id=1, source_target_pairs={{0,96},{32,0},{64,32},{96,64},{1,97},{33,1},{65,33},{97,65},{2,98}... | collective-permute-start | bytes 602120 | tf_op jit(solution)/shard_map/ppermute | solution.py:55
  161.2 13.6 %all-to-all-start.3 = ((f32[8,64,256]{2,1,0:T(8,128)}), f32[8,64,256]{2,1,0:T(8,128)S(1)}, u32[]{:S(2)}, u32[]{:S(2)}) async-start(f32[8,64,256]{2,1,0:T(8,128)} %newton.1), calls=%async_computation.3 | async-start | bytes 1048576 | tf_op jit(solution)/shard_map/all_to_all | solution.py:593
  (21 other events, 168.8 us)

commit v5 on v4

--- a/solution.py
+++ b/solution.py
@@ -78,19 +78,20 @@
         if index == count // 2:
             slot = 0
 
-        @pl.loop(0, piece.shape[0])
+        @pl.loop(0, piece.shape[0], unroll=True)
         def _(s, piece=piece, side=side, slot=slot):
             row = pl.multiple_of(place_ref[slot + s] * 128 + core_ref[side], 64)
             pltpu.make_async_copy(piece.at[s], keys.at[pl.ds(row, 64)], sem).start()
 
         slot += piece.shape[0]
-    pltpu.make_async_copy(keys, keys, sem).wait()
     factor = SCALE * LOG2E
     for half in range(2):
         acc[...] = jnp.zeros(acc.shape, F32)
         top[...] = jnp.full(top.shape, LOW, F32)
         total[...] = jnp.zeros(total.shape, F32)
         tiles = lax.div(qpos_ref[half] + 4, 4)
+        if half == 0:
+            pltpu.make_async_copy(keys, keys, sem).wait()
 
         def tile(j, masked, half=half):
             row0 = pl.multiple_of(j * TILE, TILE)

time: 177 us -> 177 us (level)
  no operation moved by 1% of the time
where the time goes in v5:
time: 177 us; the launch traced here: 176 us
  Pallas kernels  58.4 us (33%)
  waiting for transfers between devices  57 us (32%)
  starting transfers between devices  43 us (24%)
  local copies, waits for them, and re-layouts  12.7 us (7%)
  other arithmetic  3.79 us (2%)
    pallas_call x1, Pallas kernels, attention(): pl.pallas_call(functools.partial(attention_kernel, head0, heads, len(piec...  36.7 us
    ppermute x9, waiting for transfers between devices, flip(): return lax.ppermute(value, ('yl', 'yh'), pairs)  25 us
    ppermute x1, waiting for transfers between devices, shards(): m_other = lax.ppermute(m_other, 'yl', [(0, 1), (1, 0)])  16.6 us
    ppermute x9, starting transfers between devices, flip(): return lax.ppermute(value, ('yl', 'yh'), pairs)  10.3 us
    all_to_all x2, starting transfers between devices, exchange(): lax.all_to_all(value, ('z', 'x', 'c'), 0, 0, axis_index_groups=groups)  9.64 us
    ppermute x3, waiting for transfers between devices, move_z(): return lax.ppermute(value, 'z', [(i, (i + k) % 4) for i in range(4)])  8.13 us
    all_to_all x1, starting transfers between devices, shards(): lax.all_to_all(jnp.broadcast_to(key_rows[None], (16, 64, WIDE)), ('z', 'x...  8.05 us
    pallas_call x1, Pallas kernels, gradient_terms(): pl.pallas_call(gradient_kernel, out_shape=(jax.ShapeDtypeStruct((4, 4, 70...  7.27 us
  transfers between devices with their start and end apart: 29, of which 7 were waited for; matrix products, arithmetic and copies ran while one was open for 6% of the time, Pallas kernels for 29%

profile of v5, /device:TPU:24, one launch (start us, length us, event | category | flops | bytes accessed | tf_op | source)
XLA Modules:
  0.0 176.0 jit_solution(12975561265352816445)
XLA Ops:
  3.4 3.1 %collective-permute-start.4 = (bf16[64,2176]{1,0:T(8,128)(2,1)S(1)}, bf16[64,2176]{1,0:T(8,128)(2,1)}, u32[]{:S(2)}, u32[]{:S(2)}) collective-permute-start(bf16[64,2176]{1,0:T(8,128)(2,1)S(1)} %concatenate.37.rest_0_), channel_id=1, source_target_pairs={{0,6},{2,4},{4,2},{6,0},{1,7},{3,5},{5,3},{7,1},{8,14},{10,12},{12... | collective-permute-start | bytes 835592 | tf_op jit(solution)/shard_map/ppermute | solution.py:63
  8.7 8.1 %all-to-all-start = ((bf16[16,64,640]{2,1,0:T(8,128)(2,1)}), bf16[16,64,640]{2,1,0:T(8,128)(2,1)}, u32[]{:S(2)}, u32[]{:S(2)}) async-start(bf16[16,64,640]{2,1,0:T(8,128)(2,1)} %broadcast_in_dim.81), calls=%async_computation | async-start | bytes 2621440 | tf_op jit(solution)/shard_map/all_to_all | solution.py:557
  20.0 16.6 %collective-permute-done.1.m_other = f32[64,768]{1,0:T(8,128)S(1)} collective-permute-done((f32[64,768]{1,0:T(8,128)S(1)}, f32[64,768]{1,0:T(8,128)S(1)}, u32[]{:S(2)}, u32[]{:S(2)}) %collective-permute-start.1) | collective-permute-done | bytes 196640 | tf_op jit(solution)/shard_map/ppermute | solution.py:556
  39.6 2.4 %fusion.8 = (bf16[8,64,640]{2,1,0:T(8,128)(2,1)}, bf16[8,64,640]{2,1,0:T(8,128)(2,1)}) fusion(bf16[16,64,640]{2,1,0:T(8,128)(2,1)} %all-to-all-done.refs_5_), kind=kLoop, calls=%fused_computation.50 | loop fusion | bytes 2621440 | tf_op jit(solution)/shard_map/slice | solution.py:560
  42.8 2.9 %collective-permute-start.10 = (bf16[8,64,640]{2,1,0:T(8,128)(2,1)}, bf16[8,64,640]{2,1,0:T(8,128)(2,1)}, u32[]{:S(2)}, u32[]{:S(2)}) collective-permute-start(bf16[8,64,640]{2,1,0:T(8,128)(2,1)} %get-tuple-element.33), channel_id=1, source_target_pairs={{0,6},{2,4},{4,2},{6,0},{1,7},{3,5},{5,3},{7,1},{8,14},{10,12},{12... | collective-permute-start | bytes 1966088 | tf_op jit(solution)/shard_map/ppermute | solution.py:63
  46.6 7.3 %gradient_terms.1 = (f32[4,4,704,128]{3,2,1,0:T(8,128)}, bf16[256,2176]{1,0:T(8,128)(2,1)}) custom-call(s32[5]{0:T(128)} %stack.35.at_ref, bf16[256,1536]{1,0:T(8,128)(2,1)} %gq_ref.1, bf16[256,1024]{1,0:T(8,128)(2,1)} %gk_ref.1, bf16[256,1280]{1,0:T(8,128)(2,1)} %copy-done.9, f32[48,1536]{1,0:T(8,128)} %mq_ref.1, f32[16,1024]{1,0:T(8,128)} %mk_ref.1, ...), custom_call_target="tpu_custom_call" | custom-call | flops 1000 | bytes 1000 | tf_op jit(solution)/shard_map/gradient_terms/pallas_call | solution.py:284
  53.9 5.3 %all-to-all-start.1 = ((f32[4,4,704,128]{3,2,1,0:T(8,128)}), f32[4,4,704,128]{3,2,1,0:T(8,128)}, u32[]{:S(2)}, u32[]{:S(2)}) async-start(f32[4,4,704,128]{3,2,1,0:T(8,128)} %get-tuple-element.19), calls=%async_computation.1 | async-start | bytes 11534336 | tf_op jit(solution)/shard_map/all_to_all | solution.py:51
  60.7 13.9 %collective-permute-done.10.refs_1_.refs_7_ = bf16[8,64,640]{2,1,0:T(8,128)(2,1)} collective-permute-done((bf16[8,64,640]{2,1,0:T(8,128)(2,1)}, bf16[8,64,640]{2,1,0:T(8,128)(2,1)}, u32[]{:S(2)}, u32[]{:S(2)}) %collective-permute-start.10) | collective-permute-done | bytes 655392 | tf_op jit(solution)/shard_map/ppermute | solution.py:63
  76.8 2.3 %copy-done = bf16[1536,1536]{1,0:T(8,128)(2,1)S(1)} copy-done((bf16[1536,1536]{1,0:T(8,128)(2,1)S(1)}, bf16[1536,1536]{1,0:T(8,128)(2,1)}, u32[]{:S(2)}) %copy-start) | copy-done | bytes 4718616
  79.2 2.9 %queries.1.refs_4_.refs_3_ = bf16[2,1024,640]{2,1,0:T(8,128)(2,1)S(1)} custom-call(bf16[256,2176]{1,0:T(8,128)(2,1)S(1)} %copy-done.3, bf16[1536,1536]{1,0:T(8,128)(2,1)S(1)} %copy-done, bf16[512,1024]{1,0:T(8,128)(2,1)S(1)} %copy-done.2, f32[256,128]{1,0:T(8,128)S(1)} %get-tuple-element.38.cos_ref, f32[256,128]{1,0:T(8,128)S(1)} %concatenate.39.low_ref, ...), custom_call_target="tpu_custom_call" | custom-call | flops 1000 | bytes 1000 | tf_op jit(solution)/shard_map/queries/pallas_call | solution.py:227
  82.4 8.2 %collective-permute-done.13.refs_10_ = bf16[8,64,640]{2,1,0:T(8,128)(2,1)} collective-permute-done((bf16[8,64,640]{2,1,0:T(8,128)(2,1)}, bf16[8,64,640]{2,1,0:T(8,128)(2,1)}, u32[]{:S(2)}, u32[]{:S(2)}) %collective-permute-start.13) | collective-permute-done | bytes 655392 | tf_op jit(solution)/shard_map/ppermute | solution.py:63
  90.6 2.9 %collective-permute-done.14.refs_11_ = bf16[8,64,640]{2,1,0:T(8,128)(2,1)} collective-permute-done((bf16[8,64,640]{2,1,0:T(8,128)(2,1)S(1)}, bf16[8,64,640]{2,1,0:T(8,128)(2,1)}, u32[]{:S(2)}, u32[]{:S(2)}) %collective-permute-start.14) | collective-permute-done | bytes 655392 | tf_op jit(solution)/shard_map/ppermute | solution.py:63
  94.1 1.5 copy-done.1
  95.6 4.4 %sum_first.1 = f32[4,704,128]{2,1,0:T(8,128)} custom-call(f32[4,4,704,128]{3,2,1,0:T(8,128)} %all-to-all-done.1.a_ref), custom_call_target="tpu_custom_call" | custom-call | flops 1000 | bytes 1000 | tf_op jit(solution)/shard_map/sum_first/pallas_call | solution.py:310
  100.0 4.4 %all-to-all-start.2 = ((f32[4,704,128]{2,1,0:T(8,128)}), f32[4,704,128]{2,1,0:T(8,128)S(1)}, u32[]{:S(2)}, u32[]{:S(2)}) async-start(f32[4,704,128]{2,1,0:T(8,128)} %sum_first.1), calls=%async_computation.2 | async-start | bytes 2883584 | tf_op jit(solution)/shard_map/all_to_all | solution.py:51
  104.4 36.7 %attention.1 = (bf16[256,1024]{1,0:T(8,128)(2,1)}, f32[8,128]{1,0:T(8,128)S(1)}) custom-call(s32[64]{0:T(128)S(1)} %pad_add_fusion.2.refs_0_, s32[2]{0:T(128)S(1)} %pad_add_fusion.3.refs_1_, s32[2]{0:T(128)S(1)} %fusion.2.refs_2_, bf16[2,1024,640]{2,1,0:T(8,128)(2,1)} %copy-done.1, bf16[512,1024]{1,0:T(8,128)(2,1)} %refs_4_.1, ...), custom_call_target="tpu_custom_call" | custom-call | flops 20000000000 | bytes 14680064 | tf_op jit(solution)/shard_map/attention/pallas_call | solution.py:150
  142.0 1.6 collective-permute-start.22
  143.5 2.7 %collective-permute-start.23 = (f32[392,128]{1,0:T(8,128)S(1)}, f32[392,128]{1,0:T(8,128)S(1)}, u32[]{:S(2)}, u32[]{:S(2)}) collective-permute-start(f32[392,128]{1,0:T(8,128)S(1)} %get-tuple-element.22.a_ref), channel_id=1, source_target_pairs={{0,64},{32,96},{64,0},{96,32},{1,65},{33,97},{65,1},{97,33},{2,66}... | collective-permute-start | bytes 602120 | tf_op jit(solution)/shard_map/ppermute | solution.py:55
  147.6 2.7 %collective-permute-done.22.b_ref = f32[392,128]{1,0:T(8,128)S(1)} collective-permute-done((f32[392,128]{1,0:T(8,128)S(1)}, f32[392,128]{1,0:T(8,128)S(1)}, u32[]{:S(2)}, u32[]{:S(2)}) %collective-permute-start.22) | collective-permute-done | bytes 200736 | tf_op jit(solution)/shard_map/ppermute | solution.py:55
  150.3 5.5 %collective-permute-done.23.c_ref = f32[392,128]{1,0:T(8,128)S(1)} collective-permute-done((f32[392,128]{1,0:T(8,128)S(1)}, f32[392,128]{1,0:T(8,128)S(1)}, u32[]{:S(2)}, u32[]{:S(2)}) %collective-permute-start.23) | collective-permute-done | bytes 200736 | tf_op jit(solution)/shard_map/ppermute | solution.py:55
  155.7 4.9 %newton.1 = f32[8,64,256]{2,1,0:T(8,128)} custom-call(f32[704,128]{1,0:T(8,128)S(1)} %get-tuple-element.21.m_ref, f32[392,128]{1,0:T(8,128)S(1)} %get-tuple-element.22.a_ref, f32[392,128]{1,0:T(8,128)S(1)} %collective-permute-done.22.b_ref, f32[392,128]{1,0:T(8,128)S(1)} %collective-permute-done.23.c_ref, f32[392,128]{1,0:T(8,128)S(1)} %collective-permute-done.24.d_ref), custom_call_target="tpu_custom_call" | custom-call | flops 1000 | bytes 1000 | tf_op jit(solution)/shard_map/newton/pallas_call | solution.py:433
  160.6 5.7 %all-to-all-start.3 = ((f32[8,64,256]{2,1,0:T(8,128)}), f32[8,64,256]{2,1,0:T(8,128)S(1)}, u32[]{:S(2)}, u32[]{:S(2)}) async-start(f32[8,64,256]{2,1,0:T(8,128)} %newton.1), calls=%async_computation.3 | async-start | bytes 1048576 | tf_op jit(solution)/shard_map/all_to_all | solution.py:594
  167.3 7.2 %all-to-all-done.3.step_ref = f32[8,64,256]{2,1,0:T(8,128)S(1)} async-done(((f32[8,64,256]{2,1,0:T(8,128)}), f32[8,64,256]{2,1,0:T(8,128)S(1)}, u32[]{:S(2)}, u32[]{:S(2)}) %all-to-all-start.3) | async-done | bytes 524320 | tf_op jit(solution)/shard_map/all_to_all | solution.py:594
  174.5 1.5 update.1
  (109 shorter events, 20.4 us)
Async XLA Ops:
  1.7 34.9 %collective-permute-start.2 = (bf16[64,2176]{1,0:T(8,128)(2,1)S(1)}, bf16[64,2176]{1,0:T(8,128)(2,1)S(1)}, u32[]{:S(2)}, u32[]{:S(2)}) collective-permute-start(bf16[64,2176]{1,0:T(8,128)(2,1)S(1)} %concatenate.37.rest_0_), channel_id=1, source_target_pairs={{0,4},{2,6},{4,0},{6,2},{1,5},{3,7},{5,1},{7,3},{8,12},{10,14},{12... | collective-permute-start | bytes 835592 | tf_op jit(solution)/shard_map/ppermute | solution.py:63
  2.5 34.6 %collective-permute-start.3 = (bf16[64,2176]{1,0:T(8,128)(2,1)S(1)}, bf16[64,2176]{1,0:T(8,128)(2,1)}, u32[]{:S(2)}, u32[]{:S(2)}) collective-permute-start(bf16[64,2176]{1,0:T(8,128)(2,1)S(1)} %concatenate.37.rest_0_), channel_id=1, source_target_pairs={{0,2},{2,0},{4,6},{6,4},{1,3},{3,1},{5,7},{7,5},{8,10},{10,8},{12,... | collective-permute-start | bytes 835592 | tf_op jit(solution)/shard_map/ppermute | solution.py:63
  3.4 35.8 %collective-permute-start.4 = (bf16[64,2176]{1,0:T(8,128)(2,1)S(1)}, bf16[64,2176]{1,0:T(8,128)(2,1)}, u32[]{:S(2)}, u32[]{:S(2)}) collective-permute-start(bf16[64,2176]{1,0:T(8,128)(2,1)S(1)} %concatenate.37.rest_0_), channel_id=1, source_target_pairs={{0,6},{2,4},{4,2},{6,0},{1,7},{3,5},{5,3},{7,1},{8,14},{10,12},{12... | collective-permute-start | bytes 835592 | tf_op jit(solution)/shard_map/ppermute | solution.py:63
  8.7 30.9 %all-to-all-start = ((bf16[16,64,640]{2,1,0:T(8,128)(2,1)}), bf16[16,64,640]{2,1,0:T(8,128)(2,1)}, u32[]{:S(2)}, u32[]{:S(2)}) async-start(bf16[16,64,640]{2,1,0:T(8,128)(2,1)} %broadcast_in_dim.81), calls=%async_computation | async-start | bytes 2621440 | tf_op jit(solution)/shard_map/all_to_all | solution.py:557
  17.0 28.8 %collective-permute-start = (bf16[256,1280]{1,0:T(8,128)(2,1)S(1)}, bf16[256,1280]{1,0:T(8,128)(2,1)S(1)}, u32[]{:S(2)}, u32[]{:S(2)}) collective-permute-start(bf16[256,1280]{1,0:T(8,128)(2,1)S(1)} %pad_maximum_fusion), channel_id=1, source_target_pairs={{0,4},{4,0},{1,5},{5,1},{2,6},{6,2},{3,7},{7,3},{8,12},{12,8},{9,1... | collective-permute-start | bytes 1966088 | tf_op jit(solution)/shard_map/ppermute | solution.py:553
  17.9 18.7 %collective-permute-start.1 = (f32[64,768]{1,0:T(8,128)S(1)}, f32[64,768]{1,0:T(8,128)S(1)}, u32[]{:S(2)}, u32[]{:S(2)}) collective-permute-start(f32[64,768]{1,0:T(8,128)S(1)} %select_maximum_fusion), channel_id=1, source_target_pairs={{0,4},{4,0},{1,5},{5,1},{2,6},{6,2},{3,7},{7,3},{8,12},{12,8},{9,1... | collective-permute-start | bytes 589832 | tf_op jit(solution)/shard_map/ppermute | solution.py:556
  42.1 32.9 %collective-permute-start.11 = (bf16[8,64,640]{2,1,0:T(8,128)(2,1)}, bf16[8,64,640]{2,1,0:T(8,128)(2,1)S(1)}, u32[]{:S(2)}, u32[]{:S(2)}) collective-permute-start(bf16[8,64,640]{2,1,0:T(8,128)(2,1)} %get-tuple-element.32), channel_id=1, source_target_pairs={{0,4},{2,6},{4,0},{6,2},{1,5},{3,7},{5,1},{7,3},{8,12},{10,14},{12... | collective-permute-start | bytes 1966088 | tf_op jit(solution)/shard_map/ppermute | solution.py:63
  42.5 33.5 %collective-permute-start.12 = (bf16[8,64,640]{2,1,0:T(8,128)(2,1)}, bf16[8,64,640]{2,1,0:T(8,128)(2,1)}, u32[]{:S(2)}, u32[]{:S(2)}) collective-permute-start(bf16[8,64,640]{2,1,0:T(8,128)(2,1)} %get-tuple-element.32), channel_id=1, source_target_pairs={{0,6},{2,4},{4,2},{6,0},{1,7},{3,5},{5,3},{7,1},{8,14},{10,12},{12... | collective-permute-start | bytes 1966088 | tf_op jit(solution)/shard_map/ppermute | solution.py:63
  42.8 31.8 %collective-permute-start.10 = (bf16[8,64,640]{2,1,0:T(8,128)(2,1)}, bf16[8,64,640]{2,1,0:T(8,128)(2,1)}, u32[]{:S(2)}, u32[]{:S(2)}) collective-permute-start(bf16[8,64,640]{2,1,0:T(8,128)(2,1)} %get-tuple-element.33), channel_id=1, source_target_pairs={{0,6},{2,4},{4,2},{6,0},{1,7},{3,5},{5,3},{7,1},{8,14},{10,12},{12... | collective-permute-start | bytes 1966088 | tf_op jit(solution)/shard_map/ppermute | solution.py:63
  53.9 41.7 %all-to-all-start.1 = ((f32[4,4,704,128]{3,2,1,0:T(8,128)}), f32[4,4,704,128]{3,2,1,0:T(8,128)}, u32[]{:S(2)}, u32[]{:S(2)}) async-start(f32[4,4,704,128]{3,2,1,0:T(8,128)} %get-tuple-element.19), calls=%async_computation.1 | async-start | bytes 11534336 | tf_op jit(solution)/shard_map/all_to_all | solution.py:51
  60.1 21.9 %collective-permute-start.9 = (bf16[8,64,640]{2,1,0:T(8,128)(2,1)}, bf16[8,64,640]{2,1,0:T(8,128)(2,1)}, u32[]{:S(2)}, u32[]{:S(2)}) collective-permute-start(bf16[8,64,640]{2,1,0:T(8,128)(2,1)} %get-tuple-element.33), channel_id=1, source_target_pairs={{0,4},{2,6},{4,0},{6,2},{1,5},{3,7},{5,1},{7,3},{8,12},{10,14},{12... | collective-permute-start | bytes 1966088 | tf_op jit(solution)/shard_map/ppermute | solution.py:63
  74.6 16.0 %collective-permute-start.13 = (bf16[8,64,640]{2,1,0:T(8,128)(2,1)}, bf16[8,64,640]{2,1,0:T(8,128)(2,1)}, u32[]{:S(2)}, u32[]{:S(2)}) collective-permute-start(bf16[8,64,640]{2,1,0:T(8,128)(2,1)} %collective-permute-done.10.refs_1_.refs_7_), channel_id=1, source_target_pairs={{0,4},{2,6},{4,0},{6,2},{1,5},{3,7},{5,1},{7,3},{8,12},{10,14},{12... | collective-permute-start | bytes 1966088 | tf_op jit(solution)/shard_map/ppermute | solution.py:63
  75.0 18.5 %collective-permute-start.17 = (bf16[8,64,640]{2,1,0:T(8,128)(2,1)}, bf16[8,64,640]{2,1,0:T(8,128)(2,1)}, u32[]{:S(2)}, u32[]{:S(2)}) collective-permute-start(bf16[8,64,640]{2,1,0:T(8,128)(2,1)} %collective-permute-done.10.refs_1_.refs_7_), channel_id=1, source_target_pairs={{0,1},{1,0},{2,3},{3,2},{4,5},{5,4},{6,7},{7,6},{8,9},{9,8},{10,11... | collective-permute-start | bytes 1966088 | tf_op jit(solution)/shard_map/ppermute | solution.py:67
  75.1 18.5 %collective-permute-start.14 = (bf16[8,64,640]{2,1,0:T(8,128)(2,1)S(1)}, bf16[8,64,640]{2,1,0:T(8,128)(2,1)}, u32[]{:S(2)}, u32[]{:S(2)}) collective-permute-start(bf16[8,64,640]{2,1,0:T(8,128)(2,1)S(1)} %collective-permute-done.11.refs_2_.refs_8_), channel_id=1, source_target_pairs={{0,6},{2,4},{4,2},{6,0},{1,7},{3,5},{5,3},{7,1},{8,14},{10,12},{12... | collective-permute-start | bytes 1966088 | tf_op jit(solution)/shard_map/ppermute | solution.py:63
  76.0 18.1 %collective-permute-start.18 = (bf16[8,64,640]{2,1,0:T(8,128)(2,1)S(1)}, bf16[8,64,640]{2,1,0:T(8,128)(2,1)}, u32[]{:S(2)}, u32[]{:S(2)}) collective-permute-start(bf16[8,64,640]{2,1,0:T(8,128)(2,1)S(1)} %collective-permute-done.11.refs_2_.refs_8_), channel_id=1, source_target_pairs={{0,1},{1,0},{2,3},{3,2},{4,5},{5,4},{6,7},{7,6},{8,9},{9,8},{10,11... | collective-permute-start | bytes 1966088 | tf_op jit(solution)/shard_map/ppermute | solution.py:67
  82.0 22.4 %collective-permute-start.15 = (bf16[16,64,640]{2,1,0:T(8,128)(2,1)}, bf16[16,64,640]{2,1,0:T(8,128)(2,1)}, u32[]{:S(2)}, u32[]{:S(2)}) collective-permute-start(bf16[16,64,640]{2,1,0:T(8,128)(2,1)} %all-to-all-done.refs_5_), channel_id=1, source_target_pairs={{0,1},{1,0},{2,3},{3,2},{4,5},{5,4},{6,7},{7,6},{8,9},{9,8},{10,11... | collective-permute-start | bytes 3932168 | tf_op jit(solution)/shard_map/ppermute | solution.py:67
  90.6 13.8 %collective-permute-start.16 = (bf16[8,64,640]{2,1,0:T(8,128)(2,1)}, bf16[8,64,640]{2,1,0:T(8,128)(2,1)}, u32[]{:S(2)}, u32[]{:S(2)}) collective-permute-start(bf16[8,64,640]{2,1,0:T(8,128)(2,1)} %collective-permute-done.9.refs_0_.refs_6_), channel_id=1, source_target_pairs={{0,1},{1,0},{2,3},{3,2},{4,5},{5,4},{6,7},{7,6},{8,9},{9,8},{10,11... | collective-permute-start | bytes 1966088 | tf_op jit(solution)/shard_map/ppermute | solution.py:67
  93.5 10.9 %collective-permute-start.19 = (bf16[8,64,640]{2,1,0:T(8,128)(2,1)}, bf16[8,64,640]{2,1,0:T(8,128)(2,1)}, u32[]{:S(2)}, u32[]{:S(2)}) collective-permute-start(bf16[8,64,640]{2,1,0:T(8,128)(2,1)} %collective-permute-done.12.refs_3_.refs_9_), channel_id=1, source_target_pairs={{0,1},{1,0},{2,3},{3,2},{4,5},{5,4},{6,7},{7,6},{8,9},{9,8},{10,11... | collective-permute-start | bytes 1966088 | tf_op jit(solution)/shard_map/ppermute | solution.py:67
  93.5 10.9 %collective-permute-start.20 = (bf16[8,64,640]{2,1,0:T(8,128)(2,1)}, bf16[8,64,640]{2,1,0:T(8,128)(2,1)}, u32[]{:S(2)}, u32[]{:S(2)}) collective-permute-start(bf16[8,64,640]{2,1,0:T(8,128)(2,1)} %collective-permute-done.13.refs_10_), channel_id=1, source_target_pairs={{0,1},{1,0},{2,3},{3,2},{4,5},{5,4},{6,7},{7,6},{8,9},{9,8},{10,11... | collective-permute-start | bytes 1966088 | tf_op jit(solution)/shard_map/ppermute | solution.py:67
  94.0 10.4 %collective-permute-start.21 = (bf16[8,64,640]{2,1,0:T(8,128)(2,1)}, bf16[8,64,640]{2,1,0:T(8,128)(2,1)}, u32[]{:S(2)}, u32[]{:S(2)}) collective-permute-start(bf16[8,64,640]{2,1,0:T(8,128)(2,1)} %collective-permute-done.14.refs_11_), channel_id=1, source_target_pairs={{0,1},{1,0},{2,3},{3,2},{4,5},{5,4},{6,7},{7,6},{8,9},{9,8},{10,11... | collective-permute-start | bytes 1966088 | tf_op jit(solution)/shard_map/ppermute | solution.py:67
  100.0 41.1 %all-to-all-start.2 = ((f32[4,704,128]{2,1,0:T(8,128)}), f32[4,704,128]{2,1,0:T(8,128)S(1)}, u32[]{:S(2)}, u32[]{:S(2)}) async-start(f32[4,704,128]{2,1,0:T(8,128)} %sum_first.1), calls=%async_computation.2 | async-start | bytes 2883584 | tf_op jit(solution)/shard_map/all_to_all | solution.py:51
  143.5 12.2 %collective-permute-start.23 = (f32[392,128]{1,0:T(8,128)S(1)}, f32[392,128]{1,0:T(8,128)S(1)}, u32[]{:S(2)}, u32[]{:S(2)}) collective-permute-start(f32[392,128]{1,0:T(8,128)S(1)} %get-tuple-element.22.a_ref), channel_id=1, source_target_pairs={{0,64},{32,96},{64,0},{96,32},{1,65},{33,97},{65,1},{97,33},{2,66}... | collective-permute-start | bytes 602120 | tf_op jit(solution)/shard_map/ppermute | solution.py:55
  146.2 9.5 %collective-permute-start.24 = (f32[392,128]{1,0:T(8,128)S(1)}, f32[392,128]{1,0:T(8,128)S(1)}, u32[]{:S(2)}, u32[]{:S(2)}) collective-permute-start(f32[392,128]{1,0:T(8,128)S(1)} %get-tuple-element.22.a_ref), channel_id=1, source_target_pairs={{0,96},{32,0},{64,32},{96,64},{1,97},{33,1},{65,33},{97,65},{2,98}... | collective-permute-start | bytes 602120 | tf_op jit(solution)/shard_map/ppermute | solution.py:55
  160.6 13.8 %all-to-all-start.3 = ((f32[8,64,256]{2,1,0:T(8,128)}), f32[8,64,256]{2,1,0:T(8,128)S(1)}, u32[]{:S(2)}, u32[]{:S(2)}) async-start(f32[8,64,256]{2,1,0:T(8,128)} %newton.1), calls=%async_computation.3 | async-start | bytes 1048576 | tf_op jit(solution)/shard_map/all_to_all | solution.py:594
  (21 other events, 168.9 us)
